TPU v7x, 32 devices: a whole 2x2x4 slice. The times are simulated.
32 devices in a mesh: parts: 2 (over y), wide: 8 (over z, x), narrow: 2 (over core).
Axes of the slice: x: 2, y: 2, z: 4, core: 2. Of those that a mesh axis runs over, the one named last changes fastest.
Arguments:
- right_side: float32 [32768, 512], P(('parts', 'wide', 'narrow')), parts along dimension 0, may hold values from -6 to 6
- leaf_inverse: float32 [32768, 1024], P(('parts', 'wide', 'narrow')), parts along dimension 0, may hold values from -0.1875 to 0.1875
- row_bases: float32 [3, 32768, 128], P(None, ('parts', 'wide', 'narrow')), parts along dimension 1, may hold values from -0.5 to 0.5
- dual_bases: float32 [3, 32768, 128], P(None, ('parts', 'wide', 'narrow')), parts along dimension 1, may hold values from -0.0625 to 0.0625
- woodbury_cores: float32 [3584, 256], P('parts'), parts along dimension 0, may hold values from -0.375 to 0.375
Outputs:
- solution: float32 [32768, 512], P(('parts', 'wide', 'narrow')), parts along dimension 0
There are 2 independent parts, one for each index of `parts`. A program takes and returns all parts, laid end to end along the dimension named above; each array names one. Nothing has to cross between parts.
All inputs are finite; a program needn't handle non-finite values.
Results may differ from a plain program's by a relative error of at most 0.00011.
Values sent between devices are 32-bit elements; how exact they have to be, the bound alone decides.
No kernel may reach another device: no remote copies, remote signals or barrier semaphores. Data moves between devices by JAX's collectives and lax.ppermute only.
A program may use at most 128 MiB of HBM per device.

v0:
```python
import jax
import jax.numpy as jnp
from jax import lax
from jax.sharding import PartitionSpec as P


def swapped(block, axis, distance):
    count = lax.axis_size(axis)
    route = []
    for low in range(count):
        high = low | 1 << distance
        if high != low and high < count:
            route += [(low, high), (high, low)]
    return lax.ppermute(block, axis, route)


def shards(right_side, leaf_inverse, row_bases, dual_bases, woodbury_cores):
    highest = lax.Precision.HIGHEST
    wide_count = lax.axis_size("wide")
    wide_depth = wide_count.bit_length() - 1
    levels = row_bases.shape[0]
    rank = row_bases.shape[2]
    field = jnp.dot(leaf_inverse, right_side, precision=highest, preferred_element_type=jnp.float32)
    position = lax.axis_index("wide")
    for level in range(levels, 0, -1):
        below = wide_depth - level
        child = jnp.right_shift(position, below)
        count = 2**level
        left_basis = row_bases[level - 1]
        dual_basis = dual_bases[level - 1]
        own_sum = jnp.einsum("rk,rn->kn", dual_basis, field, precision=highest)
        own_sum = own_sum + swapped(own_sum, "narrow", 0)
        for bit in range(below):
            own_sum = own_sum + swapped(own_sum, "wide", bit)
        other_sum = swapped(own_sum, "wide", below)
        is_second = jnp.bitwise_and(child, 1) == 1
        stacked = jnp.where(
            is_second,
            jnp.concatenate([other_sum, own_sum], 0),
            jnp.concatenate([own_sum, other_sum], 0),
        )
        core_start = (count - 2 + child) * rank
        core_rows = lax.dynamic_slice_in_dim(woodbury_cores, core_start, rank, 0)
        coefficient = jnp.dot(
            core_rows, stacked, precision=highest, preferred_element_type=jnp.float32
        )
        field = field - jnp.dot(
            left_basis, coefficient, precision=highest, preferred_element_type=jnp.float32
        )
    return field


def solution(mesh):
    return jax.shard_map(
        shards,
        mesh=mesh,
        in_specs=(
            P(("parts", "wide", "narrow"), None),
            P(("parts", "wide", "narrow"), None),
            P(None, ("parts", "wide", "narrow"), None),
            P(None, ("parts", "wide", "narrow"), None),
            P("parts", None),
        ),
        out_specs=P(("parts", "wide", "narrow"), None),
        check_vma=False,
    )
```

profile of v0, /device:TPU:0, one launch (start us, length us, event | category | flops | bytes accessed | tf_op | source)
XLA Modules:
  0.0 96.2 jit_solution(15855102567742264007)
XLA Ops:
  0.0 0.0 copy-start
  0.0 1.6 %copy-done = f32[1024,512]{1,0:T(8,128)S(1)} copy-done((f32[1024,512]{1,0:T(8,128)S(1)}, f32[1024,512]{1,0:T(8,128)}, u32[]{:S(2)}) %copy-start) | copy-done | bytes 2097176
  1.6 8.8 %fusion.42 = f32[1024,512]{1,0:T(8,128)S(1)} fusion(f32[1024,1024]{1,0:T(8,128)} %param.6, f32[1024,512]{1,0:T(8,128)S(1)} %copy-done), kind=kOutput, calls=%fused_computation.51 | convolution fusion | flops 6442450944 | bytes 8388608 | tf_op jit(solution)/shard_map/dot_general | solution.py:23
  10.4 0.0 copy-start.3
  10.4 1.3 %copy-done.3 = f32[1024,512]{1,0:T(8,128)} copy-done((f32[1024,512]{1,0:T(8,128)}, f32[1024,512]{1,0:T(8,128)S(1)}, u32[]{:S(2)}) %copy-start.3) | copy-done | bytes 2097176
  11.7 2.5 %convolution_bitcast_fusion.2 = f32[128,512]{1,0:T(8,128)S(1)} fusion(f32[1024,512]{1,0:T(8,128)S(1)} %fusion.42, f32[3,1024,128]{2,1,0:T(8,128)} %param.8), kind=kOutput, calls=%fused_computation.5 | convolution fusion | flops 805306368 | bytes 2883584 | tf_op jit(solution)/shard_map/rk,rn->kn/dot_general | solution.py:31
  14.2 0.5 collective-permute-start
  14.8 1.2 %collective-permute-done = f32[128,512]{1,0:T(8,128)S(1)} collective-permute-done((f32[128,512]{1,0:T(8,128)S(1)}, f32[128,512]{1,0:T(8,128)S(1)}, u32[]{:S(2)}, u32[]{:S(2)}) %collective-permute-start) | collective-permute-done | bytes 262176 | tf_op jit(solution)/shard_map/ppermute | solution.py:14
  16.0 2.9 %collective-permute-start.1 = (f32[128,512]{1,0:T(8,128)S(1)}, f32[128,512]{1,0:T(8,128)S(1)}, u32[]{:S(2)}, u32[]{:S(2)}) collective-permute-start(f32[128,512]{1,0:T(8,128)S(1)} %add.31), channel_id=1, source_target_pairs={{0,2},{2,0},{4,6},{6,4},{8,10},{10,8},{12,14},{14,12},{1,3},{3,1},... | collective-permute-start | bytes 786440 | tf_op jit(solution)/shard_map/ppermute | solution.py:14
  18.9 6.6 %collective-permute-done.1 = f32[128,512]{1,0:T(8,128)S(1)} collective-permute-done((f32[128,512]{1,0:T(8,128)S(1)}, f32[128,512]{1,0:T(8,128)S(1)}, u32[]{:S(2)}, u32[]{:S(2)}) %collective-permute-start.1) | collective-permute-done | bytes 262176 | tf_op jit(solution)/shard_map/ppermute | solution.py:14
  25.5 1.4 %fusion = f32[128,512]{1,0:T(8,128)S(1)} fusion(f32[128,512]{1,0:T(8,128)S(1)} %add.31, f32[128,512]{1,0:T(8,128)S(1)} %collective-permute-done.1, pred[]{:T(512)S(6)} %eq.9, f32[1792,256]{1,0:T(8,128)} %param.9, s32[]{:T(128)S(6)} %select_n.29), kind=kOutput, calls=%fused_computation.7 | convolution fusion | flops 201719808 | bytes 917509 | tf_op jit(solution)/shard_map/dot_general | solution.py:44
  26.9 3.6 %bitcast_subtract_fusion.2 = f32[1024,512]{1,0:T(8,128)S(1)} fusion(f32[1024,512]{1,0:T(8,128)} %copy-done.3, f32[128,512]{1,0:T(8,128)S(1)} %fusion, f32[3,1024,128]{2,1,0:T(8,128)} %param.7), kind=kOutput, calls=%fused_computation.2 | convolution fusion | flops 805830656 | bytes 4980736 | tf_op jit(solution)/shard_map/dot_general | solution.py:47
  30.4 0.0 copy-start.2
  30.4 2.9 %convolution_bitcast_fusion.1 = f32[128,512]{1,0:T(8,128)S(1)} fusion(f32[1024,512]{1,0:T(8,128)S(1)} %bitcast_subtract_fusion.2, f32[3,1024,128]{2,1,0:T(8,128)} %param.8), kind=kOutput, calls=%fused_computation.4 | convolution fusion | flops 805306368 | bytes 2883584 | tf_op jit(solution)/shard_map/rk,rn->kn/dot_general | solution.py:31
  33.3 0.1 collective-permute-start.2
  33.4 1.5 %collective-permute-done.2 = f32[128,512]{1,0:T(8,128)S(1)} collective-permute-done((f32[128,512]{1,0:T(8,128)S(1)}, f32[128,512]{1,0:T(8,128)S(1)}, u32[]{:S(2)}, u32[]{:S(2)}) %collective-permute-start.2) | collective-permute-done | bytes 262176 | tf_op jit(solution)/shard_map/ppermute | solution.py:14
  35.0 1.8 %collective-permute-start.3 = (f32[128,512]{1,0:T(8,128)S(1)}, f32[128,512]{1,0:T(8,128)S(1)}, u32[]{:S(2)}, u32[]{:S(2)}) collective-permute-start(f32[128,512]{1,0:T(8,128)S(1)} %add.34), channel_id=1, source_target_pairs={{0,2},{2,0},{4,6},{6,4},{8,10},{10,8},{12,14},{14,12},{1,3},{3,1},... | collective-permute-start | bytes 786440 | tf_op jit(solution)/shard_map/ppermute | solution.py:14
  36.8 6.6 %collective-permute-done.3 = f32[128,512]{1,0:T(8,128)S(1)} collective-permute-done((f32[128,512]{1,0:T(8,128)S(1)}, f32[128,512]{1,0:T(8,128)S(1)}, u32[]{:S(2)}, u32[]{:S(2)}) %collective-permute-start.3) | collective-permute-done | bytes 262176 | tf_op jit(solution)/shard_map/ppermute | solution.py:14
  43.4 0.0 copy-done.2
  43.4 1.9 %collective-permute-start.4 = (f32[128,512]{1,0:T(8,128)S(1)}, f32[128,512]{1,0:T(8,128)S(1)}, u32[]{:S(2)}, u32[]{:S(2)}) collective-permute-start(f32[128,512]{1,0:T(8,128)S(1)} %add.35), channel_id=1, source_target_pairs={{0,4},{4,0},{2,6},{6,2},{8,12},{12,8},{10,14},{14,10},{1,5},{5,1},... | collective-permute-start | bytes 786440 | tf_op jit(solution)/shard_map/ppermute | solution.py:14
  45.3 5.8 %collective-permute-done.4 = f32[128,512]{1,0:T(8,128)S(1)} collective-permute-done((f32[128,512]{1,0:T(8,128)S(1)}, f32[128,512]{1,0:T(8,128)S(1)}, u32[]{:S(2)}, u32[]{:S(2)}) %collective-permute-start.4) | collective-permute-done | bytes 262176 | tf_op jit(solution)/shard_map/ppermute | solution.py:14
  51.1 1.4 %fusion.6 = f32[128,512]{1,0:T(8,128)S(1)} fusion(f32[128,512]{1,0:T(8,128)S(1)} %add.35, f32[128,512]{1,0:T(8,128)S(1)} %collective-permute-done.4, pred[]{:T(512)S(6)} %eq.10, f32[1792,256]{1,0:T(8,128)} %param.9, s32[]{:T(128)S(6)} %select_n.32), kind=kOutput, calls=%fused_computation.14 | convolution fusion | flops 201719808 | bytes 917509 | tf_op jit(solution)/shard_map/dot_general | solution.py:44
  52.5 3.6 %bitcast_subtract_fusion.1 = f32[1024,512]{1,0:T(8,128)S(1)} fusion(f32[1024,512]{1,0:T(8,128)} %copy-done.2, f32[128,512]{1,0:T(8,128)S(1)} %fusion.6, f32[3,1024,128]{2,1,0:T(8,128)} %param.7), kind=kOutput, calls=%fused_computation.1 | convolution fusion | flops 805830656 | bytes 4980736 | tf_op jit(solution)/shard_map/dot_general | solution.py:47
  56.0 0.0 copy-start.1
  56.1 2.9 %convolution_bitcast_fusion = f32[128,512]{1,0:T(8,128)S(1)} fusion(f32[1024,512]{1,0:T(8,128)S(1)} %bitcast_subtract_fusion.1, f32[3,1024,128]{2,1,0:T(8,128)} %param.8), kind=kOutput, calls=%fused_computation.3 | convolution fusion | flops 805306368 | bytes 2883584 | tf_op jit(solution)/shard_map/rk,rn->kn/dot_general | solution.py:31
  58.9 0.1 collective-permute-start.5
  59.0 1.5 %collective-permute-done.5 = f32[128,512]{1,0:T(8,128)S(1)} collective-permute-done((f32[128,512]{1,0:T(8,128)S(1)}, f32[128,512]{1,0:T(8,128)S(1)}, u32[]{:S(2)}, u32[]{:S(2)}) %collective-permute-start.5) | collective-permute-done | bytes 262176 | tf_op jit(solution)/shard_map/ppermute | solution.py:14
  60.6 1.7 %collective-permute-start.6 = (f32[128,512]{1,0:T(8,128)S(1)}, f32[128,512]{1,0:T(8,128)S(1)}, u32[]{:S(2)}, u32[]{:S(2)}) collective-permute-start(f32[128,512]{1,0:T(8,128)S(1)} %add.37), channel_id=1, source_target_pairs={{0,2},{2,0},{4,6},{6,4},{8,10},{10,8},{12,14},{14,12},{1,3},{3,1},... | collective-permute-start | bytes 786440 | tf_op jit(solution)/shard_map/ppermute | solution.py:14
  62.3 6.7 %collective-permute-done.6 = f32[128,512]{1,0:T(8,128)S(1)} collective-permute-done((f32[128,512]{1,0:T(8,128)S(1)}, f32[128,512]{1,0:T(8,128)S(1)}, u32[]{:S(2)}, u32[]{:S(2)}) %collective-permute-start.6) | collective-permute-done | bytes 262176 | tf_op jit(solution)/shard_map/ppermute | solution.py:14
  69.0 0.0 copy-done.1
  69.0 1.8 %collective-permute-start.7 = (f32[128,512]{1,0:T(8,128)S(1)}, f32[128,512]{1,0:T(8,128)S(1)}, u32[]{:S(2)}, u32[]{:S(2)}) collective-permute-start(f32[128,512]{1,0:T(8,128)S(1)} %add.38), channel_id=1, source_target_pairs={{0,4},{4,0},{2,6},{6,2},{8,12},{12,8},{10,14},{14,10},{1,5},{5,1},... | collective-permute-start | bytes 786440 | tf_op jit(solution)/shard_map/ppermute | solution.py:14
  70.8 5.8 %collective-permute-done.7 = f32[128,512]{1,0:T(8,128)S(1)} collective-permute-done((f32[128,512]{1,0:T(8,128)S(1)}, f32[128,512]{1,0:T(8,128)S(1)}, u32[]{:S(2)}, u32[]{:S(2)}) %collective-permute-start.7) | collective-permute-done | bytes 262176 | tf_op jit(solution)/shard_map/ppermute | solution.py:14
  76.7 2.8 %collective-permute-start.8 = (f32[128,512]{1,0:T(8,128)S(1)}, f32[128,512]{1,0:T(8,128)S(1)}, u32[]{:S(2)}, u32[]{:S(2)}) collective-permute-start(f32[128,512]{1,0:T(8,128)S(1)} %add.39), channel_id=1, source_target_pairs={{0,8},{8,0},{2,10},{10,2},{4,12},{12,4},{6,14},{14,6},{1,9},{9,1},... | collective-permute-start | bytes 786440 | tf_op jit(solution)/shard_map/ppermute | solution.py:14
  79.5 10.5 %collective-permute-done.8 = f32[128,512]{1,0:T(8,128)S(1)} collective-permute-done((f32[128,512]{1,0:T(8,128)S(1)}, f32[128,512]{1,0:T(8,128)S(1)}, u32[]{:S(2)}, u32[]{:S(2)}) %collective-permute-start.8) | collective-permute-done | bytes 262176 | tf_op jit(solution)/shard_map/ppermute | solution.py:14
  90.0 1.4 %fusion.12 = f32[128,512]{1,0:T(8,128)S(1)} fusion(f32[128,512]{1,0:T(8,128)S(1)} %add.39, f32[128,512]{1,0:T(8,128)S(1)} %collective-permute-done.8, pred[]{:T(512)S(6)} %eq.11, f32[1792,256]{1,0:T(8,128)} %param.9, s32[]{:T(128)S(6)} %select_n.35), kind=kOutput, calls=%fused_computation.21 | convolution fusion | flops 201719808 | bytes 917509 | tf_op jit(solution)/shard_map/dot_general | solution.py:44
  91.3 4.9 %bitcast_subtract_fusion = f32[1024,512]{1,0:T(8,128)} fusion(f32[1024,512]{1,0:T(8,128)} %copy-done.1, f32[128,512]{1,0:T(8,128)S(1)} %fusion.12, f32[3,1024,128]{2,1,0:T(8,128)} %param.7), kind=kOutput, calls=%fused_computation | convolution fusion | flops 805830656 | bytes 4980736 | tf_op jit(solution)/shard_map/dot_general | solution.py:47
  (6 shorter events, 0.2 us)
Async XLA Ops:
  0.0 1.6 %copy-start = (f32[1024,512]{1,0:T(8,128)S(1)}, f32[1024,512]{1,0:T(8,128)}, u32[]{:S(2)}) copy-start(f32[1024,512]{1,0:T(8,128)} %param.5) | copy-start | bytes 6291460
  10.4 1.3 %copy-start.3 = (f32[1024,512]{1,0:T(8,128)}, f32[1024,512]{1,0:T(8,128)S(1)}, u32[]{:S(2)}) copy-start(f32[1024,512]{1,0:T(8,128)S(1)} %fusion.42) | copy-start | bytes 6291460
  14.2 1.7 %collective-permute-start = (f32[128,512]{1,0:T(8,128)S(1)}, f32[128,512]{1,0:T(8,128)S(1)}, u32[]{:S(2)}, u32[]{:S(2)}) collective-permute-start(f32[128,512]{1,0:T(8,128)S(1)} %convolution_bitcast_fusion.2), channel_id=1, source_target_pairs={{0,1},{1,0},{2,3},{3,2},{4,5},{5,4},{6,7},{7,6},{8,9},{9,8},{10,11... | collective-permute-start | bytes 786440 | tf_op jit(solution)/shard_map/ppermute | solution.py:14
  16.0 9.5 %collective-permute-start.1 = (f32[128,512]{1,0:T(8,128)S(1)}, f32[128,512]{1,0:T(8,128)S(1)}, u32[]{:S(2)}, u32[]{:S(2)}) collective-permute-start(f32[128,512]{1,0:T(8,128)S(1)} %add.31), channel_id=1, source_target_pairs={{0,2},{2,0},{4,6},{6,4},{8,10},{10,8},{12,14},{14,12},{1,3},{3,1},... | collective-permute-start | bytes 786440 | tf_op jit(solution)/shard_map/ppermute | solution.py:14
  30.4 13.0 %copy-start.2 = (f32[1024,512]{1,0:T(8,128)}, f32[1024,512]{1,0:T(8,128)S(1)}, u32[]{:S(2)}) copy-start(f32[1024,512]{1,0:T(8,128)S(1)} %bitcast_subtract_fusion.2) | copy-start | bytes 6291460
  33.3 1.6 %collective-permute-start.2 = (f32[128,512]{1,0:T(8,128)S(1)}, f32[128,512]{1,0:T(8,128)S(1)}, u32[]{:S(2)}, u32[]{:S(2)}) collective-permute-start(f32[128,512]{1,0:T(8,128)S(1)} %convolution_bitcast_fusion.1), channel_id=1, source_target_pairs={{0,1},{1,0},{2,3},{3,2},{4,5},{5,4},{6,7},{7,6},{8,9},{9,8},{10,11... | collective-permute-start | bytes 786440 | tf_op jit(solution)/shard_map/ppermute | solution.py:14
  35.0 8.4 %collective-permute-start.3 = (f32[128,512]{1,0:T(8,128)S(1)}, f32[128,512]{1,0:T(8,128)S(1)}, u32[]{:S(2)}, u32[]{:S(2)}) collective-permute-start(f32[128,512]{1,0:T(8,128)S(1)} %add.34), channel_id=1, source_target_pairs={{0,2},{2,0},{4,6},{6,4},{8,10},{10,8},{12,14},{14,12},{1,3},{3,1},... | collective-permute-start | bytes 786440 | tf_op jit(solution)/shard_map/ppermute | solution.py:14
  43.4 7.7 %collective-permute-start.4 = (f32[128,512]{1,0:T(8,128)S(1)}, f32[128,512]{1,0:T(8,128)S(1)}, u32[]{:S(2)}, u32[]{:S(2)}) collective-permute-start(f32[128,512]{1,0:T(8,128)S(1)} %add.35), channel_id=1, source_target_pairs={{0,4},{4,0},{2,6},{6,2},{8,12},{12,8},{10,14},{14,10},{1,5},{5,1},... | collective-permute-start | bytes 786440 | tf_op jit(solution)/shard_map/ppermute | solution.py:14
  56.0 13.0 %copy-start.1 = (f32[1024,512]{1,0:T(8,128)}, f32[1024,512]{1,0:T(8,128)S(1)}, u32[]{:S(2)}) copy-start(f32[1024,512]{1,0:T(8,128)S(1)} %bitcast_subtract_fusion.1) | copy-start | bytes 6291460
  58.9 1.6 %collective-permute-start.5 = (f32[128,512]{1,0:T(8,128)S(1)}, f32[128,512]{1,0:T(8,128)S(1)}, u32[]{:S(2)}, u32[]{:S(2)}) collective-permute-start(f32[128,512]{1,0:T(8,128)S(1)} %convolution_bitcast_fusion), channel_id=1, source_target_pairs={{0,1},{1,0},{2,3},{3,2},{4,5},{5,4},{6,7},{7,6},{8,9},{9,8},{10,11... | collective-permute-start | bytes 786440 | tf_op jit(solution)/shard_map/ppermute | solution.py:14
  60.6 8.4 %collective-permute-start.6 = (f32[128,512]{1,0:T(8,128)S(1)}, f32[128,512]{1,0:T(8,128)S(1)}, u32[]{:S(2)}, u32[]{:S(2)}) collective-permute-start(f32[128,512]{1,0:T(8,128)S(1)} %add.37), channel_id=1, source_target_pairs={{0,2},{2,0},{4,6},{6,4},{8,10},{10,8},{12,14},{14,12},{1,3},{3,1},... | collective-permute-start | bytes 786440 | tf_op jit(solution)/shard_map/ppermute | solution.py:14
  69.0 7.6 %collective-permute-start.7 = (f32[128,512]{1,0:T(8,128)S(1)}, f32[128,512]{1,0:T(8,128)S(1)}, u32[]{:S(2)}, u32[]{:S(2)}) collective-permute-start(f32[128,512]{1,0:T(8,128)S(1)} %add.38), channel_id=1, source_target_pairs={{0,4},{4,0},{2,6},{6,2},{8,12},{12,8},{10,14},{14,10},{1,5},{5,1},... | collective-permute-start | bytes 786440 | tf_op jit(solution)/shard_map/ppermute | solution.py:14
  76.7 13.3 %collective-permute-start.8 = (f32[128,512]{1,0:T(8,128)S(1)}, f32[128,512]{1,0:T(8,128)S(1)}, u32[]{:S(2)}, u32[]{:S(2)}) collective-permute-start(f32[128,512]{1,0:T(8,128)S(1)} %add.39), channel_id=1, source_target_pairs={{0,8},{8,0},{2,10},{10,2},{4,12},{12,4},{6,14},{14,6},{1,9},{9,1},... | collective-permute-start | bytes 786440 | tf_op jit(solution)/shard_map/ppermute | solution.py:14
where the time goes:
time: 96.6 us; the launch traced here: 96.2 us
  waiting for transfers between devices  46.1 us (48%)
  matrix products  33.1 us (34%)
  starting transfers between devices  13.6 us (14%)
  local copies, waits for them, and re-layouts  2.92 us (3%)
    ppermute x9, waiting for transfers between devices, swapped(): return lax.ppermute(block, axis, route)  46.1 us
    ppermute x9, starting transfers between devices, swapped(): return lax.ppermute(block, axis, route)  13.6 us
    dot_general x3, matrix products, shards(): jnp.dot(left_basis, coefficient, precision=highest, preferred_element_typ...  12 us
    dot_general x1, matrix products, shards(): jnp.dot(leaf_inverse, right_side, precision=highest, preferred_element_ty...  8.81 us
    dot_general x3, matrix products, shards(): own_sum = jnp.einsum('rk,rn->kn', dual_basis, field, precision=highest)  8.21 us
    dot_general x3, matrix products, shards(): jnp.dot(core_rows, stacked, precision=highest, preferred_element_type=jnp...  4.07 us
    unnamed x8, local copies, waits for them, and re-layouts  2.92 us
  transfers between devices with their start and end apart: 9, of which 9 were waited for; matrix products, arithmetic and copies ran while one was open for 0% of the time, Pallas kernels for 0%

commit v1 on v0

v1 whole, which is shorter than its diff:
```python
import jax
import jax.numpy as jnp
from jax import lax
from jax.sharding import PartitionSpec as P

PRECISION = lax.Precision.HIGH


def mul(a, b):
    return jnp.dot(a, b, precision=PRECISION, preferred_element_type=jnp.float32)


def mul_t(a, b):
    return lax.dot_general(
        a, b, (((0,), (0,)), ((), ())), precision=PRECISION, preferred_element_type=jnp.float32
    )


def swap_wide(block, bit):
    count = lax.axis_size("wide")
    return lax.ppermute(block, "wide", [(w, w ^ (1 << bit)) for w in range(count)])


def swap_narrow(block):
    return lax.ppermute(block, "narrow", [(0, 1), (1, 0)])


def swap_crossed(block, first, second):
    wides, cores = lax.axis_size("wide"), lax.axis_size("narrow")
    route = []
    for w in range(wides):
        for n in range(cores):
            bit = first if n == 0 else second
            route.append((w * cores + n, (w ^ (1 << bit)) * cores + n))
    return lax.ppermute(block, ("wide", "narrow"), route)


def ordered(slot, own, other, axis=0):
    return jnp.where(
        slot == 0,
        jnp.concatenate([own, other], axis),
        jnp.concatenate([other, own], axis),
    )


def shards(right_side, leaf_inverse, row_bases, dual_bases, woodbury_cores):
    rank = row_bases.shape[2]
    rows = row_bases.shape[1]
    cols = right_side.shape[1]
    half = cols // 2
    depth = lax.axis_size("wide").bit_length() - 1
    rest = depth - 3
    bit3, bit2, bit1 = rest, rest + 1, rest + 2
    child = jnp.right_shift(lax.axis_index("wide"), rest)
    pair, side = jnp.right_shift(child, 1), jnp.right_shift(child, 2)
    slot3, slot2, slot1 = jnp.bitwise_and(child, 1), jnp.bitwise_and(pair, 1), side
    core = lax.axis_index("narrow")

    m13, m23 = mul_t(dual_bases[0], row_bases[2]), mul_t(dual_bases[1], row_bases[2])
    m12 = mul_t(dual_bases[0], row_bases[1])
    m = jnp.concatenate([m23, m13, m12], 0)
    for bit in range(rest):
        m = m + swap_wide(m, bit)
    m_other = swap_wide(m, bit3)
    m12_pair = m[2 * rank:] + m_other[2 * rank:]
    m12_other = swap_wide(m12_pair, bit2)
    cores3 = lax.dynamic_slice_in_dim(woodbury_cores, (3 + pair) * 2 * rank, 2 * rank, 0)
    cores2 = lax.dynamic_slice_in_dim(woodbury_cores, (1 + side) * 2 * rank, 2 * rank, 0)
    cores1 = woodbury_cores[: 2 * rank]
    bf = mul(
        ordered(slot3, m[: 2 * rank], m_other[: 2 * rank], 1),
        lax.dynamic_slice_in_dim(cores3, slot3 * rank, rank, 1),
    )
    e = mul(
        ordered(slot2, m12_pair, m12_other, 1),
        lax.dynamic_slice_in_dim(cores2, slot2 * rank, rank, 1),
    )
    bfe = jnp.concatenate([bf, e], 0)
    bfe = bfe + swap_narrow(bfe)

    duals = jnp.concatenate([dual_bases[0], dual_bases[1], dual_bases[2]], 1)
    g = mul_t(duals, leaf_inverse)
    keep = lax.dynamic_slice_in_dim(right_side, core * half, half, 1)
    send = lax.dynamic_slice_in_dim(right_side, (1 - core) * half, half, 1)
    q = mul(g, keep) + swap_narrow(mul(g, send))
    for bit in range(rest):
        q = q + swap_wide(q, bit)
    q1, q2, q3 = q[:rank], q[rank: 2 * rank], q[2 * rank:]
    v = q2 - mul(bfe[:rank], q3)
    w = q1 - mul(bfe[rank: 2 * rank], q3) - mul(bfe[2 * rank:], v)

    w = w + swap_crossed(w, bit2, bit3)
    w = w + swap_crossed(w, bit3, bit2)
    w_other = swap_wide(w, bit1)
    k1 = mul(
        lax.dynamic_slice_in_dim(cores1, slot1 * rank, rank, 0), ordered(slot1, w, w_other)
    )
    v = v + swap_wide(v, bit3)
    v_other = swap_wide(v, bit2)
    k2 = mul(
        lax.dynamic_slice_in_dim(cores2, slot2 * rank, rank, 0), ordered(slot2, v, v_other)
    )
    q_other = swap_wide(q3, bit3)
    k3 = mul(
        lax.dynamic_slice_in_dim(cores3, slot3 * rank, rank, 0), ordered(slot3, q3, q_other)
    )

    k23 = jnp.concatenate([k2, k3], 0)
    k23_other = swap_narrow(k23)
    k1_other = swap_narrow(k1)
    field = mul(leaf_inverse, right_side)
    lefts = jnp.concatenate([row_bases[1], row_bases[2]], 1)
    field = field - mul(lefts, ordered(core, k23, k23_other, 1))
    return field - mul(row_bases[0], ordered(core, k1, k1_other, 1))


def solution(mesh):
    return jax.shard_map(
        shards,
        mesh=mesh,
        in_specs=(
            P(("parts", "wide", "narrow"), None),
            P(("parts", "wide", "narrow"), None),
            P(None, ("parts", "wide", "narrow"), None),
            P(None, ("parts", "wide", "narrow"), None),
            P("parts", None),
        ),
        out_specs=P(("parts", "wide", "narrow"), None),
        check_vma=False,
    )
```

time: 96.6 us -> 56 us (0.58)
  waiting for transfers between devices: 46.1 us -> 8.63 us
  matrix products: 33.1 us -> 29.2 us
  starting transfers between devices: 13.6 us -> 12.1 us
  other arithmetic: 0.24 us -> 1.5 us
    ppermute x9 -> x12, waiting for transfers between devices: 46.1 us -> 8.63 us  [the longest x6 6.71 us: swap_wide(): lax.ppermute(block, 'wide', [(w, w ^ 1 << bit) for w in range(count)])]
    dot_general x10 -> x17, matrix products: 33.1 us -> 29.2 us  [the longest x13 19.1 us: mul(): jnp.dot(a, b, precision=PRECISION, preferred_element_type=jnp.float32)]
    unnamed x8 -> x14, local copies, waits for them, and re-layouts: 2.92 us -> 1.17 us
    slice x0 -> x3, local copies, waits for them, and re-layouts: none -> 1.69 us  [the longest x1 1.67 us: shards(): cores1 = woodbury_cores[:2 * rank]]
    ppermute x9 -> x12, starting transfers between devices: 13.6 us -> 12.1 us  [the longest x6 9.87 us: swap_wide(): lax.ppermute(block, 'wide', [(w, w ^ 1 << bit) for w in range(count)])]
    concatenate x0 -> x3, other arithmetic: none -> 1.42 us  [the longest x1 0.72 us: shards(): k23 = jnp.concatenate([k2, k3], 0)]
  transfers between devices with their start and end apart: 9 -> 12, of which waited for: 9 -> 5; matrix products, arithmetic and copies ran while one was open for 0% -> 42% of each run, Pallas kernels for 0% -> 0%
where the time goes in v1:
time: 56 us; the launch traced here: 55.6 us
  matrix products  29.2 us (52%)
  starting transfers between devices  12.1 us (22%)
  waiting for transfers between devices  8.63 us (15%)
  local copies, waits for them, and re-layouts  3.82 us (7%)
  other arithmetic  1.5 us (3%)
    dot_general x13, matrix products, mul(): jnp.dot(a, b, precision=PRECISION, preferred_element_type=jnp.float32)  19.1 us
    dot_general x4, matrix products, mul_t(): lax.dot_general(a, b, (((0,), (0,)), ((), ())), precision=PRECISION, pref...  10.1 us
    ppermute x6, starting transfers between devices, swap_wide(): lax.ppermute(block, 'wide', [(w, w ^ 1 << bit) for w in range(count)])  9.87 us
    ppermute x6, waiting for transfers between devices, swap_wide(): lax.ppermute(block, 'wide', [(w, w ^ 1 << bit) for w in range(count)])  6.71 us
    ppermute x2, starting transfers between devices, swap_crossed(): return lax.ppermute(block, ('wide', 'narrow'), route)  2.03 us
    slice x1, local copies, waits for them, and re-layouts, shards(): cores1 = woodbury_cores[:2 * rank]  1.67 us
    ppermute x2, waiting for transfers between devices, swap_crossed(): return lax.ppermute(block, ('wide', 'narrow'), route)  1.34 us
    unnamed x14, local copies, waits for them, and re-layouts  1.17 us
  transfers between devices with their start and end apart: 12, of which 5 were waited for; matrix products, arithmetic and copies ran while one was open for 42% of the time, Pallas kernels for 0%

profile of v1, /device:TPU:0, one launch (start us, length us, event | category | flops | bytes accessed | tf_op | source)
XLA Modules:
  0.0 55.6 jit_solution(13749378332072818492)
XLA Ops:
  0.0 1.9 %fusion.101 = f32[128,128]{1,0:T(8,128)S(1)} fusion(f32[3,1024,128]{2,1,0:T(8,128)} %param.7, f32[3,1024,128]{2,1,0:T(8,128)} %param.8), kind=kOutput, calls=%fused_computation.117 | convolution fusion | flops 100663296 | bytes 1114112 | tf_op jit(solution)/shard_map/dot_general | solution.py:14
  2.0 1.8 %fusion.102 = f32[128,128]{1,0:T(8,128)S(1)} fusion(f32[3,1024,128]{2,1,0:T(8,128)} %param.8, f32[3,1024,128]{2,1,0:T(8,128)} %param.7), kind=kOutput, calls=%fused_computation.118 | convolution fusion | flops 100663296 | bytes 1114112 | tf_op jit(solution)/shard_map/dot_general | solution.py:14
  3.8 1.6 %fusion.104 = f32[128,128]{1,0:T(8,128)S(1)} fusion(f32[3,1024,128]{2,1,0:T(8,128)} %param.7, f32[3,1024,128]{2,1,0:T(8,128)S(1)} %copy-done.6), kind=kOutput, calls=%fused_computation.120 | convolution fusion | flops 100663296 | bytes 1114112 | tf_op jit(solution)/shard_map/dot_general | solution.py:14
  5.4 0.7 %pad_maximum_fusion.1 = f32[384,128]{1,0:T(8,128)} fusion(f32[128,128]{1,0:T(8,128)S(1)} %fusion.101, f32[128,128]{1,0:T(8,128)S(1)} %fusion.104, f32[128,128]{1,0:T(8,128)S(1)} %fusion.102), kind=kLoop, calls=%fused_computation.72 | loop fusion | flops 98304 | bytes 393216 | tf_op jit(solution)/shard_map/concatenate | solution.py:61
  6.1 2.9 %collective-permute-start.1 = (f32[384,128]{1,0:T(8,128)}, f32[384,128]{1,0:T(8,128)S(1)}, u32[]{:S(2)}, u32[]{:S(2)}) collective-permute-start(f32[384,128]{1,0:T(8,128)} %pad_maximum_fusion.1), channel_id=1, source_target_pairs={{0,2},{2,0},{4,6},{6,4},{8,10},{10,8},{12,14},{14,12},{1,3},{3,1},... | collective-permute-start | bytes 589832 | tf_op jit(solution)/shard_map/ppermute | solution.py:21
  9.0 0.9 %slice_bitcast_fusion.2 = (f32[1024,128]{1,0:T(8,128)S(1)}, f32[1024,128]{1,0:T(8,128)S(1)}, f32[1024,128]{1,0:T(8,128)}) fusion(f32[3,1024,128]{2,1,0:T(8,128)S(1)} %copy-done.6), kind=kLoop, calls=%fused_computation.29 | loop fusion | bytes 3145728 | tf_op jit(solution)/shard_map/squeeze | solution.py:81
  9.9 4.8 %fusion = f32[384,1024]{1,0:T(8,128)S(1)} fusion(f32[1024,1024]{1,0:T(8,128)} %param.6, f32[1024,128]{1,0:T(8,128)S(1)} %get-tuple-element.6, f32[1024,128]{1,0:T(8,128)} %get-tuple-element.7, f32[1024,128]{1,0:T(8,128)S(1)} %get-tuple-element.5), kind=kOutput, calls=%fused_computation.1 | convolution fusion | flops 2416705536 | bytes 7340032 | tf_op jit(solution)/shard_map/dot_general | solution.py:14
  14.7 0.0 copy-start.2
  14.7 1.1 %copy-done.2 = f32[384,1024]{1,0:T(8,128)} copy-done((f32[384,1024]{1,0:T(8,128)}, f32[384,1024]{1,0:T(8,128)S(1)}, u32[]{:S(2)}) %copy-start.2) | copy-done | bytes 1572888
  15.8 0.9 %fusion.10 = f32[384,256]{1,0:T(8,128)S(1)} fusion(f32[384,1024]{1,0:T(8,128)S(1)} %fusion, f32[1024,512]{1,0:T(8,128)S(1)} %copy-done, s32[]{:T(128)S(6)} %select_n.86), kind=kOutput, calls=%fused_computation.12 | convolution fusion | flops 603979776 | bytes 3014660 | tf_op jit(solution)/shard_map/dot_general | solution.py:10
  16.7 0.1 collective-permute-start
  16.8 0.0 copy-start.3
  16.8 0.0 collective-permute-done.1
  16.8 1.6 %collective-permute-start.2 = (f32[128,128]{1,0:T(8,128)S(1)}, f32[128,128]{1,0:T(8,128)S(1)}, u32[]{:S(2)}, u32[]{:S(2)}) collective-permute-start(f32[128,128]{1,0:T(8,128)S(1)} %slice_add_fusion), channel_id=1, source_target_pairs={{0,4},{2,6},{4,0},{6,2},{8,12},{10,14},{12,8},{14,10},{1,5},{3,7},... | collective-permute-start | bytes 196616 | tf_op jit(solution)/shard_map/ppermute | solution.py:21
  18.5 1.3 %fusion.24 = f32[256,128]{1,0:T(8,128)S(1)} fusion(f32[256,128]{1,0:T(8,128)S(1)} %slice.69, f32[128,128]{1,0:T(8,128)S(1)} %fusion.104, f32[128,128]{1,0:T(8,128)S(1)} %fusion.102, f32[1792,256]{1,0:T(8,128)} %param.9, s32[]{:T(128)S(6)} %select_n.90, s32[]{:T(128)S(6)} %select_n.92, pred[]{:T(512)S(6)} %eq.17), kind=kOutput, calls=%fused_computation.33 | convolution fusion | flops 50659328 | bytes 524297 | tf_op jit(solution)/shard_map/dot_general | solution.py:10
  19.8 1.5 %collective-permute-done.2 = f32[128,128]{1,0:T(8,128)S(1)} collective-permute-done((f32[128,128]{1,0:T(8,128)S(1)}, f32[128,128]{1,0:T(8,128)S(1)}, u32[]{:S(2)}, u32[]{:S(2)}) %collective-permute-start.2) | collective-permute-done | bytes 65568 | tf_op jit(solution)/shard_map/ppermute | solution.py:21
  21.3 1.2 %fusion.59 = f32[128,128]{1,0:T(8,128)S(1)} fusion(f32[128,128]{1,0:T(8,128)S(1)} %collective-permute-done.2, f32[128,128]{1,0:T(8,128)S(1)} %slice_add_fusion, f32[1792,256]{1,0:T(8,128)} %param.9, s32[]{:T(128)S(6)} %select_n.83, s32[]{:T(128)S(6)} %select_n.81, pred[]{:T(512)S(6)} %eq.16), kind=kOutput, calls=%fused_computation.78 | convolution fusion | flops 25264128 | bytes 327689 | tf_op jit(solution)/shard_map/dot_general | solution.py:10
  22.6 0.1 collective-permute-start.3
  22.7 0.0 collective-permute-done
  22.7 0.0 copy-start.1
  22.7 0.8 %convolution_add_fusion = f32[384,256]{1,0:T(8,128)S(1)} fusion(f32[384,256]{1,0:T(8,128)S(1)} %collective-permute-done, f32[384,1024]{1,0:T(8,128)S(1)} %copy-done.3, f32[1024,512]{1,0:T(8,128)S(1)} %copy-done, s32[]{:T(128)S(6)} %select_n.85), kind=kOutput, calls=%fused_computation.7 | convolution fusion | flops 604078080 | bytes 3407876 | tf_op jit(solution)/shard_map/dot_general | solution.py:10
  23.5 0.6 %collective-permute-done.3 = f32[384,128]{1,0:T(8,128)S(1)} collective-permute-done((f32[384,128]{1,0:T(8,128)S(1)}, f32[384,128]{1,0:T(8,128)S(1)}, u32[]{:S(2)}, u32[]{:S(2)}) %collective-permute-start.3) | collective-permute-done | bytes 196640 | tf_op jit(solution)/shard_map/ppermute | solution.py:25
  24.1 0.2 fusion.79
  24.4 0.2 slice_subtract_fusion.1
  24.6 0.2 fusion.58
  24.8 1.6 %collective-permute-start.8 = (f32[128,256]{1,0:T(8,128)S(1)}, f32[128,256]{1,0:T(8,128)S(1)}, u32[]{:S(2)}, u32[]{:S(2)}) collective-permute-start(f32[128,256]{1,0:T(8,128)S(1)} %fusion.58), channel_id=1, source_target_pairs={{0,4},{1,3},{2,6},{3,1},{4,0},{5,7},{6,2},{7,5},{8,12},{9,11},{10,... | collective-permute-start | bytes 393224 | tf_op jit(solution)/shard_map/ppermute | solution.py:35
  26.4 0.5 collective-permute-start.4
  26.9 1.6 %collective-permute-start.6 = (f32[128,256]{1,0:T(8,128)S(1)}, f32[128,256]{1,0:T(8,128)S(1)}, u32[]{:S(2)}, u32[]{:S(2)}) collective-permute-start(f32[128,256]{1,0:T(8,128)S(1)} %slice.72), channel_id=1, source_target_pairs={{0,2},{2,0},{4,6},{6,4},{8,10},{10,8},{12,14},{14,12},{1,3},{3,1},... | collective-permute-start | bytes 393224 | tf_op jit(solution)/shard_map/ppermute | solution.py:21
  28.5 1.3 %collective-permute-done.8 = f32[128,256]{1,0:T(8,128)S(1)} collective-permute-done((f32[128,256]{1,0:T(8,128)S(1)}, f32[128,256]{1,0:T(8,128)S(1)}, u32[]{:S(2)}, u32[]{:S(2)}) %collective-permute-start.8) | collective-permute-done | bytes 131104 | tf_op jit(solution)/shard_map/ppermute | solution.py:35
  29.8 0.4 collective-permute-start.9
  30.3 2.5 %collective-permute-done.4 = f32[128,256]{1,0:T(8,128)S(1)} collective-permute-done((f32[128,256]{1,0:T(8,128)S(1)}, f32[128,256]{1,0:T(8,128)S(1)}, u32[]{:S(2)}, u32[]{:S(2)}) %collective-permute-start.4) | collective-permute-done | bytes 131104 | tf_op jit(solution)/shard_map/ppermute | solution.py:21
  32.8 0.5 collective-permute-start.5
  33.4 4.8 %fusion.105 = f32[1024,512]{1,0:T(8,128)} fusion(f32[1024,1024]{1,0:T(8,128)S(1)} %copy-done.1, f32[1024,512]{1,0:T(8,128)S(1)} %copy-done), kind=kOutput, calls=%fused_computation.121 | convolution fusion | flops 3221225472 | bytes 8388608 | tf_op jit(solution)/shard_map/dot_general | solution.py:10
  38.2 0.0 collective-permute-done.6
  38.2 1.3 %fusion.40 = f32[128,256]{1,0:T(8,128)S(1)} fusion(f32[128,256]{1,0:T(8,128)S(1)} %collective-permute-done.6, f32[128,256]{1,0:T(8,128)S(1)} %slice.72, f32[1792,256]{1,0:T(8,128)} %param.9, s32[]{:T(128)S(6)} %dynamic_slice.35, pred[]{:T(512)S(6)} %eq.17), kind=kOutput, calls=%fused_computation.51 | convolution fusion | flops 50528256 | bytes 524293 | tf_op jit(solution)/shard_map/dot_general | solution.py:10
  39.4 0.0 collective-permute-done.9
  39.5 2.7 %collective-permute-start.10 = (f32[128,256]{1,0:T(8,128)S(1)}, f32[128,256]{1,0:T(8,128)}, u32[]{:S(2)}, u32[]{:S(2)}) collective-permute-start(f32[128,256]{1,0:T(8,128)S(1)} %add.65), channel_id=1, source_target_pairs={{0,8},{2,10},{4,12},{6,14},{8,0},{10,2},{12,4},{14,6},{1,9},{3,11}... | collective-permute-start | bytes 393224 | tf_op jit(solution)/shard_map/ppermute | solution.py:21
  42.1 0.0 collective-permute-done.5
  42.1 1.2 %fusion.34 = f32[128,256]{1,0:T(8,128)S(1)} fusion(f32[128,256]{1,0:T(8,128)S(1)} %collective-permute-done.5, f32[128,256]{1,0:T(8,128)S(1)} %add.62, f32[1792,256]{1,0:T(8,128)} %param.9, s32[]{:T(128)S(6)} %dynamic_slice.29, pred[]{:T(512)S(6)} %eq.16), kind=kOutput, calls=%fused_computation.44 | convolution fusion | flops 50528256 | bytes 524293 | tf_op jit(solution)/shard_map/dot_general | solution.py:10
  43.3 0.7 %pad_maximum_fusion = f32[256,256]{1,0:T(8,128)} fusion(f32[128,256]{1,0:T(8,128)S(1)} %fusion.40, f32[128,256]{1,0:T(8,128)S(1)} %fusion.34), kind=kLoop, calls=%fused_computation.57 | loop fusion | flops 65536 | bytes 524288 | tf_op jit(solution)/shard_map/concatenate | solution.py:108
  44.0 0.1 slice_bitcast_fusion.4
  44.1 1.7 %slice.63 = f32[256,256]{1,0:T(8,128)} slice(f32[1792,256]{1,0:T(8,128)} %param.9), slice={[0:256], [0:256]} | slice | bytes 524288 | tf_op jit(solution)/shard_map/slice | solution.py:69
  45.8 2.6 %collective-permute-done.10 = f32[128,256]{1,0:T(8,128)} collective-permute-done((f32[128,256]{1,0:T(8,128)S(1)}, f32[128,256]{1,0:T(8,128)}, u32[]{:S(2)}, u32[]{:S(2)}) %collective-permute-start.10) | collective-permute-done | bytes 131104 | tf_op jit(solution)/shard_map/ppermute | solution.py:21
  48.4 1.3 %fusion.46 = f32[128,256]{1,0:T(8,128)S(1)} fusion(f32[128,256]{1,0:T(8,128)} %collective-permute-done.10, f32[128,256]{1,0:T(8,128)S(1)} %add.65, f32[256,256]{1,0:T(8,128)} %slice.63, s32[]{:T(128)S(6)} %select_n.99, pred[]{:T(512)S(6)} %eq.18), kind=kOutput, calls=%fused_computation.59 | convolution fusion | flops 50528256 | bytes 524293 | tf_op jit(solution)/shard_map/dot_general | solution.py:10
  49.7 0.1 collective-permute-start.11
  49.8 0.0 copy-start.4
  49.8 2.2 %fusion.6 = f32[1024,512]{1,0:T(8,128)S(1)} fusion(f32[1024,128]{1,0:T(8,128)S(1)} %get-tuple-element.9, f32[1024,128]{1,0:T(8,128)S(1)} %get-tuple-element.8, f32[256,256]{1,0:T(8,128)} %collective-permute-done.7, f32[128,256]{1,0:T(8,128)S(1)} %fusion.40, f32[128,256]{1,0:T(8,128)S(1)} %fusion.34, pred[]{:T(512)S(6)} %eq.15), kind=kOutput, calls=%fused_computation.8 | convolution fusion | flops 806223872 | bytes 3670017 | tf_op jit(solution)/shard_map/dot_general | solution.py:10
  52.0 3.6 %bitcast_subtract_fusion = f32[1024,512]{1,0:T(8,128)} fusion(f32[1024,512]{1,0:T(8,128)S(1)} %copy-done.4, f32[1024,512]{1,0:T(8,128)S(1)} %fusion.6, f32[3,1024,128]{2,1,0:T(8,128)} %param.7, f32[128,256]{1,0:T(8,128)S(1)} %collective-permute-done.11, f32[128,256]{1,0:T(8,128)S(1)} %fusion.46, pred[]{:T(512)S(6)} %eq.15), kind=kOutput, calls=%fused_computation | convolution fusion | flops 403898368 | bytes 7077889 | tf_op jit(solution)/shard_map/dot_general | solution.py:10
  (20 shorter events, 0.1 us)
Async XLA Ops:
  0.0 15.8 %copy-start = (f32[1024,512]{1,0:T(8,128)S(1)}, f32[1024,512]{1,0:T(8,128)}, u32[]{:S(2)}) copy-start(f32[1024,512]{1,0:T(8,128)} %param.5) | copy-start | bytes 6291460
  0.0 3.7 %copy-start.6 = (f32[3,1024,128]{2,1,0:T(8,128)S(1)}, f32[3,1024,128]{2,1,0:T(8,128)}, u32[]{:S(2)}) copy-start(f32[3,1024,128]{2,1,0:T(8,128)} %param.8) | copy-start | bytes 4718596
  6.1 10.7 %collective-permute-start.1 = (f32[384,128]{1,0:T(8,128)}, f32[384,128]{1,0:T(8,128)S(1)}, u32[]{:S(2)}, u32[]{:S(2)}) collective-permute-start(f32[384,128]{1,0:T(8,128)} %pad_maximum_fusion.1), channel_id=1, source_target_pairs={{0,2},{2,0},{4,6},{6,4},{8,10},{10,8},{12,14},{14,12},{1,3},{3,1},... | collective-permute-start | bytes 589832 | tf_op jit(solution)/shard_map/ppermute | solution.py:21
  14.7 1.1 %copy-start.2 = (f32[384,1024]{1,0:T(8,128)}, f32[384,1024]{1,0:T(8,128)S(1)}, u32[]{:S(2)}) copy-start(f32[384,1024]{1,0:T(8,128)S(1)} %fusion) | copy-start | bytes 4718596
  16.7 6.0 %collective-permute-start = (f32[384,256]{1,0:T(8,128)S(1)}, f32[384,256]{1,0:T(8,128)S(1)}, u32[]{:S(2)}, u32[]{:S(2)}) collective-permute-start(f32[384,256]{1,0:T(8,128)S(1)} %fusion.10), channel_id=1, source_target_pairs={{0,1},{1,0},{2,3},{3,2},{4,5},{5,4},{6,7},{7,6},{8,9},{9,8},{10,11... | collective-permute-start | bytes 1179656 | tf_op jit(solution)/shard_map/ppermute | solution.py:25
  16.8 5.9 %copy-start.3 = (f32[384,1024]{1,0:T(8,128)S(1)}, f32[384,1024]{1,0:T(8,128)}, u32[]{:S(2)}) copy-start(f32[384,1024]{1,0:T(8,128)} %copy-done.2) | copy-start | bytes 4718596
  16.8 4.5 %collective-permute-start.2 = (f32[128,128]{1,0:T(8,128)S(1)}, f32[128,128]{1,0:T(8,128)S(1)}, u32[]{:S(2)}, u32[]{:S(2)}) collective-permute-start(f32[128,128]{1,0:T(8,128)S(1)} %slice_add_fusion), channel_id=1, source_target_pairs={{0,4},{2,6},{4,0},{6,2},{8,12},{10,14},{12,8},{14,10},{1,5},{3,7},... | collective-permute-start | bytes 196616 | tf_op jit(solution)/shard_map/ppermute | solution.py:21
  22.6 1.5 %collective-permute-start.3 = (f32[384,128]{1,0:T(8,128)S(1)}, f32[384,128]{1,0:T(8,128)S(1)}, u32[]{:S(2)}, u32[]{:S(2)}) collective-permute-start(f32[384,128]{1,0:T(8,128)S(1)} %pad_maximum_fusion.2), channel_id=1, source_target_pairs={{0,1},{1,0},{2,3},{3,2},{4,5},{5,4},{6,7},{7,6},{8,9},{9,8},{10,11... | collective-permute-start | bytes 589832 | tf_op jit(solution)/shard_map/ppermute | solution.py:25
  22.7 10.7 %copy-start.1 = (f32[1024,1024]{1,0:T(8,128)S(1)}, f32[1024,1024]{1,0:T(8,128)}, u32[]{:S(2)}) copy-start(f32[1024,1024]{1,0:T(8,128)} %param.6) | copy-start | bytes 12582916
  24.8 5.0 %collective-permute-start.8 = (f32[128,256]{1,0:T(8,128)S(1)}, f32[128,256]{1,0:T(8,128)S(1)}, u32[]{:S(2)}, u32[]{:S(2)}) collective-permute-start(f32[128,256]{1,0:T(8,128)S(1)} %fusion.58), channel_id=1, source_target_pairs={{0,4},{1,3},{2,6},{3,1},{4,0},{5,7},{6,2},{7,5},{8,12},{9,11},{10,... | collective-permute-start | bytes 393224 | tf_op jit(solution)/shard_map/ppermute | solution.py:35
  26.4 6.4 %collective-permute-start.4 = (f32[128,256]{1,0:T(8,128)S(1)}, f32[128,256]{1,0:T(8,128)S(1)}, u32[]{:S(2)}, u32[]{:S(2)}) collective-permute-start(f32[128,256]{1,0:T(8,128)S(1)} %slice_subtract_fusion.1), channel_id=1, source_target_pairs={{0,2},{2,0},{4,6},{6,4},{8,10},{10,8},{12,14},{14,12},{1,3},{3,1},... | collective-permute-start | bytes 393224 | tf_op jit(solution)/shard_map/ppermute | solution.py:21
  26.9 11.2 %collective-permute-start.6 = (f32[128,256]{1,0:T(8,128)S(1)}, f32[128,256]{1,0:T(8,128)S(1)}, u32[]{:S(2)}, u32[]{:S(2)}) collective-permute-start(f32[128,256]{1,0:T(8,128)S(1)} %slice.72), channel_id=1, source_target_pairs={{0,2},{2,0},{4,6},{6,4},{8,10},{10,8},{12,14},{14,12},{1,3},{3,1},... | collective-permute-start | bytes 393224 | tf_op jit(solution)/shard_map/ppermute | solution.py:21
  29.8 9.6 %collective-permute-start.9 = (f32[128,256]{1,0:T(8,128)S(1)}, f32[128,256]{1,0:T(8,128)S(1)}, u32[]{:S(2)}, u32[]{:S(2)}) collective-permute-start(f32[128,256]{1,0:T(8,128)S(1)} %add.64), channel_id=1, source_target_pairs={{0,2},{1,5},{2,0},{3,7},{4,6},{5,1},{6,4},{7,3},{8,10},{9,13},{10,... | collective-permute-start | bytes 393224 | tf_op jit(solution)/shard_map/ppermute | solution.py:35
  32.8 9.3 %collective-permute-start.5 = (f32[128,256]{1,0:T(8,128)S(1)}, f32[128,256]{1,0:T(8,128)S(1)}, u32[]{:S(2)}, u32[]{:S(2)}) collective-permute-start(f32[128,256]{1,0:T(8,128)S(1)} %add.62), channel_id=1, source_target_pairs={{0,4},{2,6},{4,0},{6,2},{8,12},{10,14},{12,8},{14,10},{1,5},{3,7},... | collective-permute-start | bytes 393224 | tf_op jit(solution)/shard_map/ppermute | solution.py:21
  38.2 5.9 %copy-start.5 = (f32[3,1024,128]{2,1,0:T(8,128)S(1)}, f32[3,1024,128]{2,1,0:T(8,128)}, u32[]{:S(2)}) copy-start(f32[3,1024,128]{2,1,0:T(8,128)} %param.7) | copy-start | bytes 4718596
  39.5 8.9 %collective-permute-start.10 = (f32[128,256]{1,0:T(8,128)S(1)}, f32[128,256]{1,0:T(8,128)}, u32[]{:S(2)}, u32[]{:S(2)}) collective-permute-start(f32[128,256]{1,0:T(8,128)S(1)} %add.65), channel_id=1, source_target_pairs={{0,8},{2,10},{4,12},{6,14},{8,0},{10,2},{12,4},{14,6},{1,9},{3,11}... | collective-permute-start | bytes 393224 | tf_op jit(solution)/shard_map/ppermute | solution.py:21
  44.0 5.7 %collective-permute-start.7 = (f32[256,256]{1,0:T(8,128)}, f32[256,256]{1,0:T(8,128)}, u32[]{:S(2)}, u32[]{:S(2)}) collective-permute-start(f32[256,256]{1,0:T(8,128)} %pad_maximum_fusion), channel_id=1, source_target_pairs={{0,1},{1,0},{2,3},{3,2},{4,5},{5,4},{6,7},{7,6},{8,9},{9,8},{10,11... | collective-permute-start | bytes 786440 | tf_op jit(solution)/shard_map/ppermute | solution.py:25
  49.7 2.3 %collective-permute-start.11 = (f32[128,256]{1,0:T(8,128)S(1)}, f32[128,256]{1,0:T(8,128)S(1)}, u32[]{:S(2)}, u32[]{:S(2)}) collective-permute-start(f32[128,256]{1,0:T(8,128)S(1)} %fusion.46), channel_id=1, source_target_pairs={{0,1},{1,0},{2,3},{3,2},{4,5},{5,4},{6,7},{7,6},{8,9},{9,8},{10,11... | collective-permute-start | bytes 393224 | tf_op jit(solution)/shard_map/ppermute | solution.py:25
  49.8 2.2 %copy-start.4 = (f32[1024,512]{1,0:T(8,128)S(1)}, f32[1024,512]{1,0:T(8,128)}, u32[]{:S(2)}) copy-start(f32[1024,512]{1,0:T(8,128)} %fusion.105) | copy-start | bytes 6291460

commit v2 on v0

v2 whole, which is shorter than its diff:
```python
import functools

import jax
import jax.numpy as jnp
from jax import lax
from jax.experimental import pallas as pl
from jax.experimental.pallas import tpu as pltpu
from jax.sharding import PartitionSpec as P

F32, BF16 = jnp.float32, jnp.bfloat16
VMEM = pl.BlockSpec(memory_space=pltpu.VMEM)


def dot(a, b):
    return jnp.dot(a, b, precision=lax.Precision.HIGH, preferred_element_type=F32)


def dot_t(a, b):
    return lax.dot_general(
        a, b, (((0,), (0,)), ((), ())), precision=lax.Precision.HIGH, preferred_element_type=F32
    )


def halves(x):
    high = x.astype(BF16)
    return high, (x - high.astype(F32)).astype(BF16)


def dot3(a, b):
    def one(x, y):
        return jnp.dot(x, y, preferred_element_type=F32)

    return one(a[0], b[0]) + one(a[0], b[1]) + one(a[1], b[0])


def shape(*dims, dtype=F32):
    return jax.ShapeDtypeStruct(dims, dtype)


def call(body, outs, args, flops, scratch=(), aliases=None, out_specs=None):
    bytes_accessed = sum(a.size * a.dtype.itemsize for a in args)
    return pl.pallas_call(
        body,
        in_specs=[VMEM] * len(args),
        out_specs=jax.tree.map(lambda _: VMEM, outs) if out_specs is None else out_specs,
        out_shape=outs,
        scratch_shapes=list(scratch),
        input_output_aliases=aliases or {},
        compiler_params=pltpu.CompilerParams(vmem_limit_bytes=24 * 2**20),
        cost_estimate=pl.CostEstimate(
            flops=flops, bytes_accessed=bytes_accessed // 4, transcendentals=0
        ),
    )(*args)


def place(rest):
    child = lax.shift_right_logical(lax.axis_index("wide"), rest)
    return child, lax.axis_index("narrow")


def block(index, size):
    return pl.ds(pl.multiple_of(index * size, size), size)


def base_products(dual_ref, row_ref, pairs_ref, last_ref):
    rank = row_ref.shape[2]
    pairs_ref[:rank] = dot_t(dual_ref[1], row_ref[2])
    pairs_ref[rank:] = dot_t(dual_ref[0], row_ref[2])
    last_ref[...] = dot_t(dual_ref[0], row_ref[1])


def leaf_rows(start, leaf_ref, right_ref, field_ref):
    rows = field_ref.shape[0]
    step = min(256, rows)
    right = halves(right_ref[...])
    for i in range(0, rows, step):
        field_ref[i:i + step] = dot3(halves(leaf_ref[start + i:start + i + step]), right)


def projections(rest, dual_ref, first_ref, last_ref, keep_ref, send_ref, high_ref, low_ref):
    levels, rows, rank = dual_ref.shape
    for l in range(levels):
        high, low = halves(dual_ref[l].T)
        high_ref[l * rank:(l + 1) * rank] = high
        low_ref[l * rank:(l + 1) * rank] = low
    _, core = place(rest)
    half = keep_ref.shape[1]
    cut = first_ref.shape[0]
    for out, index in ((keep_ref, core), (send_ref, 1 - core)):
        cols = block(index, half)
        top, bottom = halves(first_ref[:, cols]), halves(last_ref[:, cols])
        out[...] = dot3((high_ref[:, :cut], low_ref[:, :cut]), top) + dot3(
            (high_ref[:, cut:], low_ref[:, cut:]), bottom
        )


def corrections(rest, pairs_ref, pairs_x_ref, last_ref, last_x_ref, last_z_ref, cores_ref, out_ref):
    rank = last_ref.shape[0]
    child, _ = place(rest)
    pair = lax.shift_right_logical(child, 1)
    slot3, slot2 = child & 1, pair & 1
    own = cores_ref[block(6 + child, rank), block(slot3, rank)]
    other = cores_ref[block(6 + (child ^ 1), rank), block(slot3, rank)]
    out_ref[:2 * rank] = dot(pairs_ref[...], own) + dot(pairs_x_ref[...], other)
    own = cores_ref[block(2 + pair, rank), block(slot2, rank)]
    other = cores_ref[block(2 + (pair ^ 1), rank), block(slot2, rank)]
    out_ref[2 * rank:] = dot(last_ref[...] + last_x_ref[...], own) + dot(last_z_ref[...], other)


def corrected(keep_ref, recv_ref, fix_ref, fix_other_ref, w_ref, v_ref):
    rank = w_ref.shape[0]
    q = keep_ref[...] + recv_ref[...]
    fix = fix_ref[...] + fix_other_ref[...]
    q1, q2, q3 = q[:rank], q[rank:2 * rank], q[2 * rank:]
    both = dot(fix[:2 * rank], q3)
    v = q2 - both[:rank]
    w_ref[...] = q1 - both[rank:] - dot(fix[2 * rank:], v)
    v_ref[:rank] = v
    v_ref[rank:] = q3


def lower_coefficients(rest, v_ref, vq_ref, vz_ref, vqx_ref, cores_ref, out_ref):
    rank = vz_ref.shape[0]
    child, _ = place(rest)
    pair = lax.shift_right_logical(child, 1)
    slot3, slot2 = child & 1, pair & 1
    rows2, rows3 = block(2 + pair, rank), block(6 + child, rank)
    out_ref[:rank] = dot(cores_ref[rows2, block(slot2, rank)], v_ref[...]) + dot(
        cores_ref[rows2, block(1 - slot2, rank)], vz_ref[...]
    )
    out_ref[rank:] = dot(cores_ref[rows3, block(slot3, rank)], vq_ref[rank:]) + dot(
        cores_ref[rows3, block(1 - slot3, rank)], vqx_ref[rank:]
    )


def lower_update(rest, first_ref, last_ref, row_ref, k_ref, k_other_ref, out_ref):
    rank = row_ref.shape[2]
    cut = first_ref.shape[0]
    half = k_ref.shape[1]
    _, core = place(rest)
    lefts = jnp.concatenate([row_ref[1], row_ref[2]], 1)
    for ref, index in ((k_ref, core), (k_other_ref, 1 - core)):
        cols = block(index, half)
        term = dot(lefts, ref[...])
        out_ref[:cut, cols] = first_ref[:, cols] - term[:cut]
        out_ref[cut:, cols] = last_ref[:, cols] - term[cut:]


def top_coefficient(rest, w, w_far, cores_ref):
    rank = w.shape[0]
    child, _ = place(rest)
    slot1 = lax.shift_right_logical(child, 2)
    rows1 = block(slot1, rank)
    return dot(cores_ref[rows1, block(slot1, rank)], w) + dot(
        cores_ref[rows1, block(1 - slot1, rank)], w_far
    )


def top_own(rest, field_ref, row_ref, w_ref, w_far_ref, cores_ref, out_ref):
    _, core = place(rest)
    cols = block(core, w_ref.shape[1])
    k = top_coefficient(rest, w_ref[...], w_far_ref[...], cores_ref)
    out_ref[...] = field_ref[:, cols] - dot(row_ref[0], k)


def top_other(rest, chunks, field_ref, own_ref, row_ref, w_ref, w_far_ref, cores_ref, out_ref, other_ref, sems):
    _, core = place(rest)
    rows, half = own_ref.shape
    mine, theirs = block(core, half), block(1 - core, half)
    copies = [pltpu.make_async_copy(own_ref, out_ref.at[:, mine], sems.at[chunks])]
    copies[0].start()
    k = top_coefficient(rest, w_ref[...], w_far_ref[...], cores_ref)
    step = rows // chunks
    for i in range(chunks):
        part = slice(i * step, (i + 1) * step)
        other_ref[part] = field_ref[part, theirs] - dot(row_ref[0, part], k)
        copy = pltpu.make_async_copy(other_ref.at[part], out_ref.at[part, theirs], sems.at[i])
        copy.start()
        copies.append(copy)
    for copy in copies:
        copy.wait()


def swap_wide(x, bit):
    count = lax.axis_size("wide")
    return lax.ppermute(x, "wide", [(w, w ^ (1 << bit)) for w in range(count)])


def swap_narrow(x):
    return lax.ppermute(x, "narrow", [(0, 1), (1, 0)])


def swap_crossed(x, first, second):
    wides, cores = lax.axis_size("wide"), lax.axis_size("narrow")
    route = []
    for w in range(wides):
        for n in range(cores):
            bit = first if n == 0 else second
            route.append((w * cores + n, (w ^ (1 << bit)) * cores + n))
    return lax.ppermute(x, ("wide", "narrow"), route)


def shards(right_side, leaf_inverse, row_bases, dual_bases, woodbury_cores):
    levels, rows, rank = row_bases.shape
    cols = right_side.shape[1]
    half = cols // 2
    rest = lax.axis_size("wide").bit_length() - 1 - levels
    bit3, bit2, bit1 = rest, rest + 1, rest + 2
    cut = rows * 3 // 4

    pairs, last = call(
        base_products, (shape(2 * rank, rank), shape(rank, rank)), (dual_bases, row_bases),
        6 * rows * rank * rank,
    )
    for bit in range(rest):
        pairs, last = pairs + swap_wide(pairs, bit), last + swap_wide(last, bit)
    last_x, pairs_x = swap_wide(last, bit3), swap_wide(pairs, bit3)

    first_rows = call(
        functools.partial(leaf_rows, 0), shape(cut, cols), (leaf_inverse, right_side),
        6 * cut * rows * cols,
    )
    last_z = swap_wide(last + last_x, bit2)
    last_rows = call(
        functools.partial(leaf_rows, cut), shape(rows - cut, cols), (leaf_inverse, right_side),
        6 * (rows - cut) * rows * cols,
    )
    keep, send = call(
        functools.partial(projections, rest), (shape(levels * rank, half),) * 2,
        (dual_bases, first_rows, last_rows), 6 * levels * rank * rows * cols,
        scratch=[pltpu.VMEM((levels * rank, rows), BF16)] * 2,
    )
    recv = swap_narrow(send)
    fix = call(
        functools.partial(corrections, rest), shape(levels * rank, rank),
        (pairs, pairs_x, last, last_x, last_z, woodbury_cores), 36 * rank**3,
    )
    fix_other = swap_narrow(fix)
    if rest:
        keep = keep + recv
        for bit in range(rest):
            keep = keep + swap_wide(keep, bit)
        recv = jnp.zeros_like(keep)
    w, vq = call(
        corrected, (shape(rank, half), shape(2 * rank, half)), (keep, recv, fix, fix_other),
        18 * rank * rank * half,
    )

    w = w + swap_crossed(w, bit2, bit3)
    vq_x = swap_wide(vq, bit3)
    w = w + swap_crossed(w, bit3, bit2)
    w_far = swap_wide(w, bit1)
    v = vq[:rank] + vq_x[:rank]
    v_z = swap_wide(v, bit2)
    k = call(
        functools.partial(lower_coefficients, rest), shape(2 * rank, half),
        (v, vq, v_z, vq_x, woodbury_cores), 24 * rank * rank * half,
    )
    k_other = swap_narrow(k)
    w_other = swap_narrow(w)
    field = call(
        functools.partial(lower_update, rest), shape(rows, cols),
        (first_rows, last_rows, row_bases, k, k_other), 12 * rows * rank * cols,
    )
    w_far_other = swap_narrow(w_far)
    own = call(
        functools.partial(top_own, rest), shape(rows, half),
        (field, row_bases, w, w_far, woodbury_cores), 6 * rows * rank * half,
    )
    chunks = 2
    return call(
        functools.partial(top_other, rest, chunks), shape(rows, cols),
        (field, own, row_bases, w_other, w_far_other, woodbury_cores), 6 * rows * rank * half,
        scratch=[pltpu.VMEM((rows, half), F32), pltpu.SemaphoreType.DMA((chunks + 1,))],
        out_specs=pl.BlockSpec(memory_space=pltpu.HBM),
    )


def solution(mesh):
    return jax.shard_map(
        shards,
        mesh=mesh,
        in_specs=(
            P(("parts", "wide", "narrow"), None),
            P(("parts", "wide", "narrow"), None),
            P(None, ("parts", "wide", "narrow"), None),
            P(None, ("parts", "wide", "narrow"), None),
            P("parts", None),
        ),
        out_specs=P(("parts", "wide", "narrow"), None),
        check_vma=False,
    )
```

time: 96.6 us -> 52.1 us (0.54)
  matrix products: 33.1 us -> 0 us
  waiting for transfers between devices: 46.1 us -> 21.3 us
  Pallas kernels: 0 us -> 10.9 us
  starting transfers between devices: 13.6 us -> 15.6 us
    dot_general x10 -> x0, matrix products: 33.1 us -> none  [the longest x3 12 us: shards(): jnp.dot(left_basis, coefficient, precision=highest, preferred_element_typ...]
    ppermute x9 -> x13, waiting for transfers between devices: 46.1 us -> 21.3 us  [the longest x6 19.5 us: swap_wide(): return lax.ppermute(x, 'wide', [(w, w ^ 1 << bit) for w in range(count)])]
    pallas_call x0 -> x10, Pallas kernels: none -> 10.9 us  [call(): pl.pallas_call(body, in_specs=[VMEM] * len(args), out_specs=jax.tree.map(...]
    ppermute x9 -> x13, starting transfers between devices: 13.6 us -> 15.6 us  [the longest x6 11.6 us: swap_wide(): return lax.ppermute(x, 'wide', [(w, w ^ 1 << bit) for w in range(count)])]
    unnamed x8 -> x10, local copies, waits for them, and re-layouts: 2.92 us -> 3.8 us
  transfers between devices with their start and end apart: 9 -> 13, of which waited for: 9 -> 7; matrix products, arithmetic and copies ran while one was open for 0% -> 0% of each run, Pallas kernels for 0% -> 7%
where the time goes in v2:
time: 52.1 us; the launch traced here: 51.9 us
  waiting for transfers between devices  21.3 us (41%)
  starting transfers between devices  15.6 us (30%)
  Pallas kernels  10.9 us (21%)
  local copies, waits for them, and re-layouts  3.8 us (7%)
    ppermute x6, waiting for transfers between devices, swap_wide(): return lax.ppermute(x, 'wide', [(w, w ^ 1 << bit) for w in range(count)])  19.5 us
    ppermute x6, starting transfers between devices, swap_wide(): return lax.ppermute(x, 'wide', [(w, w ^ 1 << bit) for w in range(count)])  11.6 us
    pallas_call x10, Pallas kernels, call(): pl.pallas_call(body, in_specs=[VMEM] * len(args), out_specs=jax.tree.map(...  10.9 us
    unnamed x10, local copies, waits for them, and re-layouts  3.8 us
    ppermute x2, starting transfers between devices, swap_crossed(): return lax.ppermute(x, ('wide', 'narrow'), route)  3.31 us
    ppermute x5, waiting for transfers between devices, swap_narrow(): return lax.ppermute(x, 'narrow', [(0, 1), (1, 0)])  1.44 us
  transfers between devices with their start and end apart: 13, of which 7 were waited for; matrix products, arithmetic and copies ran while one was open for 0% of the time, Pallas kernels for 7%

profile of v2, /device:TPU:0, one launch (start us, length us, event | category | flops | bytes accessed | tf_op | source)
XLA Modules:
  0.0 51.9 jit_solution(4979609732728791616)
XLA Ops:
  0.0 0.0 copy-start.2
  0.0 2.2 %copy-done.2 = f32[1024,1024]{1,0:T(8,128)S(1)} copy-done((f32[1024,1024]{1,0:T(8,128)S(1)}, f32[1024,1024]{1,0:T(8,128)}, u32[]{:S(2)}) %copy-start.2) | copy-done | bytes 4194328
  2.2 0.0 copy-start.3
  2.2 1.6 %copy-done.3 = f32[1024,512]{1,0:T(8,128)S(1)} copy-done((f32[1024,512]{1,0:T(8,128)S(1)}, f32[1024,512]{1,0:T(8,128)}, u32[]{:S(2)}) %copy-start.3) | copy-done | bytes 2097176
  3.8 1.0 %shard_map.56.last_ref = f32[256,512]{1,0:T(8,128)S(1)} custom-call(f32[1024,1024]{1,0:T(8,128)S(1)} %copy-done.2, f32[1024,512]{1,0:T(8,128)S(1)} %copy-done.3), custom_call_target="tpu_custom_call" | custom-call | flops 805306368 | bytes 1572864 | tf_op jit(solution)/shard_map/pallas_call | solution.py:42
  4.8 0.0 copy-start.4
  4.8 2.6 %shard_map.55.first_ref = f32[768,512]{1,0:T(8,128)S(1)} custom-call(f32[1024,1024]{1,0:T(8,128)S(1)} %copy-done.2, f32[1024,512]{1,0:T(8,128)S(1)} %copy-done.3), custom_call_target="tpu_custom_call" | custom-call | flops 2415919104 | bytes 1572864 | tf_op jit(solution)/shard_map/pallas_call | solution.py:42
  7.4 0.0 copy-done.4
  7.5 0.0 copy-start.1
  7.5 1.4 %shard_map.57 = (f32[384,256]{1,0:T(8,128)S(1)}, f32[384,256]{1,0:T(8,128)S(1)}) custom-call(f32[3,1024,128]{2,1,0:T(8,128)S(1)} %copy-done.4, f32[768,512]{1,0:T(8,128)S(1)} %shard_map.55.first_ref, f32[256,512]{1,0:T(8,128)S(1)} %shard_map.56.last_ref), custom_call_target="tpu_custom_call" | custom-call | flops 1207959552 | bytes 917504 | tf_op jit(solution)/shard_map/pallas_call | solution.py:42
  8.9 0.0 copy-start
  8.9 0.5 %collective-permute-start = (f32[384,256]{1,0:T(8,128)S(1)}, f32[384,256]{1,0:T(8,128)S(1)}, u32[]{:S(2)}, u32[]{:S(2)}) collective-permute-start(f32[384,256]{1,0:T(8,128)S(1)} %get-tuple-element.12), channel_id=1, source_target_pairs={{0,1},{1,0},{2,3},{3,2},{4,5},{5,4},{6,7},{7,6},{8,9},{9,8},{10,11... | collective-permute-start | bytes 1179656 | tf_op jit(solution)/shard_map/ppermute | solution.py:190
  9.4 0.0 copy-done.1
  9.4 0.8 %shard_map.58 = (f32[256,128]{1,0:T(8,128)S(1)}, f32[128,128]{1,0:T(8,128)S(1)}) custom-call(f32[3,1024,128]{2,1,0:T(8,128)S(1)} %copy-done.4, f32[3,1024,128]{2,1,0:T(8,128)S(1)} %copy-done.1), custom_call_target="tpu_custom_call" | custom-call | flops 100663296 | bytes 786432 | tf_op jit(solution)/shard_map/pallas_call | solution.py:42
  10.3 2.6 %collective-permute-start.2 = (f32[128,128]{1,0:T(8,128)S(1)}, f32[128,128]{1,0:T(8,128)S(1)}, u32[]{:S(2)}, u32[]{:S(2)}) collective-permute-start(f32[128,128]{1,0:T(8,128)S(1)} %get-tuple-element.14.last_ref), channel_id=1, source_target_pairs={{0,2},{2,0},{4,6},{6,4},{8,10},{10,8},{12,14},{14,12},{1,3},{3,1},... | collective-permute-start | bytes 196616 | tf_op jit(solution)/shard_map/ppermute | solution.py:186
  12.8 0.1 collective-permute-start.1
  12.9 2.7 %collective-permute-done.2.last_x_ref = f32[128,128]{1,0:T(8,128)S(1)} collective-permute-done((f32[128,128]{1,0:T(8,128)S(1)}, f32[128,128]{1,0:T(8,128)S(1)}, u32[]{:S(2)}, u32[]{:S(2)}) %collective-permute-start.2) | collective-permute-done | bytes 65568 | tf_op jit(solution)/shard_map/ppermute | solution.py:186
  15.6 2.1 %collective-permute-start.3 = (f32[128,128]{1,0:T(8,128)S(1)}, f32[128,128]{1,0:T(8,128)S(1)}, u32[]{:S(2)}, u32[]{:S(2)}) collective-permute-start(f32[128,128]{1,0:T(8,128)S(1)} %add.12), channel_id=1, source_target_pairs={{0,4},{2,6},{4,0},{6,2},{8,12},{10,14},{12,8},{14,10},{1,5},{3,7},... | collective-permute-start | bytes 196616 | tf_op jit(solution)/shard_map/ppermute | solution.py:186
  17.7 2.2 %collective-permute-done.3.last_z_ref = f32[128,128]{1,0:T(8,128)S(1)} collective-permute-done((f32[128,128]{1,0:T(8,128)S(1)}, f32[128,128]{1,0:T(8,128)S(1)}, u32[]{:S(2)}, u32[]{:S(2)}) %collective-permute-start.3) | collective-permute-done | bytes 65568 | tf_op jit(solution)/shard_map/ppermute | solution.py:186
  20.0 0.0 collective-permute-done.1.pairs_x_ref
  20.0 0.0 copy-done
  20.0 0.3 shard_map.59.fix_ref
  20.3 0.1 collective-permute-start.4
  20.4 1.4 %collective-permute-done.4.fix_other_ref = f32[384,128]{1,0:T(8,128)S(1)} collective-permute-done((f32[384,128]{1,0:T(8,128)S(1)}, f32[384,128]{1,0:T(8,128)S(1)}, u32[]{:S(2)}, u32[]{:S(2)}) %collective-permute-start.4) | collective-permute-done | bytes 196640 | tf_op jit(solution)/shard_map/ppermute | solution.py:190
  21.8 0.0 collective-permute-done.recv_ref
  21.8 0.5 shard_map.60
  22.3 2.2 %collective-permute-start.5 = (f32[256,256]{1,0:T(8,128)S(1)}, f32[256,256]{1,0:T(8,128)S(1)}, u32[]{:S(2)}, u32[]{:S(2)}) collective-permute-start(f32[256,256]{1,0:T(8,128)S(1)} %get-tuple-element.15.vq_ref), channel_id=1, source_target_pairs={{0,2},{2,0},{4,6},{6,4},{8,10},{10,8},{12,14},{14,12},{1,3},{3,1},... | collective-permute-start | bytes 786440 | tf_op jit(solution)/shard_map/ppermute | solution.py:186
  24.5 1.6 %collective-permute-start.8 = (f32[128,256]{1,0:T(8,128)S(1)}, f32[128,256]{1,0:T(8,128)S(1)}, u32[]{:S(2)}, u32[]{:S(2)}) collective-permute-start(f32[128,256]{1,0:T(8,128)S(1)} %get-tuple-element.16), channel_id=1, source_target_pairs={{0,4},{1,3},{2,6},{3,1},{4,0},{5,7},{6,2},{7,5},{8,12},{9,11},{10,... | collective-permute-start | bytes 393224 | tf_op jit(solution)/shard_map/ppermute | solution.py:200
  26.0 5.5 %collective-permute-done.5.vqx_ref = f32[256,256]{1,0:T(8,128)S(1)} collective-permute-done((f32[256,256]{1,0:T(8,128)S(1)}, f32[256,256]{1,0:T(8,128)S(1)}, u32[]{:S(2)}, u32[]{:S(2)}) %collective-permute-start.5) | collective-permute-done | bytes 262176 | tf_op jit(solution)/shard_map/ppermute | solution.py:186
  31.6 2.0 %collective-permute-start.6 = (f32[128,256]{1,0:T(8,128)S(1)}, f32[128,256]{1,0:T(8,128)S(1)}, u32[]{:S(2)}, u32[]{:S(2)}) collective-permute-start(f32[128,256]{1,0:T(8,128)S(1)} %slice_add_fusion.v_ref), channel_id=1, source_target_pairs={{0,4},{2,6},{4,0},{6,2},{8,12},{10,14},{12,8},{14,10},{1,5},{3,7},... | collective-permute-start | bytes 393224 | tf_op jit(solution)/shard_map/ppermute | solution.py:186
  33.6 0.0 collective-permute-done.8
  33.6 1.7 %collective-permute-start.9 = (f32[128,256]{1,0:T(8,128)S(1)}, f32[128,256]{1,0:T(8,128)S(1)}, u32[]{:S(2)}, u32[]{:S(2)}) collective-permute-start(f32[128,256]{1,0:T(8,128)S(1)} %add.14), channel_id=1, source_target_pairs={{0,2},{1,5},{2,0},{3,7},{4,6},{5,1},{6,4},{7,3},{8,10},{9,13},{10,... | collective-permute-start | bytes 393224 | tf_op jit(solution)/shard_map/ppermute | solution.py:200
  35.4 2.4 %collective-permute-done.6.vz_ref = f32[128,256]{1,0:T(8,128)S(1)} collective-permute-done((f32[128,256]{1,0:T(8,128)S(1)}, f32[128,256]{1,0:T(8,128)S(1)}, u32[]{:S(2)}, u32[]{:S(2)}) %collective-permute-start.6) | collective-permute-done | bytes 131104 | tf_op jit(solution)/shard_map/ppermute | solution.py:186
  37.8 0.4 shard_map.61.k_ref
  38.2 0.1 collective-permute-start.7
  38.2 0.4 collective-permute-done.9
  38.7 2.7 %collective-permute-start.10 = (f32[128,256]{1,0:T(8,128)S(1)}, f32[128,256]{1,0:T(8,128)S(1)}, u32[]{:S(2)}, u32[]{:S(2)}) collective-permute-start(f32[128,256]{1,0:T(8,128)S(1)} %add.15.w_ref), channel_id=1, source_target_pairs={{0,8},{2,10},{4,12},{6,14},{8,0},{10,2},{12,4},{14,6},{1,9},{3,11}... | collective-permute-start | bytes 393224 | tf_op jit(solution)/shard_map/ppermute | solution.py:186
  41.3 0.0 collective-permute-start.11
  41.3 6.6 %collective-permute-done.10.w_far_ref = f32[128,256]{1,0:T(8,128)S(1)} collective-permute-done((f32[128,256]{1,0:T(8,128)S(1)}, f32[128,256]{1,0:T(8,128)S(1)}, u32[]{:S(2)}, u32[]{:S(2)}) %collective-permute-start.10) | collective-permute-done | bytes 131104 | tf_op jit(solution)/shard_map/ppermute | solution.py:186
  48.0 0.0 collective-permute-start.12
  48.0 0.0 collective-permute-done.7.k_other_ref
  48.0 1.0 %shard_map.62.field_ref = f32[1024,512]{1,0:T(8,128)S(1)} custom-call(f32[768,512]{1,0:T(8,128)S(1)} %shard_map.55.first_ref, f32[256,512]{1,0:T(8,128)S(1)} %shard_map.56.last_ref, f32[3,1024,128]{2,1,0:T(8,128)S(1)} %copy-done.1, f32[256,256]{1,0:T(8,128)S(1)} %shard_map.61.k_ref, f32[256,256]{1,0:T(8,128)S(1)} %collective-permute-done.7.k_other_ref), custom_call_target="tpu_custom_call" | custom-call | flops 805306368 | bytes 1048576 | tf_op jit(solution)/shard_map/pallas_call | solution.py:42
  49.0 1.0 %shard_map.63.own_ref = f32[1024,256]{1,0:T(8,128)S(1)} custom-call(f32[1024,512]{1,0:T(8,128)S(1)} %shard_map.62.field_ref, f32[3,1024,128]{2,1,0:T(8,128)S(1)} %copy-done.1, f32[128,256]{1,0:T(8,128)S(1)} %add.15.w_ref, f32[128,256]{1,0:T(8,128)S(1)} %collective-permute-done.10.w_far_ref, f32[1792,256]{1,0:T(8,128)S(1)} %copy-done), custom_call_target="tpu_custom_call" | custom-call | flops 201326592 | bytes 1441792 | tf_op jit(solution)/shard_map/pallas_call | solution.py:42
  50.0 0.0 collective-permute-done.11.w_ref
  50.0 0.0 collective-permute-done.12.w_far_ref
  50.0 1.9 %shard_map.64 = f32[1024,512]{1,0:T(8,128)} custom-call(f32[1024,512]{1,0:T(8,128)S(1)} %shard_map.62.field_ref, f32[1024,256]{1,0:T(8,128)S(1)} %shard_map.63.own_ref, f32[3,1024,128]{2,1,0:T(8,128)S(1)} %copy-done.1, f32[128,256]{1,0:T(8,128)S(1)} %collective-permute-done.11.w_ref, f32[128,256]{1,0:T(8,128)S(1)} %collective-permute-done.12.w_far_ref, ...), custom_call_target="tpu_custom_call" | custom-call | flops 201326592 | bytes 1703936 | tf_op jit(solution)/shard_map/pallas_call | solution.py:42
  (4 shorter events, 0.1 us)
Async XLA Ops:
  0.0 2.2 %copy-start.2 = (f32[1024,1024]{1,0:T(8,128)S(1)}, f32[1024,1024]{1,0:T(8,128)}, u32[]{:S(2)}) copy-start(f32[1024,1024]{1,0:T(8,128)} %leaf_ref.3) | copy-start | bytes 12582916
  2.2 1.6 %copy-start.3 = (f32[1024,512]{1,0:T(8,128)S(1)}, f32[1024,512]{1,0:T(8,128)}, u32[]{:S(2)}) copy-start(f32[1024,512]{1,0:T(8,128)} %right_ref.3) | copy-start | bytes 6291460
  4.8 2.7 %copy-start.4 = (f32[3,1024,128]{2,1,0:T(8,128)S(1)}, f32[3,1024,128]{2,1,0:T(8,128)}, u32[]{:S(2)}) copy-start(f32[3,1024,128]{2,1,0:T(8,128)} %dual_ref.3) | copy-start | bytes 4718596
  7.5 2.0 %copy-start.1 = (f32[3,1024,128]{2,1,0:T(8,128)S(1)}, f32[3,1024,128]{2,1,0:T(8,128)}, u32[]{:S(2)}) copy-start(f32[3,1024,128]{2,1,0:T(8,128)} %row_ref.7) | copy-start | bytes 4718596
  8.9 11.1 %copy-start = (f32[1792,256]{1,0:T(8,128)S(1)}, f32[1792,256]{1,0:T(8,128)}, u32[]{:S(2)}) copy-start(f32[1792,256]{1,0:T(8,128)} %cores_ref.7) | copy-start | bytes 5505028
  8.9 12.9 %collective-permute-start = (f32[384,256]{1,0:T(8,128)S(1)}, f32[384,256]{1,0:T(8,128)S(1)}, u32[]{:S(2)}, u32[]{:S(2)}) collective-permute-start(f32[384,256]{1,0:T(8,128)S(1)} %get-tuple-element.12), channel_id=1, source_target_pairs={{0,1},{1,0},{2,3},{3,2},{4,5},{5,4},{6,7},{7,6},{8,9},{9,8},{10,11... | collective-permute-start | bytes 1179656 | tf_op jit(solution)/shard_map/ppermute | solution.py:190
  10.3 5.3 %collective-permute-start.2 = (f32[128,128]{1,0:T(8,128)S(1)}, f32[128,128]{1,0:T(8,128)S(1)}, u32[]{:S(2)}, u32[]{:S(2)}) collective-permute-start(f32[128,128]{1,0:T(8,128)S(1)} %get-tuple-element.14.last_ref), channel_id=1, source_target_pairs={{0,2},{2,0},{4,6},{6,4},{8,10},{10,8},{12,14},{14,12},{1,3},{3,1},... | collective-permute-start | bytes 196616 | tf_op jit(solution)/shard_map/ppermute | solution.py:186
  12.8 7.1 %collective-permute-start.1 = (f32[256,128]{1,0:T(8,128)S(1)}, f32[256,128]{1,0:T(8,128)S(1)}, u32[]{:S(2)}, u32[]{:S(2)}) collective-permute-start(f32[256,128]{1,0:T(8,128)S(1)} %get-tuple-element.13.pairs_ref), channel_id=1, source_target_pairs={{0,2},{2,0},{4,6},{6,4},{8,10},{10,8},{12,14},{14,12},{1,3},{3,1},... | collective-permute-start | bytes 393224 | tf_op jit(solution)/shard_map/ppermute | solution.py:186
  15.6 4.4 %collective-permute-start.3 = (f32[128,128]{1,0:T(8,128)S(1)}, f32[128,128]{1,0:T(8,128)S(1)}, u32[]{:S(2)}, u32[]{:S(2)}) collective-permute-start(f32[128,128]{1,0:T(8,128)S(1)} %add.12), channel_id=1, source_target_pairs={{0,4},{2,6},{4,0},{6,2},{8,12},{10,14},{12,8},{14,10},{1,5},{3,7},... | collective-permute-start | bytes 196616 | tf_op jit(solution)/shard_map/ppermute | solution.py:186
  20.3 1.5 %collective-permute-start.4 = (f32[384,128]{1,0:T(8,128)S(1)}, f32[384,128]{1,0:T(8,128)S(1)}, u32[]{:S(2)}, u32[]{:S(2)}) collective-permute-start(f32[384,128]{1,0:T(8,128)S(1)} %shard_map.59.fix_ref), channel_id=1, source_target_pairs={{0,1},{1,0},{2,3},{3,2},{4,5},{5,4},{6,7},{7,6},{8,9},{9,8},{10,11... | collective-permute-start | bytes 589832 | tf_op jit(solution)/shard_map/ppermute | solution.py:190
  22.3 9.3 %collective-permute-start.5 = (f32[256,256]{1,0:T(8,128)S(1)}, f32[256,256]{1,0:T(8,128)S(1)}, u32[]{:S(2)}, u32[]{:S(2)}) collective-permute-start(f32[256,256]{1,0:T(8,128)S(1)} %get-tuple-element.15.vq_ref), channel_id=1, source_target_pairs={{0,2},{2,0},{4,6},{6,4},{8,10},{10,8},{12,14},{14,12},{1,3},{3,1},... | collective-permute-start | bytes 786440 | tf_op jit(solution)/shard_map/ppermute | solution.py:186
  24.5 9.1 %collective-permute-start.8 = (f32[128,256]{1,0:T(8,128)S(1)}, f32[128,256]{1,0:T(8,128)S(1)}, u32[]{:S(2)}, u32[]{:S(2)}) collective-permute-start(f32[128,256]{1,0:T(8,128)S(1)} %get-tuple-element.16), channel_id=1, source_target_pairs={{0,4},{1,3},{2,6},{3,1},{4,0},{5,7},{6,2},{7,5},{8,12},{9,11},{10,... | collective-permute-start | bytes 393224 | tf_op jit(solution)/shard_map/ppermute | solution.py:200
  31.6 6.2 %collective-permute-start.6 = (f32[128,256]{1,0:T(8,128)S(1)}, f32[128,256]{1,0:T(8,128)S(1)}, u32[]{:S(2)}, u32[]{:S(2)}) collective-permute-start(f32[128,256]{1,0:T(8,128)S(1)} %slice_add_fusion.v_ref), channel_id=1, source_target_pairs={{0,4},{2,6},{4,0},{6,2},{8,12},{10,14},{12,8},{14,10},{1,5},{3,7},... | collective-permute-start | bytes 393224 | tf_op jit(solution)/shard_map/ppermute | solution.py:186
  33.6 5.0 %collective-permute-start.9 = (f32[128,256]{1,0:T(8,128)S(1)}, f32[128,256]{1,0:T(8,128)S(1)}, u32[]{:S(2)}, u32[]{:S(2)}) collective-permute-start(f32[128,256]{1,0:T(8,128)S(1)} %add.14), channel_id=1, source_target_pairs={{0,2},{1,5},{2,0},{3,7},{4,6},{5,1},{6,4},{7,3},{8,10},{9,13},{10,... | collective-permute-start | bytes 393224 | tf_op jit(solution)/shard_map/ppermute | solution.py:200
  38.2 9.8 %collective-permute-start.7 = (f32[256,256]{1,0:T(8,128)S(1)}, f32[256,256]{1,0:T(8,128)S(1)}, u32[]{:S(2)}, u32[]{:S(2)}) collective-permute-start(f32[256,256]{1,0:T(8,128)S(1)} %shard_map.61.k_ref), channel_id=1, source_target_pairs={{0,1},{1,0},{2,3},{3,2},{4,5},{5,4},{6,7},{7,6},{8,9},{9,8},{10,11... | collective-permute-start | bytes 786440 | tf_op jit(solution)/shard_map/ppermute | solution.py:190
  38.7 9.3 %collective-permute-start.10 = (f32[128,256]{1,0:T(8,128)S(1)}, f32[128,256]{1,0:T(8,128)S(1)}, u32[]{:S(2)}, u32[]{:S(2)}) collective-permute-start(f32[128,256]{1,0:T(8,128)S(1)} %add.15.w_ref), channel_id=1, source_target_pairs={{0,8},{2,10},{4,12},{6,14},{8,0},{10,2},{12,4},{14,6},{1,9},{3,11}... | collective-permute-start | bytes 393224 | tf_op jit(solution)/shard_map/ppermute | solution.py:186
  41.3 8.6 %collective-permute-start.11 = (f32[128,256]{1,0:T(8,128)S(1)}, f32[128,256]{1,0:T(8,128)S(1)}, u32[]{:S(2)}, u32[]{:S(2)}) collective-permute-start(f32[128,256]{1,0:T(8,128)S(1)} %add.15.w_ref), channel_id=1, source_target_pairs={{0,1},{1,0},{2,3},{3,2},{4,5},{5,4},{6,7},{7,6},{8,9},{9,8},{10,11... | collective-permute-start | bytes 393224 | tf_op jit(solution)/shard_map/ppermute | solution.py:190
  48.0 2.0 %collective-permute-start.12 = (f32[128,256]{1,0:T(8,128)S(1)}, f32[128,256]{1,0:T(8,128)S(1)}, u32[]{:S(2)}, u32[]{:S(2)}) collective-permute-start(f32[128,256]{1,0:T(8,128)S(1)} %collective-permute-done.10.w_far_ref), channel_id=1, source_target_pairs={{0,1},{1,0},{2,3},{3,2},{4,5},{5,4},{6,7},{7,6},{8,9},{9,8},{10,11... | collective-permute-start | bytes 393224 | tf_op jit(solution)/shard_map/ppermute | solution.py:190

commit v3 on v2

v3 whole, which is shorter than its diff:
```python
import functools

import jax
import jax.numpy as jnp
from jax import lax
from jax.experimental import pallas as pl
from jax.experimental.pallas import tpu as pltpu
from jax.sharding import PartitionSpec as P

F32, BF16 = jnp.float32, jnp.bfloat16
VMEM = pl.BlockSpec(memory_space=pltpu.VMEM)


def dot(a, b):
    return jnp.dot(a, b, precision=lax.Precision.HIGH, preferred_element_type=F32)


def dot_t(a, b):
    return lax.dot_general(
        a, b, (((0,), (0,)), ((), ())), precision=lax.Precision.HIGH, preferred_element_type=F32
    )


def halves(x):
    high = x.astype(BF16)
    return high, (x - high.astype(F32)).astype(BF16)


def dot3(a, b):
    def one(x, y):
        return jnp.dot(x, y, preferred_element_type=F32)

    return one(a[0], b[0]) + one(a[0], b[1]) + one(a[1], b[0])


def shape(*dims, dtype=F32):
    return jax.ShapeDtypeStruct(dims, dtype)


def call(body, outs, args, flops, in_specs=None, scratch=(), aliases=None, out_specs=None):
    bytes_accessed = sum(a.size * a.dtype.itemsize for a in args)
    return pl.pallas_call(
        body,
        in_specs=in_specs or [VMEM] * len(args),
        out_specs=jax.tree.map(lambda _: VMEM, outs) if out_specs is None else out_specs,
        out_shape=outs,
        scratch_shapes=list(scratch),
        input_output_aliases=aliases or {},
        compiler_params=pltpu.CompilerParams(vmem_limit_bytes=24 * 2**20),
        cost_estimate=pl.CostEstimate(
            flops=flops, bytes_accessed=0, transcendentals=0
        ),
    )(*args)


def place(rest):
    child = lax.shift_right_logical(lax.axis_index("wide"), rest)
    return child, lax.axis_index("narrow")


def block(index, size):
    return pl.ds(pl.multiple_of(index * size, size), size)


def base_products(dual_hbm, row_hbm, pairs_ref, last_ref, dual_ref, row_ref, sems):
    rank = row_hbm.shape[2]
    sources = (dual_hbm.at[0], row_hbm.at[1], row_hbm.at[2], dual_hbm.at[1])
    targets = (dual_ref.at[0], row_ref.at[0], row_ref.at[1], dual_ref.at[1])
    copies = [
        pltpu.make_async_copy(source, target, sems.at[i])
        for i, (source, target) in enumerate(zip(sources, targets))
    ]
    for copy in copies:
        copy.start()
    copies[0].wait()
    copies[1].wait()
    last_ref[...] = dot_t(dual_ref[0], row_ref[0])
    copies[2].wait()
    pairs_ref[rank:] = dot_t(dual_ref[0], row_ref[1])
    copies[3].wait()
    pairs_ref[:rank] = dot_t(dual_ref[1], row_ref[1])


def leaf_rows(start, leaf_ref, right_ref, field_ref):
    rows = field_ref.shape[0]
    step = min(256, rows)
    right = halves(right_ref[...])
    for i in range(0, rows, step):
        field_ref[i:i + step] = dot3(halves(leaf_ref[start + i:start + i + step]), right)


def projections(rest, dual_ref, first_ref, last_ref, keep_ref, send_ref, high_ref, low_ref):
    levels, rows, rank = dual_ref.shape
    for l in range(levels):
        high, low = halves(dual_ref[l].T)
        high_ref[l * rank:(l + 1) * rank] = high
        low_ref[l * rank:(l + 1) * rank] = low
    _, core = place(rest)
    half = keep_ref.shape[1]
    cut = first_ref.shape[0]
    for out, index in ((keep_ref, core), (send_ref, 1 - core)):
        cols = block(index, half)
        top, bottom = halves(first_ref[:, cols]), halves(last_ref[:, cols])
        out[...] = dot3((high_ref[:, :cut], low_ref[:, :cut]), top) + dot3(
            (high_ref[:, cut:], low_ref[:, cut:]), bottom
        )


def corrections(rest, pairs_ref, pairs_x_ref, last_ref, last_x_ref, last_z_ref, cores_ref, out_ref):
    rank = last_ref.shape[0]
    child, _ = place(rest)
    pair = lax.shift_right_logical(child, 1)
    slot3, slot2 = child & 1, pair & 1
    own = cores_ref[block(6 + child, rank), block(slot3, rank)]
    other = cores_ref[block(6 + (child ^ 1), rank), block(slot3, rank)]
    out_ref[:2 * rank] = dot(pairs_ref[...], own) + dot(pairs_x_ref[...], other)
    own = cores_ref[block(2 + pair, rank), block(slot2, rank)]
    other = cores_ref[block(2 + (pair ^ 1), rank), block(slot2, rank)]
    out_ref[2 * rank:] = dot(last_ref[...] + last_x_ref[...], own) + dot(last_z_ref[...], other)


def corrected(keep_ref, recv_ref, fix_ref, fix_other_ref, *out_refs):
    *w_refs, v_ref, q_ref = out_refs
    rank = v_ref.shape[0]
    q = keep_ref[...] + recv_ref[...]
    fix = fix_ref[...] + fix_other_ref[...]
    q1, q2, q3 = q[:rank], q[rank:2 * rank], q[2 * rank:]
    both = dot(fix[:2 * rank], q3)
    v = q2 - both[:rank]
    w = q1 - both[rank:] - dot(fix[2 * rank:], v)
    width = w.shape[1] // len(w_refs)
    for i, w_ref in enumerate(w_refs):
        w_ref[...] = w[:, i * width:(i + 1) * width]
    v_ref[...] = v
    q_ref[...] = q3


def lower_coefficients(rest, v_ref, vz_ref, q_ref, qx_ref, cores_ref, out_ref):
    rank = vz_ref.shape[0]
    child, _ = place(rest)
    pair = lax.shift_right_logical(child, 1)
    slot3, slot2 = child & 1, pair & 1
    rows2, rows3 = block(2 + pair, rank), block(6 + child, rank)
    out_ref[:rank] = dot(cores_ref[rows2, block(slot2, rank)], v_ref[...]) + dot(
        cores_ref[rows2, block(1 - slot2, rank)], vz_ref[...]
    )
    out_ref[rank:] = dot(cores_ref[rows3, block(slot3, rank)], q_ref[...]) + dot(
        cores_ref[rows3, block(1 - slot3, rank)], qx_ref[...]
    )


def solved(rest, chunk, index, first_ref, last_ref, row_ref, k_ref, w_ref, far_ref, cores_ref):
    levels, _, rank = row_ref.shape
    width = w_ref.shape[1]
    child, _ = place(rest)
    slot1 = lax.shift_right_logical(child, 2)
    rows1 = block(slot1, rank)
    top = dot(cores_ref[rows1, block(slot1, rank)], w_ref[...]) + dot(
        cores_ref[rows1, block(1 - slot1, rank)], far_ref[...]
    )
    part = slice(chunk * width, (chunk + 1) * width)
    coefficients = jnp.concatenate([top, k_ref[:, part]], 0)
    cols = block(index * (k_ref.shape[1] // width) + chunk, width)
    cut = first_ref.shape[0]

    def rows(start, stop):
        lefts = jnp.concatenate([row_ref[l, start:stop] for l in range(levels)], 1)
        term = dot(lefts, coefficients)
        if start < cut:
            return first_ref[start:stop, cols] - term
        return last_ref[start - cut:stop - cut, cols] - term

    return rows, cols


def solve_chunk(rest, chunk, sides, *refs):
    outs, ins = refs[-sides:], refs[:-sides]
    first_ref, last_ref, row_ref, cores_ref, *others = ins
    _, core = place(rest)
    for side, out_ref in enumerate(outs):
        k_ref, w_ref, far_ref = others[3 * side:3 * side + 3]
        index = core if side == 0 else 1 - core
        rows, _ = solved(
            rest, chunk, index, first_ref, last_ref, row_ref, k_ref, w_ref, far_ref, cores_ref
        )
        cut, total = first_ref.shape[0], out_ref.shape[0]
        out_ref[:cut] = rows(0, cut)
        out_ref[cut:] = rows(cut, total)


def solve_last(rest, pieces, first_ref, last_ref, row_ref, cores_ref, k_ref, w_ref, far_ref, *refs):
    done_refs, (out_ref, other_ref, sems) = refs[:-3], refs[-3:]
    _, core = place(rest)
    total, width = other_ref.shape
    copies = []
    chunks = out_ref.shape[1] // (2 * width)
    for i, ref in enumerate(done_refs):
        chunk, side = i // 2, i % 2
        index = core if side == 0 else 1 - core
        cols = block(index * chunks + chunk, width)
        copies.append(pltpu.make_async_copy(ref, out_ref.at[:, cols], sems.at[i]))
        copies[-1].start()
    rows, cols = solved(
        rest, chunks - 1, 1 - core, first_ref, last_ref, row_ref, k_ref, w_ref, far_ref, cores_ref
    )
    step = total // pieces
    for i in range(pieces):
        part = slice(i * step, (i + 1) * step)
        other_ref[part] = rows(i * step, (i + 1) * step)
        copy = pltpu.make_async_copy(
            other_ref.at[part], out_ref.at[part, cols], sems.at[len(done_refs) + i]
        )
        copy.start()
        copies.append(copy)
    for copy in copies:
        copy.wait()


def tie(x, *others):
    def body(x_ref, *refs):
        refs[-1][...] = x_ref[...]

    return call(body, shape(*x.shape), (x, *others), 0)


def after(x, *others):
    return lax.optimization_barrier((x, *others))[0]


def swap_wide(x, bit):
    count = lax.axis_size("wide")
    return lax.ppermute(x, "wide", [(w, w ^ (1 << bit)) for w in range(count)])


def swap_narrow(x):
    return lax.ppermute(x, "narrow", [(0, 1), (1, 0)])


def swap_crossed(x, first, second):
    wides, cores = lax.axis_size("wide"), lax.axis_size("narrow")
    route = []
    for w in range(wides):
        for n in range(cores):
            bit = first if n == 0 else second
            route.append((w * cores + n, (w ^ (1 << bit)) * cores + n))
    return lax.ppermute(x, ("wide", "narrow"), route)


def shards(right_side, leaf_inverse, row_bases, dual_bases, woodbury_cores):
    levels, rows, rank = row_bases.shape
    cols = right_side.shape[1]
    half = cols // 2
    rest = lax.axis_size("wide").bit_length() - 1 - levels
    bit3, bit2, bit1 = rest, rest + 1, rest + 2
    cut = rows * 3 // 4

    pairs, last = call(
        base_products, (shape(2 * rank, rank), shape(rank, rank)), tuple(pltpu.with_memory_space_constraint(x, pltpu.HBM) for x in (dual_bases, row_bases)),
        30 * rows * rows * cols, in_specs=[pl.BlockSpec(memory_space=pltpu.HBM)] * 2,
        scratch=[pltpu.VMEM((2, rows, rank), F32)] * 2 + [pltpu.SemaphoreType.DMA((4,))],
    )
    for bit in range(rest):
        pairs, last = pairs + swap_wide(pairs, bit), last + swap_wide(last, bit)
    last_x, pairs_x = swap_wide(last, bit3), swap_wide(pairs, bit3)

    first_rows = call(
        functools.partial(leaf_rows, 0), shape(cut, cols), (leaf_inverse, after(right_side, last)),
        6 * cut * rows * cols,
    )
    last_z = swap_wide(last + last_x, bit2)
    last_rows = call(
        functools.partial(leaf_rows, cut), shape(rows - cut, cols), (leaf_inverse, after(right_side, last_x)),
        6 * (rows - cut) * rows * cols,
    )
    keep, send = call(
        functools.partial(projections, rest), (shape(levels * rank, half),) * 2,
        (dual_bases, first_rows, last_rows), 6 * levels * rank * rows * cols,
        scratch=[pltpu.VMEM((levels * rank, rows), BF16)] * 2,
    )
    recv = swap_narrow(after(send, last_z, pairs_x))
    fix = call(
        functools.partial(corrections, rest), shape(levels * rank, rank),
        (pairs, pairs_x, last, last_x, last_z, woodbury_cores), 36 * rank**3,
    )
    fix_other = swap_narrow(fix)
    if rest:
        keep = keep + recv
        for bit in range(rest):
            keep = keep + swap_wide(keep, bit)
        recv = jnp.zeros_like(keep)
    chunks = 1
    width = half // chunks
    *w, v, q = call(
        corrected, (shape(rank, width),) * chunks + (shape(rank, half),) * 2,
        (keep, recv, fix, fix_other), 18 * rank * rank * half,
    )

    v = tie(v, w[0])
    v_x = swap_wide(v, bit3)
    w = w_mid = [x + swap_crossed(x, bit2, bit3) for x in w]
    q = tie(q, w_mid[0])
    q_x = swap_wide(q, bit3)
    v = v + after(v_x, w_mid[-1])
    w = [x + after(swap_crossed(x, bit3, bit2), v, q) for x in w]
    v_z = swap_wide(v, bit2)
    far = [swap_wide(x, bit1) for x in w]
    w_other = [swap_narrow(after(x, v_z, q_x)) for x in w]
    far_other = [swap_narrow(x) for x in far]
    k = call(
        functools.partial(lower_coefficients, rest), shape(2 * rank, half),
        (after(v, w[0]), v_z, q, q_x, woodbury_cores), 0,
    )
    k_other = swap_narrow(k)
    common = (first_rows, last_rows, row_bases, woodbury_cores)
    done = []
    for i in range(chunks):
        sides = 2 if i < chunks - 1 else 1
        args = (k, w[i], far[i], k_other, w_other[i], far_other[i])[:3 * sides]
        done += call(
            functools.partial(solve_chunk, rest, i, sides), (shape(rows, width),) * sides,
            common + args, 0,
        )
    pieces = 4
    return call(
        functools.partial(solve_last, rest, pieces), shape(rows, cols),
        common + (k_other, w_other[-1], far_other[-1], *done), 0,
        scratch=[pltpu.VMEM((rows, width), F32), pltpu.SemaphoreType.DMA((len(done) + pieces,))],
        out_specs=pl.BlockSpec(memory_space=pltpu.HBM),
    )


def solution(mesh):
    return jax.shard_map(
        shards,
        mesh=mesh,
        in_specs=(
            P(("parts", "wide", "narrow"), None),
            P(("parts", "wide", "narrow"), None),
            P(None, ("parts", "wide", "narrow"), None),
            P(None, ("parts", "wide", "narrow"), None),
            P("parts", None),
        ),
        out_specs=P(("parts", "wide", "narrow"), None),
        check_vma=False,
    )
```

time: 52.1 us -> 38.7 us (0.74)
  waiting for transfers between devices: 21.3 us -> 8.3 us
  local copies, waits for them, and re-layouts: 3.8 us -> 0.02 us
  starting transfers between devices: 15.6 us -> 17.5 us
  Pallas kernels: 10.9 us -> 12.5 us
    ppermute x6 -> x7, waiting for transfers between devices: 19.5 us -> 5.58 us  [swap_wide(): return lax.ppermute(x, 'wide', [(w, w ^ 1 << bit) for w in range(count)])]
    unnamed x10, local copies, waits for them, and re-layouts: 3.8 us -> 0.02 us
    pallas_call x10 -> x11, Pallas kernels: 10.9 us -> 12.5 us  [call(): pl.pallas_call(body, in_specs=in_specs or [VMEM] * len(args), out_specs=j...]
    ppermute x2, waiting for transfers between devices: 0.41 us -> 1.6 us  [swap_crossed(): return lax.ppermute(x, ('wide', 'narrow'), route)]
    ppermute x6 -> x7, starting transfers between devices: 11.6 us -> 12.7 us  [swap_wide(): return lax.ppermute(x, 'wide', [(w, w ^ 1 << bit) for w in range(count)])]
  transfers between devices with their start and end apart: 13 -> 14, of which waited for: 7 -> 5; matrix products, arithmetic and copies ran while one was open for 0% -> 0% of each run, Pallas kernels for 7% -> 19%
where the time goes in v3:
time: 38.7 us; the launch traced here: 38.5 us
  starting transfers between devices  17.5 us (45%)
  Pallas kernels  12.5 us (32%)
  waiting for transfers between devices  8.3 us (21%)
    ppermute x7, starting transfers between devices, swap_wide(): return lax.ppermute(x, 'wide', [(w, w ^ 1 << bit) for w in range(count)])  12.7 us
    pallas_call x11, Pallas kernels, call(): pl.pallas_call(body, in_specs=in_specs or [VMEM] * len(args), out_specs=j...  12.5 us
    ppermute x7, waiting for transfers between devices, swap_wide(): return lax.ppermute(x, 'wide', [(w, w ^ 1 << bit) for w in range(count)])  5.58 us
    ppermute x2, starting transfers between devices, swap_crossed(): return lax.ppermute(x, ('wide', 'narrow'), route)  3.54 us
    ppermute x2, waiting for transfers between devices, swap_crossed(): return lax.ppermute(x, ('wide', 'narrow'), route)  1.6 us
    ppermute x5, starting transfers between devices, swap_narrow(): return lax.ppermute(x, 'narrow', [(0, 1), (1, 0)])  1.18 us
    ppermute x5, waiting for transfers between devices, swap_narrow(): return lax.ppermute(x, 'narrow', [(0, 1), (1, 0)])  1.12 us
  transfers between devices with their start and end apart: 14, of which 5 were waited for; matrix products, arithmetic and copies ran while one was open for 0% of the time, Pallas kernels for 19%

profile of v3, /device:TPU:0, one launch (start us, length us, event | category | flops | bytes accessed | tf_op | source)
XLA Modules:
  0.0 38.5 jit_solution(17398795611511820889)
XLA Ops:
  0.0 0.0 copy-start.3
  0.0 0.0 copy-start.2
  0.0 2.6 %shard_map.55 = (f32[256,128]{1,0:T(8,128)S(1)}, f32[128,128]{1,0:T(8,128)S(1)}) custom-call(f32[3,1024,128]{2,1,0:T(8,128)} %dual_ref.1, f32[3,1024,128]{2,1,0:T(8,128)} %row_ref.1), custom_call_target="tpu_custom_call" | custom-call | flops 16106127360 | tf_op jit(solution)/shard_map/pallas_call | solution.py:42
  2.6 3.0 %collective-permute-start = (f32[128,128]{1,0:T(8,128)S(1)}, f32[128,128]{1,0:T(8,128)S(1)}, u32[]{:S(2)}, u32[]{:S(2)}) collective-permute-start(f32[128,128]{1,0:T(8,128)S(1)} %get-tuple-element.19.last_ref), channel_id=1, source_target_pairs={{0,2},{2,0},{4,6},{6,4},{8,10},{10,8},{12,14},{14,12},{1,3},{3,1},... | collective-permute-start | bytes 196616 | tf_op jit(solution)/shard_map/ppermute | solution.py:232
  5.7 0.1 collective-permute-start.2
  5.7 0.0 copy-done.3
  5.7 0.0 copy-done.2
  5.7 2.6 %shard_map.56.first_ref.refs_0_ = f32[768,512]{1,0:T(8,128)S(1)} custom-call(f32[1024,1024]{1,0:T(8,128)S(1)} %copy-done.2, f32[1024,512]{1,0:T(8,128)S(1)} %copy-done.3), custom_call_target="tpu_custom_call" | custom-call | flops 2415919104 | tf_op jit(solution)/shard_map/pallas_call | solution.py:42
  8.4 0.0 collective-permute-done.last_x_ref
  8.4 0.0 copy-start.4
  8.4 2.3 %collective-permute-start.1 = (f32[128,128]{1,0:T(8,128)S(1)}, f32[128,128]{1,0:T(8,128)S(1)}, u32[]{:S(2)}, u32[]{:S(2)}) collective-permute-start(f32[128,128]{1,0:T(8,128)S(1)} %add.12), channel_id=1, source_target_pairs={{0,4},{2,6},{4,0},{6,2},{8,12},{10,14},{12,8},{14,10},{1,5},{3,7},... | collective-permute-start | bytes 196616 | tf_op jit(solution)/shard_map/ppermute | solution.py:232
  10.7 1.0 %shard_map.57.last_ref.refs_1_ = f32[256,512]{1,0:T(8,128)S(1)} custom-call(f32[1024,1024]{1,0:T(8,128)S(1)} %copy-done.2, f32[1024,512]{1,0:T(8,128)S(1)} %copy-done.3), custom_call_target="tpu_custom_call" | custom-call | flops 805306368 | tf_op jit(solution)/shard_map/pallas_call | solution.py:42
  11.7 0.0 copy-done.4
  11.7 0.0 copy-start
  11.7 1.4 %shard_map.58 = (f32[384,256]{1,0:T(8,128)S(1)}, f32[384,256]{1,0:T(8,128)S(1)}) custom-call(f32[3,1024,128]{2,1,0:T(8,128)S(1)} %copy-done.4, f32[768,512]{1,0:T(8,128)S(1)} %shard_map.56.first_ref.refs_0_, f32[256,512]{1,0:T(8,128)S(1)} %shard_map.57.last_ref.refs_1_), custom_call_target="tpu_custom_call" | custom-call | flops 1207959552 | tf_op jit(solution)/shard_map/pallas_call | solution.py:42
  13.2 0.0 collective-permute-done.1.last_z_ref
  13.2 0.0 collective-permute-done.2.pairs_x_ref
  13.2 0.1 collective-permute-start.3
  13.3 0.0 copy-done
  13.3 0.3 shard_map.59.fix_ref
  13.6 0.5 %collective-permute-start.4 = (f32[384,128]{1,0:T(8,128)S(1)}, f32[384,128]{1,0:T(8,128)S(1)}, u32[]{:S(2)}, u32[]{:S(2)}) collective-permute-start(f32[384,128]{1,0:T(8,128)S(1)} %shard_map.59.fix_ref), channel_id=1, source_target_pairs={{0,1},{1,0},{2,3},{3,2},{4,5},{5,4},{6,7},{7,6},{8,9},{9,8},{10,11... | collective-permute-start | bytes 589832 | tf_op jit(solution)/shard_map/ppermute | solution.py:236
  14.2 1.1 %collective-permute-done.4.fix_other_ref = f32[384,128]{1,0:T(8,128)S(1)} collective-permute-done((f32[384,128]{1,0:T(8,128)S(1)}, f32[384,128]{1,0:T(8,128)S(1)}, u32[]{:S(2)}, u32[]{:S(2)}) %collective-permute-start.4) | collective-permute-done | bytes 196640 | tf_op jit(solution)/shard_map/ppermute | solution.py:236
  15.3 0.0 collective-permute-done.3.recv_ref
  15.3 0.5 %shard_map.60 = (f32[128,256]{1,0:T(8,128)S(1)}, f32[128,256]{1,0:T(8,128)S(1)}, f32[128,256]{1,0:T(8,128)S(1)}) custom-call(f32[384,256]{1,0:T(8,128)S(1)} %get-tuple-element.22.keep_ref, f32[384,256]{1,0:T(8,128)S(1)} %collective-permute-done.3.recv_ref, f32[384,128]{1,0:T(8,128)S(1)} %shard_map.59.fix_ref, f32[384,128]{1,0:T(8,128)S(1)} %collective-permute-done.4.fix_other_ref), custom_call_target="tpu_custom_call" | custom-call | flops 75497472 | tf_op jit(solution)/shard_map/pallas_call | solution.py:42
  15.8 1.8 %collective-permute-start.6 = (f32[128,256]{1,0:T(8,128)S(1)}, f32[128,256]{1,0:T(8,128)S(1)}, u32[]{:S(2)}, u32[]{:S(2)}) collective-permute-start(f32[128,256]{1,0:T(8,128)S(1)} %get-tuple-element.27.refs_0_), channel_id=1, source_target_pairs={{0,4},{1,3},{2,6},{3,1},{4,0},{5,7},{6,2},{7,5},{8,12},{9,11},{10,... | collective-permute-start | bytes 393224 | tf_op jit(solution)/shard_map/ppermute | solution.py:246
  17.5 1.7 %collective-permute-start.5 = (f32[128,256]{1,0:T(8,128)S(1)}, f32[128,256]{1,0:T(8,128)S(1)}, u32[]{:S(2)}, u32[]{:S(2)}) collective-permute-start(f32[128,256]{1,0:T(8,128)S(1)} %shard_map.61), channel_id=1, source_target_pairs={{0,2},{2,0},{4,6},{6,4},{8,10},{10,8},{12,14},{14,12},{1,3},{3,1},... | collective-permute-start | bytes 393224 | tf_op jit(solution)/shard_map/ppermute | solution.py:232
  19.2 1.6 %collective-permute-done.6 = f32[128,256]{1,0:T(8,128)S(1)} collective-permute-done((f32[128,256]{1,0:T(8,128)S(1)}, f32[128,256]{1,0:T(8,128)S(1)}, u32[]{:S(2)}, u32[]{:S(2)}) %collective-permute-start.6) | collective-permute-done | bytes 131104 | tf_op jit(solution)/shard_map/ppermute | solution.py:246
  20.8 1.8 %collective-permute-start.7 = (f32[128,256]{1,0:T(8,128)S(1)}, f32[128,256]{1,0:T(8,128)S(1)}, u32[]{:S(2)}, u32[]{:S(2)}) collective-permute-start(f32[128,256]{1,0:T(8,128)S(1)} %add.13.refs_0_), channel_id=1, source_target_pairs={{0,2},{1,5},{2,0},{3,7},{4,6},{5,1},{6,4},{7,3},{8,10},{9,13},{10,... | collective-permute-start | bytes 393224 | tf_op jit(solution)/shard_map/ppermute | solution.py:246
  22.6 0.0 copy-start.1
  22.6 0.5 %collective-permute-done.5 = f32[128,256]{1,0:T(8,128)S(1)} collective-permute-done((f32[128,256]{1,0:T(8,128)S(1)}, f32[128,256]{1,0:T(8,128)S(1)}, u32[]{:S(2)}, u32[]{:S(2)}) %collective-permute-start.5) | collective-permute-done | bytes 131104 | tf_op jit(solution)/shard_map/ppermute | solution.py:232
  23.1 1.3 %collective-permute-start.8 = (f32[128,256]{1,0:T(8,128)S(1)}, f32[128,256]{1,0:T(8,128)S(1)}, u32[]{:S(2)}, u32[]{:S(2)}) collective-permute-start(f32[128,256]{1,0:T(8,128)S(1)} %add.14.v_ref), channel_id=1, source_target_pairs={{0,4},{2,6},{4,0},{6,2},{8,12},{10,14},{12,8},{14,10},{1,5},{3,7},... | collective-permute-start | bytes 393224 | tf_op jit(solution)/shard_map/ppermute | solution.py:232
  24.4 1.7 %collective-permute-start.9 = (f32[128,256]{1,0:T(8,128)S(1)}, f32[128,256]{1,0:T(8,128)S(1)}, u32[]{:S(2)}, u32[]{:S(2)}) collective-permute-start(f32[128,256]{1,0:T(8,128)S(1)} %shard_map.62.q_ref), channel_id=1, source_target_pairs={{0,2},{2,0},{4,6},{6,4},{8,10},{10,8},{12,14},{14,12},{1,3},{3,1},... | collective-permute-start | bytes 393224 | tf_op jit(solution)/shard_map/ppermute | solution.py:232
  26.1 0.0 collective-permute-done.7
  26.2 2.7 %collective-permute-start.12 = (f32[128,256]{1,0:T(8,128)S(1)}, f32[128,256]{1,0:T(8,128)S(1)}, u32[]{:S(2)}, u32[]{:S(2)}) collective-permute-start(f32[128,256]{1,0:T(8,128)S(1)} %add.15.refs_5_), channel_id=1, source_target_pairs={{0,8},{2,10},{4,12},{6,14},{8,0},{10,2},{12,4},{14,6},{1,9},{3,11}... | collective-permute-start | bytes 393224 | tf_op jit(solution)/shard_map/ppermute | solution.py:232
  28.8 0.0 collective-permute-done.8.vz_ref
  28.8 0.9 %collective-permute-done.9.qx_ref = f32[128,256]{1,0:T(8,128)S(1)} collective-permute-done((f32[128,256]{1,0:T(8,128)S(1)}, f32[128,256]{1,0:T(8,128)S(1)}, u32[]{:S(2)}, u32[]{:S(2)}) %collective-permute-start.9) | collective-permute-done | bytes 131104 | tf_op jit(solution)/shard_map/ppermute | solution.py:232
  29.7 0.4 shard_map.63.refs_4_
  30.1 0.1 collective-permute-start.10
  30.2 0.5 %collective-permute-start.11 = (f32[128,256]{1,0:T(8,128)S(1)}, f32[128,256]{1,0:T(8,128)S(1)}, u32[]{:S(2)}, u32[]{:S(2)}) collective-permute-start(f32[128,256]{1,0:T(8,128)S(1)} %add.15.refs_5_), channel_id=1, source_target_pairs={{0,1},{1,0},{2,3},{3,2},{4,5},{5,4},{6,7},{7,6},{8,9},{9,8},{10,11... | collective-permute-start | bytes 393224 | tf_op jit(solution)/shard_map/ppermute | solution.py:236
  30.7 4.2 %collective-permute-done.12.refs_6_ = f32[128,256]{1,0:T(8,128)S(1)} collective-permute-done((f32[128,256]{1,0:T(8,128)S(1)}, f32[128,256]{1,0:T(8,128)S(1)}, u32[]{:S(2)}, u32[]{:S(2)}) %collective-permute-start.12) | collective-permute-done | bytes 131104 | tf_op jit(solution)/shard_map/ppermute | solution.py:232
  34.9 0.0 collective-permute-start.13
  34.9 0.0 copy-done.1
  34.9 1.4 %shard_map.64.refs_0_ = f32[1024,256]{1,0:T(8,128)S(1)} custom-call(f32[768,512]{1,0:T(8,128)S(1)} %shard_map.56.first_ref.refs_0_, f32[256,512]{1,0:T(8,128)S(1)} %shard_map.57.last_ref.refs_1_, f32[3,1024,128]{2,1,0:T(8,128)S(1)} %copy-done.1, f32[1792,256]{1,0:T(8,128)S(1)} %copy-done, f32[256,256]{1,0:T(8,128)S(1)} %shard_map.63.refs_4_, ...), custom_call_target="tpu_custom_call" | custom-call | tf_op jit(solution)/shard_map/pallas_call | solution.py:42
  36.3 0.0 collective-permute-done.11.w_ref
  36.3 0.0 collective-permute-done.13.far_ref
  36.3 0.0 collective-permute-done.10.k_ref
  36.3 2.2 %shard_map.65 = f32[1024,512]{1,0:T(8,128)} custom-call(f32[768,512]{1,0:T(8,128)S(1)} %shard_map.56.first_ref.refs_0_, f32[256,512]{1,0:T(8,128)S(1)} %shard_map.57.last_ref.refs_1_, f32[3,1024,128]{2,1,0:T(8,128)S(1)} %copy-done.1, f32[1792,256]{1,0:T(8,128)S(1)} %copy-done, f32[256,256]{1,0:T(8,128)S(1)} %collective-permute-done.10.k_ref, ...), custom_call_target="tpu_custom_call" | custom-call | tf_op jit(solution)/shard_map/pallas_call | solution.py:42
  (6 shorter events, 0.1 us)
Async XLA Ops:
  0.0 5.7 %copy-start.3 = (f32[1024,512]{1,0:T(8,128)S(1)}, f32[1024,512]{1,0:T(8,128)}, u32[]{:S(2)}) copy-start(f32[1024,512]{1,0:T(8,128)} %right_ref.1) | copy-start | bytes 6291460
  0.0 5.7 %copy-start.2 = (f32[1024,1024]{1,0:T(8,128)S(1)}, f32[1024,1024]{1,0:T(8,128)}, u32[]{:S(2)}) copy-start(f32[1024,1024]{1,0:T(8,128)} %leaf_ref.3) | copy-start | bytes 12582916
  2.6 5.7 %collective-permute-start = (f32[128,128]{1,0:T(8,128)S(1)}, f32[128,128]{1,0:T(8,128)S(1)}, u32[]{:S(2)}, u32[]{:S(2)}) collective-permute-start(f32[128,128]{1,0:T(8,128)S(1)} %get-tuple-element.19.last_ref), channel_id=1, source_target_pairs={{0,2},{2,0},{4,6},{6,4},{8,10},{10,8},{12,14},{14,12},{1,3},{3,1},... | collective-permute-start | bytes 196616 | tf_op jit(solution)/shard_map/ppermute | solution.py:232
  5.7 7.6 %collective-permute-start.2 = (f32[256,128]{1,0:T(8,128)S(1)}, f32[256,128]{1,0:T(8,128)S(1)}, u32[]{:S(2)}, u32[]{:S(2)}) collective-permute-start(f32[256,128]{1,0:T(8,128)S(1)} %get-tuple-element.24.pairs_ref), channel_id=1, source_target_pairs={{0,2},{2,0},{4,6},{6,4},{8,10},{10,8},{12,14},{14,12},{1,3},{3,1},... | collective-permute-start | bytes 393224 | tf_op jit(solution)/shard_map/ppermute | solution.py:232
  8.4 3.3 %copy-start.4 = (f32[3,1024,128]{2,1,0:T(8,128)S(1)}, f32[3,1024,128]{2,1,0:T(8,128)}, u32[]{:S(2)}) copy-start(f32[3,1024,128]{2,1,0:T(8,128)} %dual_ref.1) | copy-start | bytes 4718596
  8.4 4.8 %collective-permute-start.1 = (f32[128,128]{1,0:T(8,128)S(1)}, f32[128,128]{1,0:T(8,128)S(1)}, u32[]{:S(2)}, u32[]{:S(2)}) collective-permute-start(f32[128,128]{1,0:T(8,128)S(1)} %add.12), channel_id=1, source_target_pairs={{0,4},{2,6},{4,0},{6,2},{8,12},{10,14},{12,8},{14,10},{1,5},{3,7},... | collective-permute-start | bytes 196616 | tf_op jit(solution)/shard_map/ppermute | solution.py:232
  11.7 1.6 %copy-start = (f32[1792,256]{1,0:T(8,128)S(1)}, f32[1792,256]{1,0:T(8,128)}, u32[]{:S(2)}) copy-start(f32[1792,256]{1,0:T(8,128)} %cores_ref.5) | copy-start | bytes 5505028
  13.2 2.1 %collective-permute-start.3 = (f32[384,256]{1,0:T(8,128)S(1)}, f32[384,256]{1,0:T(8,128)S(1)}, u32[]{:S(2)}, u32[]{:S(2)}) collective-permute-start(f32[384,256]{1,0:T(8,128)S(1)} %get-tuple-element.25), channel_id=1, source_target_pairs={{0,1},{1,0},{2,3},{3,2},{4,5},{5,4},{6,7},{7,6},{8,9},{9,8},{10,11... | collective-permute-start | bytes 1179656 | tf_op jit(solution)/shard_map/ppermute | solution.py:236
  13.6 1.7 %collective-permute-start.4 = (f32[384,128]{1,0:T(8,128)S(1)}, f32[384,128]{1,0:T(8,128)S(1)}, u32[]{:S(2)}, u32[]{:S(2)}) collective-permute-start(f32[384,128]{1,0:T(8,128)S(1)} %shard_map.59.fix_ref), channel_id=1, source_target_pairs={{0,1},{1,0},{2,3},{3,2},{4,5},{5,4},{6,7},{7,6},{8,9},{9,8},{10,11... | collective-permute-start | bytes 589832 | tf_op jit(solution)/shard_map/ppermute | solution.py:236
  15.8 5.0 %collective-permute-start.6 = (f32[128,256]{1,0:T(8,128)S(1)}, f32[128,256]{1,0:T(8,128)S(1)}, u32[]{:S(2)}, u32[]{:S(2)}) collective-permute-start(f32[128,256]{1,0:T(8,128)S(1)} %get-tuple-element.27.refs_0_), channel_id=1, source_target_pairs={{0,4},{1,3},{2,6},{3,1},{4,0},{5,7},{6,2},{7,5},{8,12},{9,11},{10,... | collective-permute-start | bytes 393224 | tf_op jit(solution)/shard_map/ppermute | solution.py:246
  17.5 5.5 %collective-permute-start.5 = (f32[128,256]{1,0:T(8,128)S(1)}, f32[128,256]{1,0:T(8,128)S(1)}, u32[]{:S(2)}, u32[]{:S(2)}) collective-permute-start(f32[128,256]{1,0:T(8,128)S(1)} %shard_map.61), channel_id=1, source_target_pairs={{0,2},{2,0},{4,6},{6,4},{8,10},{10,8},{12,14},{14,12},{1,3},{3,1},... | collective-permute-start | bytes 393224 | tf_op jit(solution)/shard_map/ppermute | solution.py:232
  20.8 5.3 %collective-permute-start.7 = (f32[128,256]{1,0:T(8,128)S(1)}, f32[128,256]{1,0:T(8,128)S(1)}, u32[]{:S(2)}, u32[]{:S(2)}) collective-permute-start(f32[128,256]{1,0:T(8,128)S(1)} %add.13.refs_0_), channel_id=1, source_target_pairs={{0,2},{1,5},{2,0},{3,7},{4,6},{5,1},{6,4},{7,3},{8,10},{9,13},{10,... | collective-permute-start | bytes 393224 | tf_op jit(solution)/shard_map/ppermute | solution.py:246
  22.6 12.3 %copy-start.1 = (f32[3,1024,128]{2,1,0:T(8,128)S(1)}, f32[3,1024,128]{2,1,0:T(8,128)}, u32[]{:S(2)}) copy-start(f32[3,1024,128]{2,1,0:T(8,128)} %row_ref.1) | copy-start | bytes 4718596
  23.1 5.7 %collective-permute-start.8 = (f32[128,256]{1,0:T(8,128)S(1)}, f32[128,256]{1,0:T(8,128)S(1)}, u32[]{:S(2)}, u32[]{:S(2)}) collective-permute-start(f32[128,256]{1,0:T(8,128)S(1)} %add.14.v_ref), channel_id=1, source_target_pairs={{0,4},{2,6},{4,0},{6,2},{8,12},{10,14},{12,8},{14,10},{1,5},{3,7},... | collective-permute-start | bytes 393224 | tf_op jit(solution)/shard_map/ppermute | solution.py:232
  24.4 5.3 %collective-permute-start.9 = (f32[128,256]{1,0:T(8,128)S(1)}, f32[128,256]{1,0:T(8,128)S(1)}, u32[]{:S(2)}, u32[]{:S(2)}) collective-permute-start(f32[128,256]{1,0:T(8,128)S(1)} %shard_map.62.q_ref), channel_id=1, source_target_pairs={{0,2},{2,0},{4,6},{6,4},{8,10},{10,8},{12,14},{14,12},{1,3},{3,1},... | collective-permute-start | bytes 393224 | tf_op jit(solution)/shard_map/ppermute | solution.py:232
  26.2 8.7 %collective-permute-start.12 = (f32[128,256]{1,0:T(8,128)S(1)}, f32[128,256]{1,0:T(8,128)S(1)}, u32[]{:S(2)}, u32[]{:S(2)}) collective-permute-start(f32[128,256]{1,0:T(8,128)S(1)} %add.15.refs_5_), channel_id=1, source_target_pairs={{0,8},{2,10},{4,12},{6,14},{8,0},{10,2},{12,4},{14,6},{1,9},{3,11}... | collective-permute-start | bytes 393224 | tf_op jit(solution)/shard_map/ppermute | solution.py:232
  30.1 6.2 %collective-permute-start.10 = (f32[256,256]{1,0:T(8,128)S(1)}, f32[256,256]{1,0:T(8,128)S(1)}, u32[]{:S(2)}, u32[]{:S(2)}) collective-permute-start(f32[256,256]{1,0:T(8,128)S(1)} %shard_map.63.refs_4_), channel_id=1, source_target_pairs={{0,1},{1,0},{2,3},{3,2},{4,5},{5,4},{6,7},{7,6},{8,9},{9,8},{10,11... | collective-permute-start | bytes 786440 | tf_op jit(solution)/shard_map/ppermute | solution.py:236
  30.2 6.1 %collective-permute-start.11 = (f32[128,256]{1,0:T(8,128)S(1)}, f32[128,256]{1,0:T(8,128)S(1)}, u32[]{:S(2)}, u32[]{:S(2)}) collective-permute-start(f32[128,256]{1,0:T(8,128)S(1)} %add.15.refs_5_), channel_id=1, source_target_pairs={{0,1},{1,0},{2,3},{3,2},{4,5},{5,4},{6,7},{7,6},{8,9},{9,8},{10,11... | collective-permute-start | bytes 393224 | tf_op jit(solution)/shard_map/ppermute | solution.py:236
  34.9 1.4 %collective-permute-start.13 = (f32[128,256]{1,0:T(8,128)S(1)}, f32[128,256]{1,0:T(8,128)S(1)}, u32[]{:S(2)}, u32[]{:S(2)}) collective-permute-start(f32[128,256]{1,0:T(8,128)S(1)} %collective-permute-done.12.refs_6_), channel_id=1, source_target_pairs={{0,1},{1,0},{2,3},{3,2},{4,5},{5,4},{6,7},{7,6},{8,9},{9,8},{10,11... | collective-permute-start | bytes 393224 | tf_op jit(solution)/shard_map/ppermute | solution.py:236

commit v4 on v2

v4 whole, which is shorter than its diff:
```python
import functools

import jax
import jax.numpy as jnp
from jax import lax
from jax.experimental import pallas as pl
from jax.experimental.pallas import tpu as pltpu
from jax.sharding import PartitionSpec as P

F32, BF16 = jnp.float32, jnp.bfloat16
VMEM = pl.BlockSpec(memory_space=pltpu.VMEM)


def dot(a, b):
    return jnp.dot(a, b, precision=lax.Precision.HIGH, preferred_element_type=F32)


def dot_t(a, b):
    return lax.dot_general(
        a, b, (((0,), (0,)), ((), ())), precision=lax.Precision.HIGH, preferred_element_type=F32
    )


def halves(x):
    high = x.astype(BF16)
    return high, (x - high.astype(F32)).astype(BF16)


def dot3(a, b):
    def one(x, y):
        return jnp.dot(x, y, preferred_element_type=F32)

    return one(a[0], b[0]) + one(a[0], b[1]) + one(a[1], b[0])


def shape(*dims, dtype=F32):
    return jax.ShapeDtypeStruct(dims, dtype)


def call(body, outs, args, flops, in_specs=None, scratch=(), aliases=None, out_specs=None):
    bytes_accessed = sum(a.size * a.dtype.itemsize for a in args)
    return pl.pallas_call(
        body,
        in_specs=in_specs or [VMEM] * len(args),
        out_specs=jax.tree.map(lambda _: VMEM, outs) if out_specs is None else out_specs,
        out_shape=outs,
        scratch_shapes=list(scratch),
        input_output_aliases=aliases or {},
        compiler_params=pltpu.CompilerParams(vmem_limit_bytes=24 * 2**20),
        cost_estimate=pl.CostEstimate(
            flops=flops, bytes_accessed=0, transcendentals=0
        ),
    )(*args)


def place(rest):
    child = lax.shift_right_logical(lax.axis_index("wide"), rest)
    return child, lax.axis_index("narrow")


def block(index, size):
    return pl.ds(pl.multiple_of(index * size, size), size)


def last_product(dual_hbm, row_hbm, out_ref, dual_ref, row_ref, sems):
    rows = dual_ref.shape[0]
    pieces = sems.shape[0]
    step = rows // pieces
    copies = []
    for i in range(pieces):
        part = pl.ds(i * step, step)
        copies.append((
            pltpu.make_async_copy(dual_hbm.at[0, part], dual_ref.at[part], sems.at[i, 0]),
            pltpu.make_async_copy(row_hbm.at[1, part], row_ref.at[part], sems.at[i, 1]),
        ))
        for copy in copies[-1]:
            copy.start()
    total = jnp.zeros(out_ref.shape, F32)
    for i in range(pieces):
        for copy in copies[i]:
            copy.wait()
        part = slice(i * step, (i + 1) * step)
        total += dot_t(dual_ref[part], row_ref[part])
    out_ref[...] = total


def pair_products(dual_ref, row_ref, last_ref, out_ref):
    rank = row_ref.shape[2]
    out_ref[:rank] = dot_t(dual_ref[1], row_ref[2])
    out_ref[rank:] = dot_t(dual_ref[0], row_ref[2])


def leaf_rows(start, leaf_ref, right_ref, field_ref):
    rows = field_ref.shape[0]
    step = min(256, rows)
    right = halves(right_ref[...])
    for i in range(0, rows, step):
        field_ref[i:i + step] = dot3(halves(leaf_ref[start + i:start + i + step]), right)


def projections(rest, dual_ref, first_ref, last_ref, keep_ref, send_ref, high_ref, low_ref):
    levels, rows, rank = dual_ref.shape
    for l in range(levels):
        high, low = halves(dual_ref[l].T)
        high_ref[l * rank:(l + 1) * rank] = high
        low_ref[l * rank:(l + 1) * rank] = low
    _, core = place(rest)
    half = keep_ref.shape[1]
    cut = first_ref.shape[0]
    for out, index in ((keep_ref, core), (send_ref, 1 - core)):
        cols = block(index, half)
        top, bottom = halves(first_ref[:, cols]), halves(last_ref[:, cols])
        out[...] = dot3((high_ref[:, :cut], low_ref[:, :cut]), top) + dot3(
            (high_ref[:, cut:], low_ref[:, cut:]), bottom
        )


def corrections(rest, pairs_ref, pairs_x_ref, last_ref, last_x_ref, last_z_ref, cores_ref, out_ref):
    rank = last_ref.shape[0]
    child, _ = place(rest)
    pair = lax.shift_right_logical(child, 1)
    slot3, slot2 = child & 1, pair & 1
    own = cores_ref[block(6 + child, rank), block(slot3, rank)]
    other = cores_ref[block(6 + (child ^ 1), rank), block(slot3, rank)]
    out_ref[:2 * rank] = dot(pairs_ref[...], own) + dot(pairs_x_ref[...], other)
    own = cores_ref[block(2 + pair, rank), block(slot2, rank)]
    other = cores_ref[block(2 + (pair ^ 1), rank), block(slot2, rank)]
    out_ref[2 * rank:] = dot(last_ref[...] + last_x_ref[...], own) + dot(last_z_ref[...], other)


def corrected(keep_ref, recv_ref, fix_ref, fix_other_ref, w_ref, v_ref, q_ref):
    rank = v_ref.shape[0]
    q = keep_ref[...] + recv_ref[...]
    fix = fix_ref[...] + fix_other_ref[...]
    q1, q2, q3 = q[:rank], q[rank:2 * rank], q[2 * rank:]
    both = dot(fix[:2 * rank], q3)
    v = q2 - both[:rank]
    w_ref[...] = q1 - both[rank:] - dot(fix[2 * rank:], v)
    v_ref[...] = v
    q_ref[...] = q3


def coefficient(level, child, cores_ref, own, other):
    rank = own.shape[0]
    slot = child & 1
    rows = block(2**level - 2 + child, rank)
    return dot(cores_ref[rows, block(slot, rank)], own) + dot(
        cores_ref[rows, block(1 - slot, rank)], other
    )


def lower_two(rest, v_ref, vz_ref, cores_ref, first_ref, last_ref, row_ref, k_ref, out_ref):
    child, core = place(rest)
    k = coefficient(2, lax.shift_right_logical(child, 1), cores_ref, v_ref[...], vz_ref[...])
    k_ref[...] = k
    cols = block(core, k.shape[1])
    cut = first_ref.shape[0]
    term = dot(row_ref[1], k)
    out_ref[:cut] = first_ref[:, cols] - term[:cut]
    out_ref[cut:] = last_ref[:, cols] - term[cut:]


def lower_three(rest, q_ref, qx_ref, cores_ref, field_ref, row_ref, k_ref, out_ref):
    child, _ = place(rest)
    k = coefficient(3, child, cores_ref, q_ref[...], qx_ref[...])
    k_ref[...] = k
    out_ref[...] = field_ref[...] - dot(row_ref[2], k)


def lower_update(index, first_ref, last_ref, row_ref, k, out_ref):
    cols = block(index, k.shape[1])
    cut = first_ref.shape[0]
    lefts = jnp.concatenate([row_ref[1], row_ref[2]], 1)
    term = dot(lefts, k)
    out_ref[:cut] = first_ref[:, cols] - term[:cut]
    out_ref[cut:] = last_ref[:, cols] - term[cut:]


def top_coefficient(rest, w_ref, far_ref, cores_ref):
    rank = w_ref.shape[0]
    child, _ = place(rest)
    slot1 = lax.shift_right_logical(child, 2)
    rows1 = block(slot1, rank)
    return dot(cores_ref[rows1, block(slot1, rank)], w_ref[...]) + dot(
        cores_ref[rows1, block(1 - slot1, rank)], far_ref[...]
    )


def solve_own(rest, own_ref, first_ref, last_ref, row_ref, cores_ref, w_ref, far_ref, *refs):
    *k_refs, out_ref, other_ref = refs
    _, core = place(rest)
    out_ref[...] = own_ref[...] - dot(row_ref[0], top_coefficient(rest, w_ref, far_ref, cores_ref))
    k = jnp.concatenate([ref[...] for ref in k_refs], 0)
    lower_update(1 - core, first_ref, last_ref, row_ref, k, other_ref)


def solve_other(rest, pieces, own_ref, less_ref, row_ref, cores_ref, w_ref, far_ref, out_ref, other_ref, sems):
    _, core = place(rest)
    total, half = own_ref.shape
    mine, theirs = block(core, half), block(1 - core, half)
    copies = [pltpu.make_async_copy(own_ref, out_ref.at[:, mine], sems.at[pieces])]
    copies[0].start()
    top = top_coefficient(rest, w_ref, far_ref, cores_ref)
    step = total // pieces
    for i in range(pieces):
        part = slice(i * step, (i + 1) * step)
        other_ref[part] = less_ref[part] - dot(row_ref[0, part], top)
        copy = pltpu.make_async_copy(other_ref.at[part], out_ref.at[part, theirs], sems.at[i])
        copy.start()
        copies.append(copy)
    for copy in copies:
        copy.wait()


def tie(x, *others):
    def body(x_ref, *refs):
        refs[-1][...] = x_ref[...]

    return call(body, shape(*x.shape), (x, *others), 0)


def after(x, *others):
    return lax.optimization_barrier((x, *others))[0]


def swap_wide(x, bit):
    count = lax.axis_size("wide")
    return lax.ppermute(x, "wide", [(w, w ^ (1 << bit)) for w in range(count)])


def swap_narrow(x):
    return lax.ppermute(x, "narrow", [(0, 1), (1, 0)])


def swap_crossed(x, first, second):
    wides, cores = lax.axis_size("wide"), lax.axis_size("narrow")
    route = []
    for w in range(wides):
        for n in range(cores):
            bit = first if n == 0 else second
            route.append((w * cores + n, (w ^ (1 << bit)) * cores + n))
    return lax.ppermute(x, ("wide", "narrow"), route)


def shards(right_side, leaf_inverse, row_bases, dual_bases, woodbury_cores):
    levels, rows, rank = row_bases.shape
    cols = right_side.shape[1]
    half = cols // 2
    rest = lax.axis_size("wide").bit_length() - 1 - levels
    bit3, bit2, bit1 = rest, rest + 1, rest + 2
    cut = rows // 2

    pieces = 1
    last = call(
        last_product, shape(rank, rank),
        tuple(pltpu.with_memory_space_constraint(x, pltpu.HBM) for x in (dual_bases, row_bases)),
        30 * rows * rows * cols, in_specs=[pl.BlockSpec(memory_space=pltpu.HBM)] * 2,
        scratch=[pltpu.VMEM((rows, rank), F32)] * 2 + [pltpu.SemaphoreType.DMA((pieces, 2))],
    )
    pairs = call(
        pair_products, shape(2 * rank, rank), (dual_bases, row_bases, last), 4 * rows * rank * rank,
    )
    for bit in range(rest):
        pairs, last = pairs + swap_wide(pairs, bit), last + swap_wide(last, bit)
    last_x, pairs_x = swap_wide(last, bit3), swap_wide(pairs, bit3)

    first_rows = call(
        functools.partial(leaf_rows, 0), shape(cut, cols), (leaf_inverse, after(right_side, last)),
        6 * cut * rows * cols,
    )
    last_z = swap_wide(last + last_x, bit2)
    last_rows = call(
        functools.partial(leaf_rows, cut), shape(rows - cut, cols), (leaf_inverse, after(right_side, last_x)),
        6 * (rows - cut) * rows * cols,
    )
    keep, send = call(
        functools.partial(projections, rest), (shape(levels * rank, half),) * 2,
        (dual_bases, first_rows, last_rows), 6 * levels * rank * rows * cols,
        scratch=[pltpu.VMEM((levels * rank, rows), BF16)] * 2,
    )
    recv = swap_narrow(after(send, last_z, pairs_x))
    fix = call(
        functools.partial(corrections, rest), shape(levels * rank, rank),
        (pairs, pairs_x, last, last_x, last_z, woodbury_cores), 36 * rank**3,
    )
    fix_other = swap_narrow(fix)
    if rest:
        keep = keep + recv
        for bit in range(rest):
            keep = keep + swap_wide(keep, bit)
        recv = jnp.zeros_like(keep)
    w, v, q = call(
        corrected, (shape(rank, half),) * 3, (keep, recv, fix, fix_other), 18 * rank * rank * half
    )

    v = tie(v, w)
    v_x = swap_wide(v, bit3)
    w = w_mid = w + swap_crossed(w, bit2, bit3)
    q = tie(q, w_mid)
    q_x = swap_wide(q, bit3)
    v = v + after(v_x, w_mid)
    v_z = swap_wide(v, bit2)
    w = w + after(swap_crossed(w, bit3, bit2), v, q)
    far = swap_wide(w, bit1)
    k2, lower = call(
        functools.partial(lower_two, rest), (shape(rank, half), shape(rows, half)),
        (after(v, w), v_z, woodbury_cores, first_rows, last_rows, row_bases), 0,
    )
    k3, lower = call(
        functools.partial(lower_three, rest), (shape(rank, half), shape(rows, half)),
        (q, q_x, woodbury_cores, lower, row_bases), 0,
    )
    k_other = [swap_narrow(k2), swap_narrow(k3)]
    w_other = swap_narrow(after(w, v_z, q_x))
    far_other = swap_narrow(far)
    own, less = call(
        functools.partial(solve_own, rest), (shape(rows, half),) * 2,
        (lower, first_rows, last_rows, row_bases, woodbury_cores, w, far, *k_other), 0,
    )
    pieces = 4
    return call(
        functools.partial(solve_other, rest, pieces), shape(rows, cols),
        (own, less, row_bases, woodbury_cores, w_other, far_other), 0,
        scratch=[pltpu.VMEM((rows, half), F32), pltpu.SemaphoreType.DMA((pieces + 1,))],
        out_specs=pl.BlockSpec(memory_space=pltpu.HBM),
    )


def solution(mesh):
    return jax.shard_map(
        shards,
        mesh=mesh,
        in_specs=(
            P(("parts", "wide", "narrow"), None),
            P(("parts", "wide", "narrow"), None),
            P(None, ("parts", "wide", "narrow"), None),
            P(None, ("parts", "wide", "narrow"), None),
            P("parts", None),
        ),
        out_specs=P(("parts", "wide", "narrow"), None),
        check_vma=False,
    )
```

time: 52.1 us -> 37.4 us (0.72)
  waiting for transfers between devices: 21.3 us -> 6.71 us
  local copies, waits for them, and re-layouts: 3.8 us -> 0.02 us
  Pallas kernels: 10.9 us -> 13.4 us
  starting transfers between devices: 15.6 us -> 16.8 us
    ppermute x6 -> x7, waiting for transfers between devices: 19.5 us -> 3.5 us  [swap_wide(): return lax.ppermute(x, 'wide', [(w, w ^ 1 << bit) for w in range(count)])]
    unnamed x10, local copies, waits for them, and re-layouts: 3.8 us -> 0.02 us
    pallas_call x10 -> x13, Pallas kernels: 10.9 us -> 13.4 us  [call(): pl.pallas_call(body, in_specs=in_specs or [VMEM] * len(args), out_specs=j...]
    ppermute x2, waiting for transfers between devices: 0.41 us -> 2.09 us  [swap_crossed(): return lax.ppermute(x, ('wide', 'narrow'), route)]
    ppermute x6 -> x7, starting transfers between devices: 11.6 us -> 12.6 us  [swap_wide(): return lax.ppermute(x, 'wide', [(w, w ^ 1 << bit) for w in range(count)])]
    ppermute x5 -> x6, starting transfers between devices: 0.67 us -> 1.26 us  [swap_narrow(): return lax.ppermute(x, 'narrow', [(0, 1), (1, 0)])]
    ppermute x5 -> x6, waiting for transfers between devices: 1.44 us -> 1.12 us  [swap_narrow(): return lax.ppermute(x, 'narrow', [(0, 1), (1, 0)])]
  transfers between devices with their start and end apart: 13 -> 15, of which waited for: 7 -> 5; matrix products, arithmetic and copies ran while one was open for 0% -> 0% of each run, Pallas kernels for 7% -> 25%
where the time goes in v4:
time: 37.4 us; the launch traced here: 37.2 us
  starting transfers between devices  16.8 us (45%)
  Pallas kernels  13.4 us (36%)
  waiting for transfers between devices  6.71 us (18%)
    pallas_call x13, Pallas kernels, call(): pl.pallas_call(body, in_specs=in_specs or [VMEM] * len(args), out_specs=j...  13.4 us
    ppermute x7, starting transfers between devices, swap_wide(): return lax.ppermute(x, 'wide', [(w, w ^ 1 << bit) for w in range(count)])  12.6 us
    ppermute x7, waiting for transfers between devices, swap_wide(): return lax.ppermute(x, 'wide', [(w, w ^ 1 << bit) for w in range(count)])  3.5 us
    ppermute x2, starting transfers between devices, swap_crossed(): return lax.ppermute(x, ('wide', 'narrow'), route)  2.93 us
    ppermute x2, waiting for transfers between devices, swap_crossed(): return lax.ppermute(x, ('wide', 'narrow'), route)  2.09 us
    ppermute x6, starting transfers between devices, swap_narrow(): return lax.ppermute(x, 'narrow', [(0, 1), (1, 0)])  1.26 us
    ppermute x6, waiting for transfers between devices, swap_narrow(): return lax.ppermute(x, 'narrow', [(0, 1), (1, 0)])  1.12 us
  transfers between devices with their start and end apart: 15, of which 5 were waited for; matrix products, arithmetic and copies ran while one was open for 0% of the time, Pallas kernels for 25%

profile of v4, /device:TPU:0, one launch (start us, length us, event | category | flops | bytes accessed | tf_op | source)
XLA Modules:
  0.0 37.2 jit_solution(16171379957680412036)
XLA Ops:
  0.0 1.8 %shard_map.55.last_ref = f32[128,128]{1,0:T(8,128)S(1)} custom-call(f32[3,1024,128]{2,1,0:T(8,128)} %dual_ref.3, f32[3,1024,128]{2,1,0:T(8,128)} %row_ref.9), custom_call_target="tpu_custom_call" | custom-call | flops 16106127360 | tf_op jit(solution)/shard_map/pallas_call | solution.py:42
  1.8 0.0 copy-start.3
  1.8 3.0 %collective-permute-start = (f32[128,128]{1,0:T(8,128)S(1)}, f32[128,128]{1,0:T(8,128)S(1)}, u32[]{:S(2)}, u32[]{:S(2)}) collective-permute-start(f32[128,128]{1,0:T(8,128)S(1)} %shard_map.55.last_ref), channel_id=1, source_target_pairs={{0,2},{2,0},{4,6},{6,4},{8,10},{10,8},{12,14},{14,12},{1,3},{3,1},... | collective-permute-start | bytes 196616 | tf_op jit(solution)/shard_map/ppermute | solution.py:228
  4.8 0.0 copy-done.1
  4.8 0.0 copy-done.4
  4.8 0.6 %shard_map.59.pairs_ref = f32[256,128]{1,0:T(8,128)S(1)} custom-call(f32[3,1024,128]{2,1,0:T(8,128)S(1)} %copy-done.4, f32[3,1024,128]{2,1,0:T(8,128)S(1)} %copy-done.1, f32[128,128]{1,0:T(8,128)S(1)} %shard_map.55.last_ref), custom_call_target="tpu_custom_call" | custom-call | flops 67108864 | tf_op jit(solution)/shard_map/pallas_call | solution.py:42
  5.5 0.4 collective-permute-start.2
  5.8 0.0 copy-done.2
  5.8 0.0 copy-done.3
  5.8 1.8 %shard_map.56.first_ref = f32[512,512]{1,0:T(8,128)S(1)} custom-call(f32[1024,1024]{1,0:T(8,128)S(1)} %copy-done.2, f32[1024,512]{1,0:T(8,128)S(1)} %copy-done.3), custom_call_target="tpu_custom_call" | custom-call | flops 1610612736 | tf_op jit(solution)/shard_map/pallas_call | solution.py:42
  7.6 0.0 collective-permute-done.last_x_ref
  7.7 1.9 %collective-permute-start.1 = (f32[128,128]{1,0:T(8,128)S(1)}, f32[128,128]{1,0:T(8,128)S(1)}, u32[]{:S(2)}, u32[]{:S(2)}) collective-permute-start(f32[128,128]{1,0:T(8,128)S(1)} %add.12), channel_id=1, source_target_pairs={{0,4},{2,6},{4,0},{6,2},{8,12},{10,14},{12,8},{14,10},{1,5},{3,7},... | collective-permute-start | bytes 196616 | tf_op jit(solution)/shard_map/ppermute | solution.py:228
  9.5 1.8 %shard_map.57.last_ref = f32[512,512]{1,0:T(8,128)S(1)} custom-call(f32[1024,1024]{1,0:T(8,128)S(1)} %copy-done.2, f32[1024,512]{1,0:T(8,128)S(1)} %copy-done.3), custom_call_target="tpu_custom_call" | custom-call | flops 1610612736 | tf_op jit(solution)/shard_map/pallas_call | solution.py:42
  11.4 0.0 copy-start
  11.4 1.4 %shard_map.58 = (f32[384,256]{1,0:T(8,128)S(1)}, f32[384,256]{1,0:T(8,128)S(1)}) custom-call(f32[3,1024,128]{2,1,0:T(8,128)S(1)} %copy-done.4, f32[512,512]{1,0:T(8,128)S(1)} %shard_map.56.first_ref, f32[512,512]{1,0:T(8,128)S(1)} %shard_map.57.last_ref), custom_call_target="tpu_custom_call" | custom-call | flops 1207959552 | tf_op jit(solution)/shard_map/pallas_call | solution.py:42
  12.8 0.0 collective-permute-done.1.last_z_ref
  12.8 0.0 collective-permute-done.2.pairs_x_ref
  12.8 0.1 collective-permute-start.3
  12.9 0.0 copy-done
  12.9 0.3 shard_map.60.fix_ref
  13.3 0.5 %collective-permute-start.4 = (f32[384,128]{1,0:T(8,128)S(1)}, f32[384,128]{1,0:T(8,128)S(1)}, u32[]{:S(2)}, u32[]{:S(2)}) collective-permute-start(f32[384,128]{1,0:T(8,128)S(1)} %shard_map.60.fix_ref), channel_id=1, source_target_pairs={{0,1},{1,0},{2,3},{3,2},{4,5},{5,4},{6,7},{7,6},{8,9},{9,8},{10,11... | collective-permute-start | bytes 589832 | tf_op jit(solution)/shard_map/ppermute | solution.py:232
  13.8 1.1 %collective-permute-done.4.fix_other_ref = f32[384,128]{1,0:T(8,128)S(1)} collective-permute-done((f32[384,128]{1,0:T(8,128)S(1)}, f32[384,128]{1,0:T(8,128)S(1)}, u32[]{:S(2)}, u32[]{:S(2)}) %collective-permute-start.4) | collective-permute-done | bytes 196640 | tf_op jit(solution)/shard_map/ppermute | solution.py:232
  14.9 0.0 collective-permute-done.3.recv_ref
  14.9 0.5 %shard_map.61 = (f32[128,256]{1,0:T(8,128)S(1)}, f32[128,256]{1,0:T(8,128)S(1)}, f32[128,256]{1,0:T(8,128)S(1)}) custom-call(f32[384,256]{1,0:T(8,128)S(1)} %get-tuple-element.25.keep_ref, f32[384,256]{1,0:T(8,128)S(1)} %collective-permute-done.3.recv_ref, f32[384,128]{1,0:T(8,128)S(1)} %shard_map.60.fix_ref, f32[384,128]{1,0:T(8,128)S(1)} %collective-permute-done.4.fix_other_ref), custom_call_target="tpu_custom_call" | custom-call | flops 75497472 | tf_op jit(solution)/shard_map/pallas_call | solution.py:42
  15.4 1.0 %collective-permute-start.5 = (f32[128,256]{1,0:T(8,128)S(1)}, f32[128,256]{1,0:T(8,128)S(1)}, u32[]{:S(2)}, u32[]{:S(2)}) collective-permute-start(f32[128,256]{1,0:T(8,128)S(1)} %get-tuple-element.29.refs_0_), channel_id=1, source_target_pairs={{0,4},{1,3},{2,6},{3,1},{4,0},{5,7},{6,2},{7,5},{8,12},{9,11},{10,... | collective-permute-start | bytes 393224 | tf_op jit(solution)/shard_map/ppermute | solution.py:242
  16.4 2.0 %collective-permute-start.7 = (f32[128,256]{1,0:T(8,128)S(1)}, f32[128,256]{1,0:T(8,128)S(1)}, u32[]{:S(2)}, u32[]{:S(2)}) collective-permute-start(f32[128,256]{1,0:T(8,128)S(1)} %shard_map.63), channel_id=1, source_target_pairs={{0,2},{2,0},{4,6},{6,4},{8,10},{10,8},{12,14},{14,12},{1,3},{3,1},... | collective-permute-start | bytes 393224 | tf_op jit(solution)/shard_map/ppermute | solution.py:228
  18.3 2.1 %collective-permute-done.5 = f32[128,256]{1,0:T(8,128)S(1)} collective-permute-done((f32[128,256]{1,0:T(8,128)S(1)}, f32[128,256]{1,0:T(8,128)S(1)}, u32[]{:S(2)}, u32[]{:S(2)}) %collective-permute-start.5) | collective-permute-done | bytes 131104 | tf_op jit(solution)/shard_map/ppermute | solution.py:242
  20.5 2.0 %collective-permute-start.8 = (f32[128,256]{1,0:T(8,128)S(1)}, f32[128,256]{1,0:T(8,128)S(1)}, u32[]{:S(2)}, u32[]{:S(2)}) collective-permute-start(f32[128,256]{1,0:T(8,128)S(1)} %add.13.refs_0_), channel_id=1, source_target_pairs={{0,2},{1,5},{2,0},{3,7},{4,6},{5,1},{6,4},{7,3},{8,10},{9,13},{10,... | collective-permute-start | bytes 393224 | tf_op jit(solution)/shard_map/ppermute | solution.py:242
  22.4 0.3 collective-permute-done.7
  22.8 1.2 %collective-permute-start.9 = (f32[128,256]{1,0:T(8,128)S(1)}, f32[128,256]{1,0:T(8,128)S(1)}, u32[]{:S(2)}, u32[]{:S(2)}) collective-permute-start(f32[128,256]{1,0:T(8,128)S(1)} %add.14.v_ref), channel_id=1, source_target_pairs={{0,4},{2,6},{4,0},{6,2},{8,12},{10,14},{12,8},{14,10},{1,5},{3,7},... | collective-permute-start | bytes 393224 | tf_op jit(solution)/shard_map/ppermute | solution.py:228
  23.9 1.6 %collective-permute-start.6 = (f32[128,256]{1,0:T(8,128)S(1)}, f32[128,256]{1,0:T(8,128)S(1)}, u32[]{:S(2)}, u32[]{:S(2)}) collective-permute-start(f32[128,256]{1,0:T(8,128)S(1)} %shard_map.62.q_ref), channel_id=1, source_target_pairs={{0,2},{2,0},{4,6},{6,4},{8,10},{10,8},{12,14},{14,12},{1,3},{3,1},... | collective-permute-start | bytes 393224 | tf_op jit(solution)/shard_map/ppermute | solution.py:228
  25.5 0.0 collective-permute-done.8
  25.5 2.6 %collective-permute-start.10 = (f32[128,256]{1,0:T(8,128)S(1)}, f32[128,256]{1,0:T(8,128)S(1)}, u32[]{:S(2)}, u32[]{:S(2)}) collective-permute-start(f32[128,256]{1,0:T(8,128)S(1)} %add.15.w_ref), channel_id=1, source_target_pairs={{0,8},{2,10},{4,12},{6,14},{8,0},{10,2},{12,4},{14,6},{1,9},{3,11}... | collective-permute-start | bytes 393224 | tf_op jit(solution)/shard_map/ppermute | solution.py:228
  28.2 1.6 %collective-permute-done.9.vz_ref = f32[128,256]{1,0:T(8,128)S(1)} collective-permute-done((f32[128,256]{1,0:T(8,128)S(1)}, f32[128,256]{1,0:T(8,128)S(1)}, u32[]{:S(2)}, u32[]{:S(2)}) %collective-permute-start.9) | collective-permute-done | bytes 131104 | tf_op jit(solution)/shard_map/ppermute | solution.py:228
  29.7 0.0 collective-permute-done.6.qx_ref
  29.7 1.0 %shard_map.64 = (f32[128,256]{1,0:T(8,128)S(1)}, f32[1024,256]{1,0:T(8,128)S(1)}) custom-call(f32[128,256]{1,0:T(8,128)S(1)} %add.14.v_ref, f32[128,256]{1,0:T(8,128)S(1)} %collective-permute-done.9.vz_ref, f32[1792,256]{1,0:T(8,128)S(1)} %copy-done, f32[512,512]{1,0:T(8,128)S(1)} %shard_map.56.first_ref, f32[512,512]{1,0:T(8,128)S(1)} %shard_map.57.last_ref, ...), custom_call_target="tpu_custom_call" | custom-call | tf_op jit(solution)/shard_map/pallas_call | solution.py:42
  30.7 1.0 %shard_map.65 = (f32[128,256]{1,0:T(8,128)S(1)}, f32[1024,256]{1,0:T(8,128)S(1)}) custom-call(f32[128,256]{1,0:T(8,128)S(1)} %shard_map.62.q_ref, f32[128,256]{1,0:T(8,128)S(1)} %collective-permute-done.6.qx_ref, f32[1792,256]{1,0:T(8,128)S(1)} %copy-done, f32[1024,256]{1,0:T(8,128)S(1)} %get-tuple-element.34.field_ref, f32[3,1024,128]{2,1,0:T(8,128)S(1)} %copy-done.1), custom_call_target="tpu_custom_call" | custom-call | tf_op jit(solution)/shard_map/pallas_call | solution.py:42
  31.7 0.1 collective-permute-start.12
  31.8 0.5 %collective-permute-start.11 = (f32[128,256]{1,0:T(8,128)S(1)}, f32[128,256]{1,0:T(8,128)S(1)}, u32[]{:S(2)}, u32[]{:S(2)}) collective-permute-start(f32[128,256]{1,0:T(8,128)S(1)} %get-tuple-element.36), channel_id=1, source_target_pairs={{0,1},{1,0},{2,3},{3,2},{4,5},{5,4},{6,7},{7,6},{8,9},{9,8},{10,11... | collective-permute-start | bytes 393224 | tf_op jit(solution)/shard_map/ppermute | solution.py:232
  32.3 0.1 collective-permute-start.13
  32.4 1.6 %collective-permute-done.10.far_ref = f32[128,256]{1,0:T(8,128)S(1)} collective-permute-done((f32[128,256]{1,0:T(8,128)S(1)}, f32[128,256]{1,0:T(8,128)S(1)}, u32[]{:S(2)}, u32[]{:S(2)}) %collective-permute-start.10) | collective-permute-done | bytes 131104 | tf_op jit(solution)/shard_map/ppermute | solution.py:228
  34.0 0.0 collective-permute-start.14
  34.0 0.0 collective-permute-done.12.refs_1_
  34.0 0.0 collective-permute-done.11.refs_0_
  34.0 1.4 %shard_map.66 = (f32[1024,256]{1,0:T(8,128)S(1)}, f32[1024,256]{1,0:T(8,128)S(1)}) custom-call(f32[1024,256]{1,0:T(8,128)S(1)} %get-tuple-element.35.own_ref, f32[512,512]{1,0:T(8,128)S(1)} %shard_map.56.first_ref, f32[512,512]{1,0:T(8,128)S(1)} %shard_map.57.last_ref, f32[3,1024,128]{2,1,0:T(8,128)S(1)} %copy-done.1, f32[1792,256]{1,0:T(8,128)S(1)} %copy-done, ...), custom_call_target="tpu_custom_call" | custom-call | tf_op jit(solution)/shard_map/pallas_call | solution.py:42
  35.4 0.0 collective-permute-done.13.w_ref
  35.4 0.0 collective-permute-done.14.far_ref
  35.4 1.8 %shard_map.67 = f32[1024,512]{1,0:T(8,128)} custom-call(f32[1024,256]{1,0:T(8,128)S(1)} %get-tuple-element.38.own_ref, f32[1024,256]{1,0:T(8,128)S(1)} %get-tuple-element.39.less_ref, f32[3,1024,128]{2,1,0:T(8,128)S(1)} %copy-done.1, f32[1792,256]{1,0:T(8,128)S(1)} %copy-done, f32[128,256]{1,0:T(8,128)S(1)} %collective-permute-done.13.w_ref, ...), custom_call_target="tpu_custom_call" | custom-call | tf_op jit(solution)/shard_map/pallas_call | solution.py:42
  (9 shorter events, 0.1 us)
Async XLA Ops:
  0.0 4.8 %copy-start.1 = (f32[3,1024,128]{2,1,0:T(8,128)S(1)}, f32[3,1024,128]{2,1,0:T(8,128)}, u32[]{:S(2)}) copy-start(f32[3,1024,128]{2,1,0:T(8,128)} %row_ref.9) | copy-start | bytes 4718596
  0.0 4.8 %copy-start.4 = (f32[3,1024,128]{2,1,0:T(8,128)S(1)}, f32[3,1024,128]{2,1,0:T(8,128)}, u32[]{:S(2)}) copy-start(f32[3,1024,128]{2,1,0:T(8,128)} %dual_ref.3) | copy-start | bytes 4718596
  0.0 5.8 %copy-start.2 = (f32[1024,1024]{1,0:T(8,128)S(1)}, f32[1024,1024]{1,0:T(8,128)}, u32[]{:S(2)}) copy-start(f32[1024,1024]{1,0:T(8,128)} %leaf_ref.3) | copy-start | bytes 12582916
  1.8 4.0 %copy-start.3 = (f32[1024,512]{1,0:T(8,128)S(1)}, f32[1024,512]{1,0:T(8,128)}, u32[]{:S(2)}) copy-start(f32[1024,512]{1,0:T(8,128)} %right_ref.1) | copy-start | bytes 6291460
  1.8 5.8 %collective-permute-start = (f32[128,128]{1,0:T(8,128)S(1)}, f32[128,128]{1,0:T(8,128)S(1)}, u32[]{:S(2)}, u32[]{:S(2)}) collective-permute-start(f32[128,128]{1,0:T(8,128)S(1)} %shard_map.55.last_ref), channel_id=1, source_target_pairs={{0,2},{2,0},{4,6},{6,4},{8,10},{10,8},{12,14},{14,12},{1,3},{3,1},... | collective-permute-start | bytes 196616 | tf_op jit(solution)/shard_map/ppermute | solution.py:228
  5.5 7.4 %collective-permute-start.2 = (f32[256,128]{1,0:T(8,128)S(1)}, f32[256,128]{1,0:T(8,128)S(1)}, u32[]{:S(2)}, u32[]{:S(2)}) collective-permute-start(f32[256,128]{1,0:T(8,128)S(1)} %shard_map.59.pairs_ref), channel_id=1, source_target_pairs={{0,2},{2,0},{4,6},{6,4},{8,10},{10,8},{12,14},{14,12},{1,3},{3,1},... | collective-permute-start | bytes 393224 | tf_op jit(solution)/shard_map/ppermute | solution.py:228
  7.7 5.2 %collective-permute-start.1 = (f32[128,128]{1,0:T(8,128)S(1)}, f32[128,128]{1,0:T(8,128)S(1)}, u32[]{:S(2)}, u32[]{:S(2)}) collective-permute-start(f32[128,128]{1,0:T(8,128)S(1)} %add.12), channel_id=1, source_target_pairs={{0,4},{2,6},{4,0},{6,2},{8,12},{10,14},{12,8},{14,10},{1,5},{3,7},... | collective-permute-start | bytes 196616 | tf_op jit(solution)/shard_map/ppermute | solution.py:228
  11.4 1.6 %copy-start = (f32[1792,256]{1,0:T(8,128)S(1)}, f32[1792,256]{1,0:T(8,128)}, u32[]{:S(2)}) copy-start(f32[1792,256]{1,0:T(8,128)} %cores_ref.9) | copy-start | bytes 5505028
  12.8 2.1 %collective-permute-start.3 = (f32[384,256]{1,0:T(8,128)S(1)}, f32[384,256]{1,0:T(8,128)S(1)}, u32[]{:S(2)}, u32[]{:S(2)}) collective-permute-start(f32[384,256]{1,0:T(8,128)S(1)} %get-tuple-element.27), channel_id=1, source_target_pairs={{0,1},{1,0},{2,3},{3,2},{4,5},{5,4},{6,7},{7,6},{8,9},{9,8},{10,11... | collective-permute-start | bytes 1179656 | tf_op jit(solution)/shard_map/ppermute | solution.py:232
  13.3 1.6 %collective-permute-start.4 = (f32[384,128]{1,0:T(8,128)S(1)}, f32[384,128]{1,0:T(8,128)S(1)}, u32[]{:S(2)}, u32[]{:S(2)}) collective-permute-start(f32[384,128]{1,0:T(8,128)S(1)} %shard_map.60.fix_ref), channel_id=1, source_target_pairs={{0,1},{1,0},{2,3},{3,2},{4,5},{5,4},{6,7},{7,6},{8,9},{9,8},{10,11... | collective-permute-start | bytes 589832 | tf_op jit(solution)/shard_map/ppermute | solution.py:232
  15.4 5.0 %collective-permute-start.5 = (f32[128,256]{1,0:T(8,128)S(1)}, f32[128,256]{1,0:T(8,128)S(1)}, u32[]{:S(2)}, u32[]{:S(2)}) collective-permute-start(f32[128,256]{1,0:T(8,128)S(1)} %get-tuple-element.29.refs_0_), channel_id=1, source_target_pairs={{0,4},{1,3},{2,6},{3,1},{4,0},{5,7},{6,2},{7,5},{8,12},{9,11},{10,... | collective-permute-start | bytes 393224 | tf_op jit(solution)/shard_map/ppermute | solution.py:242
  16.4 6.3 %collective-permute-start.7 = (f32[128,256]{1,0:T(8,128)S(1)}, f32[128,256]{1,0:T(8,128)S(1)}, u32[]{:S(2)}, u32[]{:S(2)}) collective-permute-start(f32[128,256]{1,0:T(8,128)S(1)} %shard_map.63), channel_id=1, source_target_pairs={{0,2},{2,0},{4,6},{6,4},{8,10},{10,8},{12,14},{14,12},{1,3},{3,1},... | collective-permute-start | bytes 393224 | tf_op jit(solution)/shard_map/ppermute | solution.py:228
  20.5 5.1 %collective-permute-start.8 = (f32[128,256]{1,0:T(8,128)S(1)}, f32[128,256]{1,0:T(8,128)S(1)}, u32[]{:S(2)}, u32[]{:S(2)}) collective-permute-start(f32[128,256]{1,0:T(8,128)S(1)} %add.13.refs_0_), channel_id=1, source_target_pairs={{0,2},{1,5},{2,0},{3,7},{4,6},{5,1},{6,4},{7,3},{8,10},{9,13},{10,... | collective-permute-start | bytes 393224 | tf_op jit(solution)/shard_map/ppermute | solution.py:242
  22.8 7.0 %collective-permute-start.9 = (f32[128,256]{1,0:T(8,128)S(1)}, f32[128,256]{1,0:T(8,128)S(1)}, u32[]{:S(2)}, u32[]{:S(2)}) collective-permute-start(f32[128,256]{1,0:T(8,128)S(1)} %add.14.v_ref), channel_id=1, source_target_pairs={{0,4},{2,6},{4,0},{6,2},{8,12},{10,14},{12,8},{14,10},{1,5},{3,7},... | collective-permute-start | bytes 393224 | tf_op jit(solution)/shard_map/ppermute | solution.py:228
  23.9 5.8 %collective-permute-start.6 = (f32[128,256]{1,0:T(8,128)S(1)}, f32[128,256]{1,0:T(8,128)S(1)}, u32[]{:S(2)}, u32[]{:S(2)}) collective-permute-start(f32[128,256]{1,0:T(8,128)S(1)} %shard_map.62.q_ref), channel_id=1, source_target_pairs={{0,2},{2,0},{4,6},{6,4},{8,10},{10,8},{12,14},{14,12},{1,3},{3,1},... | collective-permute-start | bytes 393224 | tf_op jit(solution)/shard_map/ppermute | solution.py:228
  25.5 8.5 %collective-permute-start.10 = (f32[128,256]{1,0:T(8,128)S(1)}, f32[128,256]{1,0:T(8,128)S(1)}, u32[]{:S(2)}, u32[]{:S(2)}) collective-permute-start(f32[128,256]{1,0:T(8,128)S(1)} %add.15.w_ref), channel_id=1, source_target_pairs={{0,8},{2,10},{4,12},{6,14},{8,0},{10,2},{12,4},{14,6},{1,9},{3,11}... | collective-permute-start | bytes 393224 | tf_op jit(solution)/shard_map/ppermute | solution.py:228
  31.7 2.3 %collective-permute-start.12 = (f32[128,256]{1,0:T(8,128)S(1)}, f32[128,256]{1,0:T(8,128)S(1)}, u32[]{:S(2)}, u32[]{:S(2)}) collective-permute-start(f32[128,256]{1,0:T(8,128)S(1)} %get-tuple-element.37), channel_id=1, source_target_pairs={{0,1},{1,0},{2,3},{3,2},{4,5},{5,4},{6,7},{7,6},{8,9},{9,8},{10,11... | collective-permute-start | bytes 393224 | tf_op jit(solution)/shard_map/ppermute | solution.py:232
  31.8 2.2 %collective-permute-start.11 = (f32[128,256]{1,0:T(8,128)S(1)}, f32[128,256]{1,0:T(8,128)S(1)}, u32[]{:S(2)}, u32[]{:S(2)}) collective-permute-start(f32[128,256]{1,0:T(8,128)S(1)} %get-tuple-element.36), channel_id=1, source_target_pairs={{0,1},{1,0},{2,3},{3,2},{4,5},{5,4},{6,7},{7,6},{8,9},{9,8},{10,11... | collective-permute-start | bytes 393224 | tf_op jit(solution)/shard_map/ppermute | solution.py:232
  32.3 3.1 %collective-permute-start.13 = (f32[128,256]{1,0:T(8,128)S(1)}, f32[128,256]{1,0:T(8,128)S(1)}, u32[]{:S(2)}, u32[]{:S(2)}) collective-permute-start(f32[128,256]{1,0:T(8,128)S(1)} %add.15.w_ref), channel_id=1, source_target_pairs={{0,1},{1,0},{2,3},{3,2},{4,5},{5,4},{6,7},{7,6},{8,9},{9,8},{10,11... | collective-permute-start | bytes 393224 | tf_op jit(solution)/shard_map/ppermute | solution.py:232
  34.0 1.4 %collective-permute-start.14 = (f32[128,256]{1,0:T(8,128)S(1)}, f32[128,256]{1,0:T(8,128)S(1)}, u32[]{:S(2)}, u32[]{:S(2)}) collective-permute-start(f32[128,256]{1,0:T(8,128)S(1)} %collective-permute-done.10.far_ref), channel_id=1, source_target_pairs={{0,1},{1,0},{2,3},{3,2},{4,5},{5,4},{6,7},{7,6},{8,9},{9,8},{10,11... | collective-permute-start | bytes 393224 | tf_op jit(solution)/shard_map/ppermute | solution.py:232

commit v5 on v4

--- a/solution.py
+++ b/solution.py
@@ -98,7 +98,10 @@
         field_ref[i:i + step] = dot3(halves(leaf_ref[start + i:start + i + step]), right)
 
 
-def projections(rest, dual_ref, first_ref, last_ref, keep_ref, send_ref, high_ref, low_ref):
+def projections(
+    rest, leaf_ref, right_ref, dual_ref, first_ref, last_ref, keep_ref, send_ref, high_ref, low_ref
+):
+    leaf_rows(first_ref.shape[0], leaf_ref, right_ref, last_ref)
     levels, rows, rank = dual_ref.shape
     for l in range(levels):
         high, low = halves(dual_ref[l].T)
@@ -115,29 +118,37 @@
         )
 
 
-def corrections(rest, pairs_ref, pairs_x_ref, last_ref, last_x_ref, last_z_ref, cores_ref, out_ref):
+def pair_corrections(rest, pairs_ref, pairs_x_ref, cores_ref, out_ref):
+    rank = pairs_ref.shape[1]
+    child, _ = place(rest)
+    cols = block(child & 1, rank)
+    out_ref[...] = dot(pairs_ref[...], cores_ref[block(6 + child, rank), cols]) + dot(
+        pairs_x_ref[...], cores_ref[block(6 + (child ^ 1), rank), cols]
+    )
+
+
+def last_corrections(rest, last_ref, last_x_ref, last_z_ref, cores_ref, out_ref):
     rank = last_ref.shape[0]
     child, _ = place(rest)
     pair = lax.shift_right_logical(child, 1)
-    slot3, slot2 = child & 1, pair & 1
-    own = cores_ref[block(6 + child, rank), block(slot3, rank)]
-    other = cores_ref[block(6 + (child ^ 1), rank), block(slot3, rank)]
-    out_ref[:2 * rank] = dot(pairs_ref[...], own) + dot(pairs_x_ref[...], other)
-    own = cores_ref[block(2 + pair, rank), block(slot2, rank)]
-    other = cores_ref[block(2 + (pair ^ 1), rank), block(slot2, rank)]
-    out_ref[2 * rank:] = dot(last_ref[...] + last_x_ref[...], own) + dot(last_z_ref[...], other)
+    cols = block(pair & 1, rank)
+    out_ref[...] = dot(
+        last_ref[...] + last_x_ref[...], cores_ref[block(2 + pair, rank), cols]
+    ) + dot(last_z_ref[...], cores_ref[block(2 + (pair ^ 1), rank), cols])
 
 
 def corrected(keep_ref, recv_ref, fix_ref, fix_other_ref, w_ref, v_ref, q_ref):
     rank = v_ref.shape[0]
     q = keep_ref[...] + recv_ref[...]
-    fix = fix_ref[...] + fix_other_ref[...]
     q1, q2, q3 = q[:rank], q[rank:2 * rank], q[2 * rank:]
-    both = dot(fix[:2 * rank], q3)
-    v = q2 - both[:rank]
-    w_ref[...] = q1 - both[rank:] - dot(fix[2 * rank:], v)
-    v_ref[...] = v
+    both = dot(fix_ref[...] + fix_other_ref[...], q3)
+    v_ref[...] = q2 - both[:rank]
+    w_ref[...] = q1 - both[rank:]
     q_ref[...] = q3
+
+
+def corrected_top(w_ref, v_ref, fix_ref, fix_other_ref, out_ref):
+    out_ref[...] = w_ref[...] - dot(fix_ref[...] + fix_other_ref[...], v_ref[...])
 
 
 def coefficient(level, child, cores_ref, own, other):
@@ -147,6 +158,14 @@
     return dot(cores_ref[rows, block(slot, rank)], own) + dot(
         cores_ref[rows, block(1 - slot, rank)], other
     )
+
+
+def top_matrix(rest, row_ref, cores_ref, out_ref):
+    rank = row_ref.shape[2]
+    child, _ = place(rest)
+    both = dot(row_ref[0], cores_ref[block(lax.shift_right_logical(child, 2), rank)])
+    out_ref[0] = both[:, :rank]
+    out_ref[1] = both[:, rank:]
 
 
 def lower_two(rest, v_ref, vz_ref, cores_ref, first_ref, last_ref, row_ref, k_ref, out_ref):
@@ -160,51 +179,39 @@
     out_ref[cut:] = last_ref[:, cols] - term[cut:]
 
 
-def lower_three(rest, q_ref, qx_ref, cores_ref, field_ref, row_ref, k_ref, out_ref):
+def lower_three(rest, q_ref, qx_ref, cores_ref, field_ref, row_ref, top_ref, w_ref, k_ref, out_ref):
     child, _ = place(rest)
+    side = lax.shift_right_logical(child, 2)
     k = coefficient(3, child, cores_ref, q_ref[...], qx_ref[...])
     k_ref[...] = k
-    out_ref[...] = field_ref[...] - dot(row_ref[2], k)
-
-
-def lower_update(index, first_ref, last_ref, row_ref, k, out_ref):
-    cols = block(index, k.shape[1])
+    lefts = jnp.concatenate([row_ref[2], top_ref[side]], 1)
+    out_ref[...] = field_ref[...] - dot(lefts, jnp.concatenate([k, w_ref[...]], 0))
+
+
+def solve_own(rest, own_ref, first_ref, last_ref, row_ref, top_ref, far_ref, w_ref, *refs):
+    *k_refs, out_ref, other_ref = refs
+    child, core = place(rest)
+    side = lax.shift_right_logical(child, 2)
+    out_ref[...] = own_ref[...] - dot(top_ref[1 - side], far_ref[...])
+    cols = block(1 - core, w_ref.shape[1])
     cut = first_ref.shape[0]
-    lefts = jnp.concatenate([row_ref[1], row_ref[2]], 1)
-    term = dot(lefts, k)
-    out_ref[:cut] = first_ref[:, cols] - term[:cut]
-    out_ref[cut:] = last_ref[:, cols] - term[cut:]
-
-
-def top_coefficient(rest, w_ref, far_ref, cores_ref):
-    rank = w_ref.shape[0]
-    child, _ = place(rest)
-    slot1 = lax.shift_right_logical(child, 2)
-    rows1 = block(slot1, rank)
-    return dot(cores_ref[rows1, block(slot1, rank)], w_ref[...]) + dot(
-        cores_ref[rows1, block(1 - slot1, rank)], far_ref[...]
-    )
-
-
-def solve_own(rest, own_ref, first_ref, last_ref, row_ref, cores_ref, w_ref, far_ref, *refs):
-    *k_refs, out_ref, other_ref = refs
-    _, core = place(rest)
-    out_ref[...] = own_ref[...] - dot(row_ref[0], top_coefficient(rest, w_ref, far_ref, cores_ref))
-    k = jnp.concatenate([ref[...] for ref in k_refs], 0)
-    lower_update(1 - core, first_ref, last_ref, row_ref, k, other_ref)
-
-
-def solve_other(rest, pieces, own_ref, less_ref, row_ref, cores_ref, w_ref, far_ref, out_ref, other_ref, sems):
-    _, core = place(rest)
+    lefts = jnp.concatenate([row_ref[1], row_ref[2], top_ref[side]], 1)
+    term = dot(lefts, jnp.concatenate([ref[...] for ref in (*k_refs, w_ref)], 0))
+    other_ref[:cut] = first_ref[:, cols] - term[:cut]
+    other_ref[cut:] = last_ref[:, cols] - term[cut:]
+
+
+def solve_other(rest, pieces, own_ref, less_ref, top_ref, far_ref, out_ref, other_ref, sems):
+    child, core = place(rest)
+    side = lax.shift_right_logical(child, 2)
     total, half = own_ref.shape
     mine, theirs = block(core, half), block(1 - core, half)
     copies = [pltpu.make_async_copy(own_ref, out_ref.at[:, mine], sems.at[pieces])]
     copies[0].start()
-    top = top_coefficient(rest, w_ref, far_ref, cores_ref)
     step = total // pieces
     for i in range(pieces):
         part = slice(i * step, (i + 1) * step)
-        other_ref[part] = less_ref[part] - dot(row_ref[0, part], top)
+        other_ref[part] = less_ref[part] - dot(top_ref[1 - side, part], far_ref[...])
         copy = pltpu.make_async_copy(other_ref.at[part], out_ref.at[part, theirs], sems.at[i])
         copy.start()
         copies.append(copy)
@@ -232,14 +239,18 @@
     return lax.ppermute(x, "narrow", [(0, 1), (1, 0)])
 
 
-def swap_crossed(x, first, second):
+def swap_crossed(x, first, second, other_core=False):
     wides, cores = lax.axis_size("wide"), lax.axis_size("narrow")
     route = []
     for w in range(wides):
         for n in range(cores):
             bit = first if n == 0 else second
-            route.append((w * cores + n, (w ^ (1 << bit)) * cores + n))
+            route.append((w * cores + n, (w ^ (1 << bit)) * cores + (n ^ other_core)))
     return lax.ppermute(x, ("wide", "narrow"), route)
+
+
+def swap_diagonal(x, bit):
+    return swap_crossed(x, bit, bit, True)
 
 
 def shards(right_side, leaf_inverse, row_bases, dual_bases, woodbury_cores):
@@ -262,28 +273,30 @@
     )
     for bit in range(rest):
         pairs, last = pairs + swap_wide(pairs, bit), last + swap_wide(last, bit)
-    last_x, pairs_x = swap_wide(last, bit3), swap_wide(pairs, bit3)
+    last_x, pairs_x = swap_diagonal(last, bit3), swap_diagonal(pairs, bit3)
 
     first_rows = call(
         functools.partial(leaf_rows, 0), shape(cut, cols), (leaf_inverse, after(right_side, last)),
         6 * cut * rows * cols,
     )
-    last_z = swap_wide(last + last_x, bit2)
-    last_rows = call(
-        functools.partial(leaf_rows, cut), shape(rows - cut, cols), (leaf_inverse, after(right_side, last_x)),
-        6 * (rows - cut) * rows * cols,
-    )
-    keep, send = call(
-        functools.partial(projections, rest), (shape(levels * rank, half),) * 2,
-        (dual_bases, first_rows, last_rows), 6 * levels * rank * rows * cols,
+    last_z = swap_diagonal(last + after(last_x, first_rows), bit2)
+    last_rows, keep, send = call(
+        functools.partial(projections, rest),
+        (shape(rows - cut, cols),) + (shape(levels * rank, half),) * 2,
+        (leaf_inverse, after(right_side, last_x), dual_bases, first_rows), 0,
         scratch=[pltpu.VMEM((levels * rank, rows), BF16)] * 2,
     )
-    recv = swap_narrow(after(send, last_z, pairs_x))
     fix = call(
-        functools.partial(corrections, rest), shape(levels * rank, rank),
-        (pairs, pairs_x, last, last_x, last_z, woodbury_cores), 36 * rank**3,
-    )
-    fix_other = swap_narrow(fix)
+        functools.partial(pair_corrections, rest), shape(2 * rank, rank),
+        (pairs, pairs_x, woodbury_cores), 0,
+    )
+    recv = swap_narrow(after(send, last_z, fix))
+    fix_other = swap_narrow(after(fix, last_z))
+    fix_top = call(
+        functools.partial(last_corrections, rest), shape(rank, rank),
+        (last, last_x, last_z, woodbury_cores), 0,
+    )
+    fix_top_other = swap_narrow(after(fix_top, fix))
     if rest:
         keep = keep + recv
         for bit in range(rest):
@@ -292,10 +305,15 @@
     w, v, q = call(
         corrected, (shape(rank, half),) * 3, (keep, recv, fix, fix_other), 18 * rank * rank * half
     )
+    w = call(corrected_top, shape(rank, half), (w, v, fix_top, fix_top_other), 0)
 
     v = tie(v, w)
     v_x = swap_wide(v, bit3)
-    w = w_mid = w + swap_crossed(w, bit2, bit3)
+    top = call(
+        functools.partial(top_matrix, rest), shape(2, rows, rank),
+        (row_bases, after(woodbury_cores, w)), 0,
+    )
+    w = w_mid = w + after(swap_crossed(w, bit2, bit3), top)
     q = tie(q, w_mid)
     q_x = swap_wide(q, bit3)
     v = v + after(v_x, w_mid)
@@ -308,19 +326,19 @@
     )
     k3, lower = call(
         functools.partial(lower_three, rest), (shape(rank, half), shape(rows, half)),
-        (q, q_x, woodbury_cores, lower, row_bases), 0,
+        (q, q_x, woodbury_cores, lower, row_bases, top, w), 0,
     )
     k_other = [swap_narrow(k2), swap_narrow(k3)]
-    w_other = swap_narrow(after(w, v_z, q_x))
+    w_other = swap_narrow(after(w, k2))
     far_other = swap_narrow(far)
     own, less = call(
         functools.partial(solve_own, rest), (shape(rows, half),) * 2,
-        (lower, first_rows, last_rows, row_bases, woodbury_cores, w, far, *k_other), 0,
+        (lower, first_rows, last_rows, row_bases, top, far, w_other, *k_other), 0,
     )
     pieces = 4
     return call(
         functools.partial(solve_other, rest, pieces), shape(rows, cols),
-        (own, less, row_bases, woodbury_cores, w_other, far_other), 0,
+        (own, less, top, far_other), 0,
         scratch=[pltpu.VMEM((rows, half), F32), pltpu.SemaphoreType.DMA((pieces + 1,))],
         out_specs=pl.BlockSpec(memory_space=pltpu.HBM),
     )

time: 37.4 us -> 36.5 us (0.976)
  starting transfers between devices: 16.8 us -> 15.7 us
    ppermute x7 -> x4, starting transfers between devices: 12.6 us -> 6.65 us  [swap_wide(): return lax.ppermute(x, 'wide', [(w, w ^ 1 << bit) for w in range(count)])]
    ppermute x2 -> x5, starting transfers between devices: 2.93 us -> 7.29 us  [swap_crossed(): return lax.ppermute(x, ('wide', 'narrow'), route)]
    ppermute x6 -> x7, starting transfers between devices: 1.26 us -> 1.73 us  [swap_narrow(): return lax.ppermute(x, 'narrow', [(0, 1), (1, 0)])]
    ppermute x2 -> x5, waiting for transfers between devices: 2.09 us -> 2.5 us  [swap_crossed(): return lax.ppermute(x, ('wide', 'narrow'), route)]
    ppermute x6 -> x7, waiting for transfers between devices: 1.12 us -> 0.76 us  [swap_narrow(): return lax.ppermute(x, 'narrow', [(0, 1), (1, 0)])]
    pallas_call x13 -> x15, Pallas kernels: 13.4 us -> 13.7 us  [call(): pl.pallas_call(body, in_specs=in_specs or [VMEM] * len(args), out_specs=j...]
    ppermute x7 -> x4, waiting for transfers between devices: 3.5 us -> 3.32 us  [swap_wide(): return lax.ppermute(x, 'wide', [(w, w ^ 1 << bit) for w in range(count)])]
  transfers between devices with their start and end apart: 15 -> 16, of which waited for: 5 -> 6; matrix products, arithmetic and copies ran while one was open for 0% -> 0% of each run, Pallas kernels for 25% -> 28%
where the time goes in v5:
time: 36.5 us; the launch traced here: 36.3 us
  starting transfers between devices  15.7 us (43%)
  Pallas kernels  13.7 us (38%)
  waiting for transfers between devices  6.58 us (18%)
    pallas_call x15, Pallas kernels, call(): pl.pallas_call(body, in_specs=in_specs or [VMEM] * len(args), out_specs=j...  13.7 us
    ppermute x5, starting transfers between devices, swap_crossed(): return lax.ppermute(x, ('wide', 'narrow'), route)  7.29 us
    ppermute x4, starting transfers between devices, swap_wide(): return lax.ppermute(x, 'wide', [(w, w ^ 1 << bit) for w in range(count)])  6.65 us
    ppermute x4, waiting for transfers between devices, swap_wide(): return lax.ppermute(x, 'wide', [(w, w ^ 1 << bit) for w in range(count)])  3.32 us
    ppermute x5, waiting for transfers between devices, swap_crossed(): return lax.ppermute(x, ('wide', 'narrow'), route)  2.5 us
    ppermute x7, starting transfers between devices, swap_narrow(): return lax.ppermute(x, 'narrow', [(0, 1), (1, 0)])  1.73 us
    ppermute x7, waiting for transfers between devices, swap_narrow(): return lax.ppermute(x, 'narrow', [(0, 1), (1, 0)])  0.76 us
  transfers between devices with their start and end apart: 16, of which 6 were waited for; matrix products, arithmetic and copies ran while one was open for 0% of the time, Pallas kernels for 28%

profile of v5, /device:TPU:0, one launch (start us, length us, event | category | flops | bytes accessed | tf_op | source)
XLA Modules:
  0.0 36.3 jit_solution(15754572311970214772)
XLA Ops:
  0.0 1.8 %shard_map.55.last_ref = f32[128,128]{1,0:T(8,128)S(1)} custom-call(f32[3,1024,128]{2,1,0:T(8,128)} %dual_ref.3, f32[3,1024,128]{2,1,0:T(8,128)} %row_ref.9), custom_call_target="tpu_custom_call" | custom-call | flops 16106127360 | tf_op jit(solution)/shard_map/pallas_call | solution.py:42
  1.8 0.0 copy-start.3
  1.8 2.4 %collective-permute-start = (f32[128,128]{1,0:T(8,128)S(1)}, f32[128,128]{1,0:T(8,128)S(1)}, u32[]{:S(2)}, u32[]{:S(2)}) collective-permute-start(f32[128,128]{1,0:T(8,128)S(1)} %shard_map.55.last_ref), channel_id=1, source_target_pairs={{0,3},{1,2},{2,1},{3,0},{4,7},{5,6},{6,5},{7,4},{8,11},{9,10},{10,... | collective-permute-start | bytes 196616 | tf_op jit(solution)/shard_map/ppermute | solution.py:249
  4.3 0.0 copy-done.1
  4.3 0.6 %shard_map.58.pairs_ref = f32[256,128]{1,0:T(8,128)S(1)} custom-call(f32[3,1024,128]{2,1,0:T(8,128)S(1)} %copy-done.4, f32[3,1024,128]{2,1,0:T(8,128)S(1)} %copy-done.1, f32[128,128]{1,0:T(8,128)S(1)} %shard_map.55.last_ref), custom_call_target="tpu_custom_call" | custom-call | flops 67108864 | tf_op jit(solution)/shard_map/pallas_call | solution.py:42
  4.9 0.4 %collective-permute-start.2 = (f32[256,128]{1,0:T(8,128)S(1)}, f32[256,128]{1,0:T(8,128)S(1)}, u32[]{:S(2)}, u32[]{:S(2)}) collective-permute-start(f32[256,128]{1,0:T(8,128)S(1)} %shard_map.58.pairs_ref), channel_id=1, source_target_pairs={{0,3},{1,2},{2,1},{3,0},{4,7},{5,6},{6,5},{7,4},{8,11},{9,10},{10,... | collective-permute-start | bytes 393224 | tf_op jit(solution)/shard_map/ppermute | solution.py:249
  5.3 1.8 %shard_map.56.first_ref = f32[512,512]{1,0:T(8,128)S(1)} custom-call(f32[1024,1024]{1,0:T(8,128)S(1)} %copy-done.2, f32[1024,512]{1,0:T(8,128)S(1)} %copy-done.3), custom_call_target="tpu_custom_call" | custom-call | flops 1610612736 | tf_op jit(solution)/shard_map/pallas_call | solution.py:42
  7.1 0.0 collective-permute-done.last_x_ref
  7.1 0.0 copy-start
  7.1 1.9 %collective-permute-start.1 = (f32[128,128]{1,0:T(8,128)S(1)}, f32[128,128]{1,0:T(8,128)S(1)}, u32[]{:S(2)}, u32[]{:S(2)}) collective-permute-start(f32[128,128]{1,0:T(8,128)S(1)} %add.12), channel_id=1, source_target_pairs={{0,5},{1,4},{2,7},{3,6},{4,1},{5,0},{6,3},{7,2},{8,13},{9,12},{10,... | collective-permute-start | bytes 196616 | tf_op jit(solution)/shard_map/ppermute | solution.py:249
  9.1 3.1 %shard_map.57 = (f32[512,512]{1,0:T(8,128)S(1)}, f32[384,256]{1,0:T(8,128)S(1)}, f32[384,256]{1,0:T(8,128)S(1)}) custom-call(f32[1024,1024]{1,0:T(8,128)S(1)} %copy-done.2, f32[1024,512]{1,0:T(8,128)S(1)} %copy-done.3, f32[3,1024,128]{2,1,0:T(8,128)S(1)} %copy-done.4, f32[512,512]{1,0:T(8,128)S(1)} %shard_map.56.first_ref), custom_call_target="tpu_custom_call" | custom-call | tf_op jit(solution)/shard_map/pallas_call | solution.py:42
  12.2 0.0 collective-permute-done.2.pairs_x_ref
  12.2 0.3 shard_map.59.fix_ref
  12.4 0.0 collective-permute-done.1.last_z_ref
  12.5 0.4 %collective-permute-start.3 = (f32[384,256]{1,0:T(8,128)S(1)}, f32[384,256]{1,0:T(8,128)S(1)}, u32[]{:S(2)}, u32[]{:S(2)}) collective-permute-start(f32[384,256]{1,0:T(8,128)S(1)} %get-tuple-element.34), channel_id=1, source_target_pairs={{0,1},{1,0},{2,3},{3,2},{4,5},{5,4},{6,7},{7,6},{8,9},{9,8},{10,11... | collective-permute-start | bytes 1179656 | tf_op jit(solution)/shard_map/ppermute | solution.py:239
  12.9 0.1 collective-permute-start.4
  13.0 0.2 shard_map.61.fix_ref
  13.3 0.4 %collective-permute-start.5 = (f32[128,128]{1,0:T(8,128)S(1)}, f32[128,128]{1,0:T(8,128)S(1)}, u32[]{:S(2)}, u32[]{:S(2)}) collective-permute-start(f32[128,128]{1,0:T(8,128)S(1)} %shard_map.61.fix_ref), channel_id=1, source_target_pairs={{0,1},{1,0},{2,3},{3,2},{4,5},{5,4},{6,7},{7,6},{8,9},{9,8},{10,11... | collective-permute-start | bytes 196616 | tf_op jit(solution)/shard_map/ppermute | solution.py:239
  13.7 0.7 %collective-permute-done.4.fix_other_ref = f32[256,128]{1,0:T(8,128)S(1)} collective-permute-done((f32[256,128]{1,0:T(8,128)S(1)}, f32[256,128]{1,0:T(8,128)S(1)}, u32[]{:S(2)}, u32[]{:S(2)}) %collective-permute-start.4) | collective-permute-done | bytes 131104 | tf_op jit(solution)/shard_map/ppermute | solution.py:239
  14.4 0.0 collective-permute-done.3.recv_ref
  14.4 0.3 shard_map.60
  14.7 0.0 collective-permute-done.5.fix_other_ref
  14.7 0.2 shard_map.62.refs_0_
  14.9 0.9 %collective-permute-start.6 = (f32[128,256]{1,0:T(8,128)S(1)}, f32[128,256]{1,0:T(8,128)S(1)}, u32[]{:S(2)}, u32[]{:S(2)}) collective-permute-start(f32[128,256]{1,0:T(8,128)S(1)} %shard_map.62.refs_0_), channel_id=1, source_target_pairs={{0,4},{1,3},{2,6},{3,1},{4,0},{5,7},{6,2},{7,5},{8,12},{9,11},{10,... | collective-permute-start | bytes 393224 | tf_op jit(solution)/shard_map/ppermute | solution.py:249
  15.9 1.6 %collective-permute-start.8 = (f32[128,256]{1,0:T(8,128)S(1)}, f32[128,256]{1,0:T(8,128)S(1)}, u32[]{:S(2)}, u32[]{:S(2)}) collective-permute-start(f32[128,256]{1,0:T(8,128)S(1)} %shard_map.65), channel_id=1, source_target_pairs={{0,2},{2,0},{4,6},{6,4},{8,10},{10,8},{12,14},{14,12},{1,3},{3,1},... | collective-permute-start | bytes 393224 | tf_op jit(solution)/shard_map/ppermute | solution.py:235
  17.5 0.6 %shard_map.63.top_ref = f32[2,1024,128]{2,1,0:T(8,128)S(1)} custom-call(f32[3,1024,128]{2,1,0:T(8,128)S(1)} %copy-done.1, f32[1792,256]{1,0:T(8,128)S(1)} %copy-done), custom_call_target="tpu_custom_call" | custom-call | tf_op jit(solution)/shard_map/pallas_call | solution.py:42
  18.1 1.9 %collective-permute-done.6 = f32[128,256]{1,0:T(8,128)S(1)} collective-permute-done((f32[128,256]{1,0:T(8,128)S(1)}, f32[128,256]{1,0:T(8,128)S(1)}, u32[]{:S(2)}, u32[]{:S(2)}) %collective-permute-start.6) | collective-permute-done | bytes 131104 | tf_op jit(solution)/shard_map/ppermute | solution.py:249
  20.0 1.6 %collective-permute-start.9 = (f32[128,256]{1,0:T(8,128)S(1)}, f32[128,256]{1,0:T(8,128)S(1)}, u32[]{:S(2)}, u32[]{:S(2)}) collective-permute-start(f32[128,256]{1,0:T(8,128)S(1)} %add.13.refs_0_), channel_id=1, source_target_pairs={{0,2},{1,5},{2,0},{3,7},{4,6},{5,1},{6,4},{7,3},{8,10},{9,13},{10,... | collective-permute-start | bytes 393224 | tf_op jit(solution)/shard_map/ppermute | solution.py:249
  21.6 0.6 %collective-permute-done.8 = f32[128,256]{1,0:T(8,128)S(1)} collective-permute-done((f32[128,256]{1,0:T(8,128)S(1)}, f32[128,256]{1,0:T(8,128)S(1)}, u32[]{:S(2)}, u32[]{:S(2)}) %collective-permute-start.8) | collective-permute-done | bytes 131104 | tf_op jit(solution)/shard_map/ppermute | solution.py:235
  22.2 0.7 %collective-permute-start.10 = (f32[128,256]{1,0:T(8,128)S(1)}, f32[128,256]{1,0:T(8,128)S(1)}, u32[]{:S(2)}, u32[]{:S(2)}) collective-permute-start(f32[128,256]{1,0:T(8,128)S(1)} %add.14.v_ref), channel_id=1, source_target_pairs={{0,4},{2,6},{4,0},{6,2},{8,12},{10,14},{12,8},{14,10},{1,5},{3,7},... | collective-permute-start | bytes 393224 | tf_op jit(solution)/shard_map/ppermute | solution.py:235
  22.9 1.6 %collective-permute-start.7 = (f32[128,256]{1,0:T(8,128)S(1)}, f32[128,256]{1,0:T(8,128)S(1)}, u32[]{:S(2)}, u32[]{:S(2)}) collective-permute-start(f32[128,256]{1,0:T(8,128)S(1)} %shard_map.64.q_ref), channel_id=1, source_target_pairs={{0,2},{2,0},{4,6},{6,4},{8,10},{10,8},{12,14},{14,12},{1,3},{3,1},... | collective-permute-start | bytes 393224 | tf_op jit(solution)/shard_map/ppermute | solution.py:235
  24.6 0.6 %collective-permute-done.9 = f32[128,256]{1,0:T(8,128)S(1)} collective-permute-done((f32[128,256]{1,0:T(8,128)S(1)}, f32[128,256]{1,0:T(8,128)S(1)}, u32[]{:S(2)}, u32[]{:S(2)}) %collective-permute-start.9) | collective-permute-done | bytes 131104 | tf_op jit(solution)/shard_map/ppermute | solution.py:249
  25.2 2.7 %collective-permute-start.11 = (f32[128,256]{1,0:T(8,128)S(1)}, f32[128,256]{1,0:T(8,128)S(1)}, u32[]{:S(2)}, u32[]{:S(2)}) collective-permute-start(f32[128,256]{1,0:T(8,128)S(1)} %add.15.w_ref), channel_id=1, source_target_pairs={{0,8},{2,10},{4,12},{6,14},{8,0},{10,2},{12,4},{14,6},{1,9},{3,11}... | collective-permute-start | bytes 393224 | tf_op jit(solution)/shard_map/ppermute | solution.py:235
  27.9 1.1 %collective-permute-done.10.vz_ref = f32[128,256]{1,0:T(8,128)S(1)} collective-permute-done((f32[128,256]{1,0:T(8,128)S(1)}, f32[128,256]{1,0:T(8,128)S(1)}, u32[]{:S(2)}, u32[]{:S(2)}) %collective-permute-start.10) | collective-permute-done | bytes 131104 | tf_op jit(solution)/shard_map/ppermute | solution.py:235
  29.0 1.0 %shard_map.66 = (f32[128,256]{1,0:T(8,128)S(1)}, f32[1024,256]{1,0:T(8,128)S(1)}) custom-call(f32[128,256]{1,0:T(8,128)S(1)} %add.14.v_ref, f32[128,256]{1,0:T(8,128)S(1)} %collective-permute-done.10.vz_ref, f32[1792,256]{1,0:T(8,128)S(1)} %copy-done, f32[512,512]{1,0:T(8,128)S(1)} %shard_map.56.first_ref, f32[512,512]{1,0:T(8,128)S(1)} %get-tuple-element.45.last_ref, ...), custom_call_target="tpu_custom_call" | custom-call | tf_op jit(solution)/shard_map/pallas_call | solution.py:42
  30.0 0.1 collective-permute-start.12
  30.0 0.0 collective-permute-done.7.qx_ref
  30.1 1.0 %shard_map.67 = (f32[128,256]{1,0:T(8,128)S(1)}, f32[1024,256]{1,0:T(8,128)S(1)}) custom-call(f32[128,256]{1,0:T(8,128)S(1)} %shard_map.64.q_ref, f32[128,256]{1,0:T(8,128)S(1)} %collective-permute-done.7.qx_ref, f32[1792,256]{1,0:T(8,128)S(1)} %copy-done, f32[1024,256]{1,0:T(8,128)S(1)} %get-tuple-element.46.field_ref, f32[3,1024,128]{2,1,0:T(8,128)S(1)} %copy-done.1, ...), custom_call_target="tpu_custom_call" | custom-call | tf_op jit(solution)/shard_map/pallas_call | solution.py:42
  31.1 0.6 %collective-permute-start.14 = (f32[128,256]{1,0:T(8,128)S(1)}, f32[128,256]{1,0:T(8,128)S(1)}, u32[]{:S(2)}, u32[]{:S(2)}) collective-permute-start(f32[128,256]{1,0:T(8,128)S(1)} %get-tuple-element.50), channel_id=1, source_target_pairs={{0,1},{1,0},{2,3},{3,2},{4,5},{5,4},{6,7},{7,6},{8,9},{9,8},{10,11... | collective-permute-start | bytes 393224 | tf_op jit(solution)/shard_map/ppermute | solution.py:239
  31.6 0.1 collective-permute-start.13
  31.7 1.6 %collective-permute-done.11.far_ref = f32[128,256]{1,0:T(8,128)S(1)} collective-permute-done((f32[128,256]{1,0:T(8,128)S(1)}, f32[128,256]{1,0:T(8,128)S(1)}, u32[]{:S(2)}, u32[]{:S(2)}) %collective-permute-start.11) | collective-permute-done | bytes 131104 | tf_op jit(solution)/shard_map/ppermute | solution.py:235
  33.3 0.0 collective-permute-start.15
  33.3 0.0 collective-permute-done.12.w_ref
  33.3 0.0 collective-permute-done.14.refs_1_
  33.3 0.0 collective-permute-done.13.refs_0_
  33.3 1.4 %shard_map.68 = (f32[1024,256]{1,0:T(8,128)S(1)}, f32[1024,256]{1,0:T(8,128)S(1)}) custom-call(f32[1024,256]{1,0:T(8,128)S(1)} %get-tuple-element.47.own_ref, f32[512,512]{1,0:T(8,128)S(1)} %shard_map.56.first_ref, f32[512,512]{1,0:T(8,128)S(1)} %get-tuple-element.45.last_ref, f32[3,1024,128]{2,1,0:T(8,128)S(1)} %copy-done.1, ...), custom_call_target="tpu_custom_call" | custom-call | tf_op jit(solution)/shard_map/pallas_call | solution.py:42
  34.7 0.0 collective-permute-done.15.far_ref
  34.8 1.5 %shard_map.69 = f32[1024,512]{1,0:T(8,128)} custom-call(f32[1024,256]{1,0:T(8,128)S(1)} %get-tuple-element.51.own_ref, f32[1024,256]{1,0:T(8,128)S(1)} %get-tuple-element.52.less_ref, f32[2,1024,128]{2,1,0:T(8,128)S(1)} %shard_map.63.top_ref, f32[128,256]{1,0:T(8,128)S(1)} %collective-permute-done.15.far_ref), custom_call_target="tpu_custom_call" | custom-call | tf_op jit(solution)/shard_map/pallas_call | solution.py:42
  (13 shorter events, 0.1 us)
Async XLA Ops:
  0.0 4.3 %copy-start.1 = (f32[3,1024,128]{2,1,0:T(8,128)S(1)}, f32[3,1024,128]{2,1,0:T(8,128)}, u32[]{:S(2)}) copy-start(f32[3,1024,128]{2,1,0:T(8,128)} %row_ref.9) | copy-start | bytes 4718596
  0.0 4.3 %copy-start.4 = (f32[3,1024,128]{2,1,0:T(8,128)S(1)}, f32[3,1024,128]{2,1,0:T(8,128)}, u32[]{:S(2)}) copy-start(f32[3,1024,128]{2,1,0:T(8,128)} %dual_ref.3) | copy-start | bytes 4718596
  0.0 5.3 %copy-start.2 = (f32[1024,1024]{1,0:T(8,128)S(1)}, f32[1024,1024]{1,0:T(8,128)}, u32[]{:S(2)}) copy-start(f32[1024,1024]{1,0:T(8,128)} %leaf_ref.3) | copy-start | bytes 12582916
  1.8 3.5 %copy-start.3 = (f32[1024,512]{1,0:T(8,128)S(1)}, f32[1024,512]{1,0:T(8,128)}, u32[]{:S(2)}) copy-start(f32[1024,512]{1,0:T(8,128)} %right_ref.1) | copy-start | bytes 6291460
  1.8 5.3 %collective-permute-start = (f32[128,128]{1,0:T(8,128)S(1)}, f32[128,128]{1,0:T(8,128)S(1)}, u32[]{:S(2)}, u32[]{:S(2)}) collective-permute-start(f32[128,128]{1,0:T(8,128)S(1)} %shard_map.55.last_ref), channel_id=1, source_target_pairs={{0,3},{1,2},{2,1},{3,0},{4,7},{5,6},{6,5},{7,4},{8,11},{9,10},{10,... | collective-permute-start | bytes 196616 | tf_op jit(solution)/shard_map/ppermute | solution.py:249
  4.9 7.3 %collective-permute-start.2 = (f32[256,128]{1,0:T(8,128)S(1)}, f32[256,128]{1,0:T(8,128)S(1)}, u32[]{:S(2)}, u32[]{:S(2)}) collective-permute-start(f32[256,128]{1,0:T(8,128)S(1)} %shard_map.58.pairs_ref), channel_id=1, source_target_pairs={{0,3},{1,2},{2,1},{3,0},{4,7},{5,6},{6,5},{7,4},{8,11},{9,10},{10,... | collective-permute-start | bytes 393224 | tf_op jit(solution)/shard_map/ppermute | solution.py:249
  7.1 5.0 %copy-start = (f32[1792,256]{1,0:T(8,128)S(1)}, f32[1792,256]{1,0:T(8,128)}, u32[]{:S(2)}) copy-start(f32[1792,256]{1,0:T(8,128)} %cores_ref.8) | copy-start | bytes 5505028
  7.1 5.3 %collective-permute-start.1 = (f32[128,128]{1,0:T(8,128)S(1)}, f32[128,128]{1,0:T(8,128)S(1)}, u32[]{:S(2)}, u32[]{:S(2)}) collective-permute-start(f32[128,128]{1,0:T(8,128)S(1)} %add.12), channel_id=1, source_target_pairs={{0,5},{1,4},{2,7},{3,6},{4,1},{5,0},{6,3},{7,2},{8,13},{9,12},{10,... | collective-permute-start | bytes 196616 | tf_op jit(solution)/shard_map/ppermute | solution.py:249
  12.5 2.0 %collective-permute-start.3 = (f32[384,256]{1,0:T(8,128)S(1)}, f32[384,256]{1,0:T(8,128)S(1)}, u32[]{:S(2)}, u32[]{:S(2)}) collective-permute-start(f32[384,256]{1,0:T(8,128)S(1)} %get-tuple-element.34), channel_id=1, source_target_pairs={{0,1},{1,0},{2,3},{3,2},{4,5},{5,4},{6,7},{7,6},{8,9},{9,8},{10,11... | collective-permute-start | bytes 1179656 | tf_op jit(solution)/shard_map/ppermute | solution.py:239
  12.9 1.5 %collective-permute-start.4 = (f32[256,128]{1,0:T(8,128)S(1)}, f32[256,128]{1,0:T(8,128)S(1)}, u32[]{:S(2)}, u32[]{:S(2)}) collective-permute-start(f32[256,128]{1,0:T(8,128)S(1)} %shard_map.59.fix_ref), channel_id=1, source_target_pairs={{0,1},{1,0},{2,3},{3,2},{4,5},{5,4},{6,7},{7,6},{8,9},{9,8},{10,11... | collective-permute-start | bytes 393224 | tf_op jit(solution)/shard_map/ppermute | solution.py:239
  13.3 1.5 %collective-permute-start.5 = (f32[128,128]{1,0:T(8,128)S(1)}, f32[128,128]{1,0:T(8,128)S(1)}, u32[]{:S(2)}, u32[]{:S(2)}) collective-permute-start(f32[128,128]{1,0:T(8,128)S(1)} %shard_map.61.fix_ref), channel_id=1, source_target_pairs={{0,1},{1,0},{2,3},{3,2},{4,5},{5,4},{6,7},{7,6},{8,9},{9,8},{10,11... | collective-permute-start | bytes 196616 | tf_op jit(solution)/shard_map/ppermute | solution.py:239
  14.9 5.0 %collective-permute-start.6 = (f32[128,256]{1,0:T(8,128)S(1)}, f32[128,256]{1,0:T(8,128)S(1)}, u32[]{:S(2)}, u32[]{:S(2)}) collective-permute-start(f32[128,256]{1,0:T(8,128)S(1)} %shard_map.62.refs_0_), channel_id=1, source_target_pairs={{0,4},{1,3},{2,6},{3,1},{4,0},{5,7},{6,2},{7,5},{8,12},{9,11},{10,... | collective-permute-start | bytes 393224 | tf_op jit(solution)/shard_map/ppermute | solution.py:249
  15.9 6.3 %collective-permute-start.8 = (f32[128,256]{1,0:T(8,128)S(1)}, f32[128,256]{1,0:T(8,128)S(1)}, u32[]{:S(2)}, u32[]{:S(2)}) collective-permute-start(f32[128,256]{1,0:T(8,128)S(1)} %shard_map.65), channel_id=1, source_target_pairs={{0,2},{2,0},{4,6},{6,4},{8,10},{10,8},{12,14},{14,12},{1,3},{3,1},... | collective-permute-start | bytes 393224 | tf_op jit(solution)/shard_map/ppermute | solution.py:235
  20.0 5.2 %collective-permute-start.9 = (f32[128,256]{1,0:T(8,128)S(1)}, f32[128,256]{1,0:T(8,128)S(1)}, u32[]{:S(2)}, u32[]{:S(2)}) collective-permute-start(f32[128,256]{1,0:T(8,128)S(1)} %add.13.refs_0_), channel_id=1, source_target_pairs={{0,2},{1,5},{2,0},{3,7},{4,6},{5,1},{6,4},{7,3},{8,10},{9,13},{10,... | collective-permute-start | bytes 393224 | tf_op jit(solution)/shard_map/ppermute | solution.py:249
  22.2 6.8 %collective-permute-start.10 = (f32[128,256]{1,0:T(8,128)S(1)}, f32[128,256]{1,0:T(8,128)S(1)}, u32[]{:S(2)}, u32[]{:S(2)}) collective-permute-start(f32[128,256]{1,0:T(8,128)S(1)} %add.14.v_ref), channel_id=1, source_target_pairs={{0,4},{2,6},{4,0},{6,2},{8,12},{10,14},{12,8},{14,10},{1,5},{3,7},... | collective-permute-start | bytes 393224 | tf_op jit(solution)/shard_map/ppermute | solution.py:235
  22.9 7.1 %collective-permute-start.7 = (f32[128,256]{1,0:T(8,128)S(1)}, f32[128,256]{1,0:T(8,128)S(1)}, u32[]{:S(2)}, u32[]{:S(2)}) collective-permute-start(f32[128,256]{1,0:T(8,128)S(1)} %shard_map.64.q_ref), channel_id=1, source_target_pairs={{0,2},{2,0},{4,6},{6,4},{8,10},{10,8},{12,14},{14,12},{1,3},{3,1},... | collective-permute-start | bytes 393224 | tf_op jit(solution)/shard_map/ppermute | solution.py:235
  25.2 8.1 %collective-permute-start.11 = (f32[128,256]{1,0:T(8,128)S(1)}, f32[128,256]{1,0:T(8,128)S(1)}, u32[]{:S(2)}, u32[]{:S(2)}) collective-permute-start(f32[128,256]{1,0:T(8,128)S(1)} %add.15.w_ref), channel_id=1, source_target_pairs={{0,8},{2,10},{4,12},{6,14},{8,0},{10,2},{12,4},{14,6},{1,9},{3,11}... | collective-permute-start | bytes 393224 | tf_op jit(solution)/shard_map/ppermute | solution.py:235
  30.0 3.4 %collective-permute-start.12 = (f32[128,256]{1,0:T(8,128)S(1)}, f32[128,256]{1,0:T(8,128)S(1)}, u32[]{:S(2)}, u32[]{:S(2)}) collective-permute-start(f32[128,256]{1,0:T(8,128)S(1)} %add.15.w_ref), channel_id=1, source_target_pairs={{0,1},{1,0},{2,3},{3,2},{4,5},{5,4},{6,7},{7,6},{8,9},{9,8},{10,11... | collective-permute-start | bytes 393224 | tf_op jit(solution)/shard_map/ppermute | solution.py:239
  31.1 2.3 %collective-permute-start.14 = (f32[128,256]{1,0:T(8,128)S(1)}, f32[128,256]{1,0:T(8,128)S(1)}, u32[]{:S(2)}, u32[]{:S(2)}) collective-permute-start(f32[128,256]{1,0:T(8,128)S(1)} %get-tuple-element.50), channel_id=1, source_target_pairs={{0,1},{1,0},{2,3},{3,2},{4,5},{5,4},{6,7},{7,6},{8,9},{9,8},{10,11... | collective-permute-start | bytes 393224 | tf_op jit(solution)/shard_map/ppermute | solution.py:239
  31.6 1.7 %collective-permute-start.13 = (f32[128,256]{1,0:T(8,128)S(1)}, f32[128,256]{1,0:T(8,128)S(1)}, u32[]{:S(2)}, u32[]{:S(2)}) collective-permute-start(f32[128,256]{1,0:T(8,128)S(1)} %get-tuple-element.48), channel_id=1, source_target_pairs={{0,1},{1,0},{2,3},{3,2},{4,5},{5,4},{6,7},{7,6},{8,9},{9,8},{10,11... | collective-permute-start | bytes 393224 | tf_op jit(solution)/shard_map/ppermute | solution.py:239
  33.3 1.4 %collective-permute-start.15 = (f32[128,256]{1,0:T(8,128)S(1)}, f32[128,256]{1,0:T(8,128)S(1)}, u32[]{:S(2)}, u32[]{:S(2)}) collective-permute-start(f32[128,256]{1,0:T(8,128)S(1)} %collective-permute-done.11.far_ref), channel_id=1, source_target_pairs={{0,1},{1,0},{2,3},{3,2},{4,5},{5,4},{6,7},{7,6},{8,9},{9,8},{10,11... | collective-permute-start | bytes 393224 | tf_op jit(solution)/shard_map/ppermute | solution.py:239

commit v6 on v5

--- a/solution.py
+++ b/solution.py
@@ -188,30 +188,32 @@
     out_ref[...] = field_ref[...] - dot(lefts, jnp.concatenate([k, w_ref[...]], 0))
 
 
-def solve_own(rest, own_ref, first_ref, last_ref, row_ref, top_ref, far_ref, w_ref, *refs):
+def solve_own(rest, own_ref, first_ref, last_ref, row_ref, top_ref, far_ref, *refs):
     *k_refs, out_ref, other_ref = refs
     child, core = place(rest)
     side = lax.shift_right_logical(child, 2)
     out_ref[...] = own_ref[...] - dot(top_ref[1 - side], far_ref[...])
-    cols = block(1 - core, w_ref.shape[1])
+    cols = block(1 - core, far_ref.shape[1])
     cut = first_ref.shape[0]
-    lefts = jnp.concatenate([row_ref[1], row_ref[2], top_ref[side]], 1)
-    term = dot(lefts, jnp.concatenate([ref[...] for ref in (*k_refs, w_ref)], 0))
+    lefts = jnp.concatenate([row_ref[1], row_ref[2]], 1)
+    term = dot(lefts, jnp.concatenate([ref[...] for ref in k_refs], 0))
     other_ref[:cut] = first_ref[:, cols] - term[:cut]
     other_ref[cut:] = last_ref[:, cols] - term[cut:]
 
 
-def solve_other(rest, pieces, own_ref, less_ref, top_ref, far_ref, out_ref, other_ref, sems):
+def solve_other(rest, pieces, own_ref, less_ref, top_ref, w_ref, far_ref, out_ref, other_ref, sems):
     child, core = place(rest)
     side = lax.shift_right_logical(child, 2)
     total, half = own_ref.shape
     mine, theirs = block(core, half), block(1 - core, half)
     copies = [pltpu.make_async_copy(own_ref, out_ref.at[:, mine], sems.at[pieces])]
     copies[0].start()
+    both = jnp.concatenate([w_ref[...], far_ref[...]], 0)
     step = total // pieces
     for i in range(pieces):
         part = slice(i * step, (i + 1) * step)
-        other_ref[part] = less_ref[part] - dot(top_ref[1 - side, part], far_ref[...])
+        lefts = jnp.concatenate([top_ref[side, part], top_ref[1 - side, part]], 1)
+        other_ref[part] = less_ref[part] - dot(lefts, both)
         copy = pltpu.make_async_copy(other_ref.at[part], out_ref.at[part, theirs], sems.at[i])
         copy.start()
         copies.append(copy)
@@ -291,7 +293,7 @@
         (pairs, pairs_x, woodbury_cores), 0,
     )
     recv = swap_narrow(after(send, last_z, fix))
-    fix_other = swap_narrow(after(fix, last_z))
+    fix_other = swap_narrow(fix)
     fix_top = call(
         functools.partial(last_corrections, rest), shape(rank, rank),
         (last, last_x, last_z, woodbury_cores), 0,
@@ -313,12 +315,12 @@
         functools.partial(top_matrix, rest), shape(2, rows, rank),
         (row_bases, after(woodbury_cores, w)), 0,
     )
-    w = w_mid = w + after(swap_crossed(w, bit2, bit3), top)
-    q = tie(q, w_mid)
+    w = w_mid = w + after(swap_crossed(w, bit2, bit3), top, q)
+    q = tie(q, top)
     q_x = swap_wide(q, bit3)
     v = v + after(v_x, w_mid)
     v_z = swap_wide(v, bit2)
-    w = w + after(swap_crossed(w, bit3, bit2), v, q)
+    w = w + after(swap_crossed(w, bit3, bit2), v)
     far = swap_wide(w, bit1)
     k2, lower = call(
         functools.partial(lower_two, rest), (shape(rank, half), shape(rows, half)),
@@ -333,12 +335,12 @@
     far_other = swap_narrow(far)
     own, less = call(
         functools.partial(solve_own, rest), (shape(rows, half),) * 2,
-        (lower, first_rows, last_rows, row_bases, top, far, w_other, *k_other), 0,
+        (lower, first_rows, last_rows, row_bases, top, far, *k_other), 0,
     )
     pieces = 4
     return call(
         functools.partial(solve_other, rest, pieces), shape(rows, cols),
-        (own, less, top, far_other), 0,
+        (own, less, top, w_other, far_other), 0,
         scratch=[pltpu.VMEM((rows, half), F32), pltpu.SemaphoreType.DMA((pieces + 1,))],
         out_specs=pl.BlockSpec(memory_space=pltpu.HBM),
     )

time: 36.5 us -> 36.3 us (level)
  Pallas kernels: 13.7 us -> 13.2 us
    pallas_call x15, Pallas kernels: 13.7 us -> 13.2 us  [call(): pl.pallas_call(body, in_specs=in_specs or [VMEM] * len(args), out_specs=j...]
  transfers between devices with their start and end apart: 16 -> 16, of which waited for: 6 -> 7; matrix products, arithmetic and copies ran while one was open for 0% -> 0% of each run, Pallas kernels for 28% -> 27%
where the time goes in v6:
time: 36.3 us; the launch traced here: 36.1 us
  starting transfers between devices  15.7 us (43%)
  Pallas kernels  13.2 us (36%)
  waiting for transfers between devices  6.93 us (19%)
    pallas_call x15, Pallas kernels, call(): pl.pallas_call(body, in_specs=in_specs or [VMEM] * len(args), out_specs=j...  13.2 us
    ppermute x5, starting transfers between devices, swap_crossed(): return lax.ppermute(x, ('wide', 'narrow'), route)  7.29 us
    ppermute x4, starting transfers between devices, swap_wide(): return lax.ppermute(x, 'wide', [(w, w ^ 1 << bit) for w in range(count)])  6.65 us
    ppermute x4, waiting for transfers between devices, swap_wide(): return lax.ppermute(x, 'wide', [(w, w ^ 1 << bit) for w in range(count)])  3.32 us
    ppermute x5, waiting for transfers between devices, swap_crossed(): return lax.ppermute(x, ('wide', 'narrow'), route)  2.5 us
    ppermute x7, starting transfers between devices, swap_narrow(): return lax.ppermute(x, 'narrow', [(0, 1), (1, 0)])  1.73 us
    ppermute x7, waiting for transfers between devices, swap_narrow(): return lax.ppermute(x, 'narrow', [(0, 1), (1, 0)])  1.11 us
  transfers between devices with their start and end apart: 16, of which 7 were waited for; matrix products, arithmetic and copies ran while one was open for 0% of the time, Pallas kernels for 27%

profile of v6, /device:TPU:0, one launch (start us, length us, event | category | flops | bytes accessed | tf_op | source)
XLA Modules:
  0.0 36.1 jit_solution(11333578062901387768)
XLA Ops:
  0.0 1.8 %shard_map.55.last_ref = f32[128,128]{1,0:T(8,128)S(1)} custom-call(f32[3,1024,128]{2,1,0:T(8,128)} %dual_ref.3, f32[3,1024,128]{2,1,0:T(8,128)} %row_ref.9), custom_call_target="tpu_custom_call" | custom-call | flops 16106127360 | tf_op jit(solution)/shard_map/pallas_call | solution.py:42
  1.8 0.0 copy-start.3
  1.8 2.4 %collective-permute-start = (f32[128,128]{1,0:T(8,128)S(1)}, f32[128,128]{1,0:T(8,128)S(1)}, u32[]{:S(2)}, u32[]{:S(2)}) collective-permute-start(f32[128,128]{1,0:T(8,128)S(1)} %shard_map.55.last_ref), channel_id=1, source_target_pairs={{0,3},{1,2},{2,1},{3,0},{4,7},{5,6},{6,5},{7,4},{8,11},{9,10},{10,... | collective-permute-start | bytes 196616 | tf_op jit(solution)/shard_map/ppermute | solution.py:251
  4.3 0.0 copy-done.4
  4.3 0.6 %shard_map.58.pairs_ref = f32[256,128]{1,0:T(8,128)S(1)} custom-call(f32[3,1024,128]{2,1,0:T(8,128)S(1)} %copy-done.4, f32[3,1024,128]{2,1,0:T(8,128)S(1)} %copy-done.1, f32[128,128]{1,0:T(8,128)S(1)} %shard_map.55.last_ref), custom_call_target="tpu_custom_call" | custom-call | flops 67108864 | tf_op jit(solution)/shard_map/pallas_call | solution.py:42
  4.9 0.4 %collective-permute-start.2 = (f32[256,128]{1,0:T(8,128)S(1)}, f32[256,128]{1,0:T(8,128)S(1)}, u32[]{:S(2)}, u32[]{:S(2)}) collective-permute-start(f32[256,128]{1,0:T(8,128)S(1)} %shard_map.58.pairs_ref), channel_id=1, source_target_pairs={{0,3},{1,2},{2,1},{3,0},{4,7},{5,6},{6,5},{7,4},{8,11},{9,10},{10,... | collective-permute-start | bytes 393224 | tf_op jit(solution)/shard_map/ppermute | solution.py:251
  5.3 1.8 %shard_map.56.first_ref = f32[512,512]{1,0:T(8,128)S(1)} custom-call(f32[1024,1024]{1,0:T(8,128)S(1)} %copy-done.2, f32[1024,512]{1,0:T(8,128)S(1)} %copy-done.3), custom_call_target="tpu_custom_call" | custom-call | flops 1610612736 | tf_op jit(solution)/shard_map/pallas_call | solution.py:42
  7.1 0.0 collective-permute-done.last_x_ref
  7.1 0.0 copy-start
  7.1 1.9 %collective-permute-start.1 = (f32[128,128]{1,0:T(8,128)S(1)}, f32[128,128]{1,0:T(8,128)S(1)}, u32[]{:S(2)}, u32[]{:S(2)}) collective-permute-start(f32[128,128]{1,0:T(8,128)S(1)} %add.12), channel_id=1, source_target_pairs={{0,5},{1,4},{2,7},{3,6},{4,1},{5,0},{6,3},{7,2},{8,13},{9,12},{10,... | collective-permute-start | bytes 196616 | tf_op jit(solution)/shard_map/ppermute | solution.py:251
  9.1 3.1 %shard_map.57 = (f32[512,512]{1,0:T(8,128)S(1)}, f32[384,256]{1,0:T(8,128)S(1)}, f32[384,256]{1,0:T(8,128)S(1)}) custom-call(f32[1024,1024]{1,0:T(8,128)S(1)} %copy-done.2, f32[1024,512]{1,0:T(8,128)S(1)} %copy-done.3, f32[3,1024,128]{2,1,0:T(8,128)S(1)} %copy-done.4, f32[512,512]{1,0:T(8,128)S(1)} %shard_map.56.first_ref), custom_call_target="tpu_custom_call" | custom-call | tf_op jit(solution)/shard_map/pallas_call | solution.py:42
  12.2 0.0 collective-permute-done.2.pairs_x_ref
  12.2 0.3 shard_map.59.fix_ref
  12.4 0.0 collective-permute-done.1.last_z_ref
  12.5 0.4 %collective-permute-start.3 = (f32[384,256]{1,0:T(8,128)S(1)}, f32[384,256]{1,0:T(8,128)S(1)}, u32[]{:S(2)}, u32[]{:S(2)}) collective-permute-start(f32[384,256]{1,0:T(8,128)S(1)} %get-tuple-element.33), channel_id=1, source_target_pairs={{0,1},{1,0},{2,3},{3,2},{4,5},{5,4},{6,7},{7,6},{8,9},{9,8},{10,11... | collective-permute-start | bytes 1179656 | tf_op jit(solution)/shard_map/ppermute | solution.py:241
  12.9 0.1 collective-permute-start.4
  13.0 0.2 shard_map.61.fix_ref
  13.3 0.4 %collective-permute-start.5 = (f32[128,128]{1,0:T(8,128)S(1)}, f32[128,128]{1,0:T(8,128)S(1)}, u32[]{:S(2)}, u32[]{:S(2)}) collective-permute-start(f32[128,128]{1,0:T(8,128)S(1)} %shard_map.61.fix_ref), channel_id=1, source_target_pairs={{0,1},{1,0},{2,3},{3,2},{4,5},{5,4},{6,7},{7,6},{8,9},{9,8},{10,11... | collective-permute-start | bytes 196616 | tf_op jit(solution)/shard_map/ppermute | solution.py:241
  13.7 0.7 %collective-permute-done.4.fix_other_ref = f32[256,128]{1,0:T(8,128)S(1)} collective-permute-done((f32[256,128]{1,0:T(8,128)S(1)}, f32[256,128]{1,0:T(8,128)S(1)}, u32[]{:S(2)}, u32[]{:S(2)}) %collective-permute-start.4) | collective-permute-done | bytes 131104 | tf_op jit(solution)/shard_map/ppermute | solution.py:241
  14.4 0.0 collective-permute-done.3.recv_ref
  14.4 0.3 shard_map.60
  14.7 0.0 collective-permute-done.5.fix_other_ref
  14.7 0.2 shard_map.62.refs_0_
  14.9 0.9 %collective-permute-start.8 = (f32[128,256]{1,0:T(8,128)S(1)}, f32[128,256]{1,0:T(8,128)S(1)}, u32[]{:S(2)}, u32[]{:S(2)}) collective-permute-start(f32[128,256]{1,0:T(8,128)S(1)} %shard_map.62.refs_0_), channel_id=1, source_target_pairs={{0,4},{1,3},{2,6},{3,1},{4,0},{5,7},{6,2},{7,5},{8,12},{9,11},{10,... | collective-permute-start | bytes 393224 | tf_op jit(solution)/shard_map/ppermute | solution.py:251
  15.9 1.6 %collective-permute-start.7 = (f32[128,256]{1,0:T(8,128)S(1)}, f32[128,256]{1,0:T(8,128)S(1)}, u32[]{:S(2)}, u32[]{:S(2)}) collective-permute-start(f32[128,256]{1,0:T(8,128)S(1)} %shard_map.65), channel_id=1, source_target_pairs={{0,2},{2,0},{4,6},{6,4},{8,10},{10,8},{12,14},{14,12},{1,3},{3,1},... | collective-permute-start | bytes 393224 | tf_op jit(solution)/shard_map/ppermute | solution.py:237
  17.5 0.6 %shard_map.63.refs_0_.top_ref = f32[2,1024,128]{2,1,0:T(8,128)S(1)} custom-call(f32[3,1024,128]{2,1,0:T(8,128)S(1)} %copy-done.1, f32[1792,256]{1,0:T(8,128)S(1)} %copy-done), custom_call_target="tpu_custom_call" | custom-call | tf_op jit(solution)/shard_map/pallas_call | solution.py:42
  18.1 1.9 %collective-permute-done.8 = f32[128,256]{1,0:T(8,128)S(1)} collective-permute-done((f32[128,256]{1,0:T(8,128)S(1)}, f32[128,256]{1,0:T(8,128)S(1)}, u32[]{:S(2)}, u32[]{:S(2)}) %collective-permute-start.8) | collective-permute-done | bytes 131104 | tf_op jit(solution)/shard_map/ppermute | solution.py:251
  20.0 1.6 %collective-permute-start.9 = (f32[128,256]{1,0:T(8,128)S(1)}, f32[128,256]{1,0:T(8,128)S(1)}, u32[]{:S(2)}, u32[]{:S(2)}) collective-permute-start(f32[128,256]{1,0:T(8,128)S(1)} %add.13), channel_id=1, source_target_pairs={{0,2},{1,5},{2,0},{3,7},{4,6},{5,1},{6,4},{7,3},{8,10},{9,13},{10,... | collective-permute-start | bytes 393224 | tf_op jit(solution)/shard_map/ppermute | solution.py:251
  21.6 0.6 %collective-permute-done.7 = f32[128,256]{1,0:T(8,128)S(1)} collective-permute-done((f32[128,256]{1,0:T(8,128)S(1)}, f32[128,256]{1,0:T(8,128)S(1)}, u32[]{:S(2)}, u32[]{:S(2)}) %collective-permute-start.7) | collective-permute-done | bytes 131104 | tf_op jit(solution)/shard_map/ppermute | solution.py:237
  22.2 0.7 %collective-permute-start.10 = (f32[128,256]{1,0:T(8,128)S(1)}, f32[128,256]{1,0:T(8,128)S(1)}, u32[]{:S(2)}, u32[]{:S(2)}) collective-permute-start(f32[128,256]{1,0:T(8,128)S(1)} %add.14.v_ref), channel_id=1, source_target_pairs={{0,4},{2,6},{4,0},{6,2},{8,12},{10,14},{12,8},{14,10},{1,5},{3,7},... | collective-permute-start | bytes 393224 | tf_op jit(solution)/shard_map/ppermute | solution.py:237
  22.9 1.6 %collective-permute-start.6 = (f32[128,256]{1,0:T(8,128)S(1)}, f32[128,256]{1,0:T(8,128)S(1)}, u32[]{:S(2)}, u32[]{:S(2)}) collective-permute-start(f32[128,256]{1,0:T(8,128)S(1)} %shard_map.64.q_ref), channel_id=1, source_target_pairs={{0,2},{2,0},{4,6},{6,4},{8,10},{10,8},{12,14},{14,12},{1,3},{3,1},... | collective-permute-start | bytes 393224 | tf_op jit(solution)/shard_map/ppermute | solution.py:237
  24.6 0.6 %collective-permute-done.9 = f32[128,256]{1,0:T(8,128)S(1)} collective-permute-done((f32[128,256]{1,0:T(8,128)S(1)}, f32[128,256]{1,0:T(8,128)S(1)}, u32[]{:S(2)}, u32[]{:S(2)}) %collective-permute-start.9) | collective-permute-done | bytes 131104 | tf_op jit(solution)/shard_map/ppermute | solution.py:251
  25.2 2.7 %collective-permute-start.11 = (f32[128,256]{1,0:T(8,128)S(1)}, f32[128,256]{1,0:T(8,128)S(1)}, u32[]{:S(2)}, u32[]{:S(2)}) collective-permute-start(f32[128,256]{1,0:T(8,128)S(1)} %add.15.w_ref), channel_id=1, source_target_pairs={{0,8},{2,10},{4,12},{6,14},{8,0},{10,2},{12,4},{14,6},{1,9},{3,11}... | collective-permute-start | bytes 393224 | tf_op jit(solution)/shard_map/ppermute | solution.py:237
  27.9 1.1 %collective-permute-done.10.vz_ref = f32[128,256]{1,0:T(8,128)S(1)} collective-permute-done((f32[128,256]{1,0:T(8,128)S(1)}, f32[128,256]{1,0:T(8,128)S(1)}, u32[]{:S(2)}, u32[]{:S(2)}) %collective-permute-start.10) | collective-permute-done | bytes 131104 | tf_op jit(solution)/shard_map/ppermute | solution.py:237
  29.0 1.0 %shard_map.66 = (f32[128,256]{1,0:T(8,128)S(1)}, f32[1024,256]{1,0:T(8,128)S(1)}) custom-call(f32[128,256]{1,0:T(8,128)S(1)} %add.14.v_ref, f32[128,256]{1,0:T(8,128)S(1)} %collective-permute-done.10.vz_ref, f32[1792,256]{1,0:T(8,128)S(1)} %copy-done, f32[512,512]{1,0:T(8,128)S(1)} %shard_map.56.first_ref, f32[512,512]{1,0:T(8,128)S(1)} %get-tuple-element.43.last_ref, ...), custom_call_target="tpu_custom_call" | custom-call | tf_op jit(solution)/shard_map/pallas_call | solution.py:42
  30.0 0.1 collective-permute-start.12
  30.0 0.0 collective-permute-done.6.qx_ref
  30.1 1.0 %shard_map.67 = (f32[128,256]{1,0:T(8,128)S(1)}, f32[1024,256]{1,0:T(8,128)S(1)}) custom-call(f32[128,256]{1,0:T(8,128)S(1)} %shard_map.64.q_ref, f32[128,256]{1,0:T(8,128)S(1)} %collective-permute-done.6.qx_ref, f32[1792,256]{1,0:T(8,128)S(1)} %copy-done, f32[1024,256]{1,0:T(8,128)S(1)} %get-tuple-element.44.field_ref, f32[3,1024,128]{2,1,0:T(8,128)S(1)} %copy-done.1, ...), custom_call_target="tpu_custom_call" | custom-call | tf_op jit(solution)/shard_map/pallas_call | solution.py:42
  31.1 0.6 %collective-permute-start.13 = (f32[128,256]{1,0:T(8,128)S(1)}, f32[128,256]{1,0:T(8,128)S(1)}, u32[]{:S(2)}, u32[]{:S(2)}) collective-permute-start(f32[128,256]{1,0:T(8,128)S(1)} %get-tuple-element.47), channel_id=1, source_target_pairs={{0,1},{1,0},{2,3},{3,2},{4,5},{5,4},{6,7},{7,6},{8,9},{9,8},{10,11... | collective-permute-start | bytes 393224 | tf_op jit(solution)/shard_map/ppermute | solution.py:241
  31.6 0.1 collective-permute-start.14
  31.7 1.6 %collective-permute-done.11.far_ref = f32[128,256]{1,0:T(8,128)S(1)} collective-permute-done((f32[128,256]{1,0:T(8,128)S(1)}, f32[128,256]{1,0:T(8,128)S(1)}, u32[]{:S(2)}, u32[]{:S(2)}) %collective-permute-start.11) | collective-permute-done | bytes 131104 | tf_op jit(solution)/shard_map/ppermute | solution.py:237
  33.3 0.0 collective-permute-start.15
  33.3 0.0 collective-permute-done.13.refs_1_
  33.3 0.0 collective-permute-done.12.refs_0_
  33.3 1.0 %shard_map.68 = (f32[1024,256]{1,0:T(8,128)S(1)}, f32[1024,256]{1,0:T(8,128)S(1)}) custom-call(f32[1024,256]{1,0:T(8,128)S(1)} %get-tuple-element.45.own_ref, f32[512,512]{1,0:T(8,128)S(1)} %shard_map.56.first_ref, f32[512,512]{1,0:T(8,128)S(1)} %get-tuple-element.43.last_ref, f32[3,1024,128]{2,1,0:T(8,128)S(1)} %copy-done.1, ...), custom_call_target="tpu_custom_call" | custom-call | tf_op jit(solution)/shard_map/pallas_call | solution.py:42
  34.3 0.0 collective-permute-done.14.w_ref
  34.3 0.3 collective-permute-done.15.far_ref
  34.7 1.4 %shard_map.69 = f32[1024,512]{1,0:T(8,128)} custom-call(f32[1024,256]{1,0:T(8,128)S(1)} %get-tuple-element.48.own_ref, f32[1024,256]{1,0:T(8,128)S(1)} %get-tuple-element.49.less_ref, f32[2,1024,128]{2,1,0:T(8,128)S(1)} %shard_map.63.refs_0_.top_ref, f32[128,256]{1,0:T(8,128)S(1)} %collective-permute-done.14.w_ref, ...), custom_call_target="tpu_custom_call" | custom-call | tf_op jit(solution)/shard_map/pallas_call | solution.py:42
  (13 shorter events, 0.1 us)
Async XLA Ops:
  0.0 4.3 %copy-start.1 = (f32[3,1024,128]{2,1,0:T(8,128)S(1)}, f32[3,1024,128]{2,1,0:T(8,128)}, u32[]{:S(2)}) copy-start(f32[3,1024,128]{2,1,0:T(8,128)} %row_ref.9) | copy-start | bytes 4718596
  0.0 4.3 %copy-start.4 = (f32[3,1024,128]{2,1,0:T(8,128)S(1)}, f32[3,1024,128]{2,1,0:T(8,128)}, u32[]{:S(2)}) copy-start(f32[3,1024,128]{2,1,0:T(8,128)} %dual_ref.3) | copy-start | bytes 4718596
  0.0 5.3 %copy-start.2 = (f32[1024,1024]{1,0:T(8,128)S(1)}, f32[1024,1024]{1,0:T(8,128)}, u32[]{:S(2)}) copy-start(f32[1024,1024]{1,0:T(8,128)} %leaf_ref.3) | copy-start | bytes 12582916
  1.8 3.5 %copy-start.3 = (f32[1024,512]{1,0:T(8,128)S(1)}, f32[1024,512]{1,0:T(8,128)}, u32[]{:S(2)}) copy-start(f32[1024,512]{1,0:T(8,128)} %right_ref.1) | copy-start | bytes 6291460
  1.8 5.3 %collective-permute-start = (f32[128,128]{1,0:T(8,128)S(1)}, f32[128,128]{1,0:T(8,128)S(1)}, u32[]{:S(2)}, u32[]{:S(2)}) collective-permute-start(f32[128,128]{1,0:T(8,128)S(1)} %shard_map.55.last_ref), channel_id=1, source_target_pairs={{0,3},{1,2},{2,1},{3,0},{4,7},{5,6},{6,5},{7,4},{8,11},{9,10},{10,... | collective-permute-start | bytes 196616 | tf_op jit(solution)/shard_map/ppermute | solution.py:251
  4.9 7.3 %collective-permute-start.2 = (f32[256,128]{1,0:T(8,128)S(1)}, f32[256,128]{1,0:T(8,128)S(1)}, u32[]{:S(2)}, u32[]{:S(2)}) collective-permute-start(f32[256,128]{1,0:T(8,128)S(1)} %shard_map.58.pairs_ref), channel_id=1, source_target_pairs={{0,3},{1,2},{2,1},{3,0},{4,7},{5,6},{6,5},{7,4},{8,11},{9,10},{10,... | collective-permute-start | bytes 393224 | tf_op jit(solution)/shard_map/ppermute | solution.py:251
  7.1 5.0 %copy-start = (f32[1792,256]{1,0:T(8,128)S(1)}, f32[1792,256]{1,0:T(8,128)}, u32[]{:S(2)}) copy-start(f32[1792,256]{1,0:T(8,128)} %cores_ref.8) | copy-start | bytes 5505028
  7.1 5.3 %collective-permute-start.1 = (f32[128,128]{1,0:T(8,128)S(1)}, f32[128,128]{1,0:T(8,128)S(1)}, u32[]{:S(2)}, u32[]{:S(2)}) collective-permute-start(f32[128,128]{1,0:T(8,128)S(1)} %add.12), channel_id=1, source_target_pairs={{0,5},{1,4},{2,7},{3,6},{4,1},{5,0},{6,3},{7,2},{8,13},{9,12},{10,... | collective-permute-start | bytes 196616 | tf_op jit(solution)/shard_map/ppermute | solution.py:251
  12.5 2.0 %collective-permute-start.3 = (f32[384,256]{1,0:T(8,128)S(1)}, f32[384,256]{1,0:T(8,128)S(1)}, u32[]{:S(2)}, u32[]{:S(2)}) collective-permute-start(f32[384,256]{1,0:T(8,128)S(1)} %get-tuple-element.33), channel_id=1, source_target_pairs={{0,1},{1,0},{2,3},{3,2},{4,5},{5,4},{6,7},{7,6},{8,9},{9,8},{10,11... | collective-permute-start | bytes 1179656 | tf_op jit(solution)/shard_map/ppermute | solution.py:241
  12.9 1.5 %collective-permute-start.4 = (f32[256,128]{1,0:T(8,128)S(1)}, f32[256,128]{1,0:T(8,128)S(1)}, u32[]{:S(2)}, u32[]{:S(2)}) collective-permute-start(f32[256,128]{1,0:T(8,128)S(1)} %shard_map.59.fix_ref), channel_id=1, source_target_pairs={{0,1},{1,0},{2,3},{3,2},{4,5},{5,4},{6,7},{7,6},{8,9},{9,8},{10,11... | collective-permute-start | bytes 393224 | tf_op jit(solution)/shard_map/ppermute | solution.py:241
  13.3 1.5 %collective-permute-start.5 = (f32[128,128]{1,0:T(8,128)S(1)}, f32[128,128]{1,0:T(8,128)S(1)}, u32[]{:S(2)}, u32[]{:S(2)}) collective-permute-start(f32[128,128]{1,0:T(8,128)S(1)} %shard_map.61.fix_ref), channel_id=1, source_target_pairs={{0,1},{1,0},{2,3},{3,2},{4,5},{5,4},{6,7},{7,6},{8,9},{9,8},{10,11... | collective-permute-start | bytes 196616 | tf_op jit(solution)/shard_map/ppermute | solution.py:241
  14.9 5.0 %collective-permute-start.8 = (f32[128,256]{1,0:T(8,128)S(1)}, f32[128,256]{1,0:T(8,128)S(1)}, u32[]{:S(2)}, u32[]{:S(2)}) collective-permute-start(f32[128,256]{1,0:T(8,128)S(1)} %shard_map.62.refs_0_), channel_id=1, source_target_pairs={{0,4},{1,3},{2,6},{3,1},{4,0},{5,7},{6,2},{7,5},{8,12},{9,11},{10,... | collective-permute-start | bytes 393224 | tf_op jit(solution)/shard_map/ppermute | solution.py:251
  15.9 6.3 %collective-permute-start.7 = (f32[128,256]{1,0:T(8,128)S(1)}, f32[128,256]{1,0:T(8,128)S(1)}, u32[]{:S(2)}, u32[]{:S(2)}) collective-permute-start(f32[128,256]{1,0:T(8,128)S(1)} %shard_map.65), channel_id=1, source_target_pairs={{0,2},{2,0},{4,6},{6,4},{8,10},{10,8},{12,14},{14,12},{1,3},{3,1},... | collective-permute-start | bytes 393224 | tf_op jit(solution)/shard_map/ppermute | solution.py:237
  20.0 5.2 %collective-permute-start.9 = (f32[128,256]{1,0:T(8,128)S(1)}, f32[128,256]{1,0:T(8,128)S(1)}, u32[]{:S(2)}, u32[]{:S(2)}) collective-permute-start(f32[128,256]{1,0:T(8,128)S(1)} %add.13), channel_id=1, source_target_pairs={{0,2},{1,5},{2,0},{3,7},{4,6},{5,1},{6,4},{7,3},{8,10},{9,13},{10,... | collective-permute-start | bytes 393224 | tf_op jit(solution)/shard_map/ppermute | solution.py:251
  22.2 6.8 %collective-permute-start.10 = (f32[128,256]{1,0:T(8,128)S(1)}, f32[128,256]{1,0:T(8,128)S(1)}, u32[]{:S(2)}, u32[]{:S(2)}) collective-permute-start(f32[128,256]{1,0:T(8,128)S(1)} %add.14.v_ref), channel_id=1, source_target_pairs={{0,4},{2,6},{4,0},{6,2},{8,12},{10,14},{12,8},{14,10},{1,5},{3,7},... | collective-permute-start | bytes 393224 | tf_op jit(solution)/shard_map/ppermute | solution.py:237
  22.9 7.1 %collective-permute-start.6 = (f32[128,256]{1,0:T(8,128)S(1)}, f32[128,256]{1,0:T(8,128)S(1)}, u32[]{:S(2)}, u32[]{:S(2)}) collective-permute-start(f32[128,256]{1,0:T(8,128)S(1)} %shard_map.64.q_ref), channel_id=1, source_target_pairs={{0,2},{2,0},{4,6},{6,4},{8,10},{10,8},{12,14},{14,12},{1,3},{3,1},... | collective-permute-start | bytes 393224 | tf_op jit(solution)/shard_map/ppermute | solution.py:237
  25.2 8.1 %collective-permute-start.11 = (f32[128,256]{1,0:T(8,128)S(1)}, f32[128,256]{1,0:T(8,128)S(1)}, u32[]{:S(2)}, u32[]{:S(2)}) collective-permute-start(f32[128,256]{1,0:T(8,128)S(1)} %add.15.w_ref), channel_id=1, source_target_pairs={{0,8},{2,10},{4,12},{6,14},{8,0},{10,2},{12,4},{14,6},{1,9},{3,11}... | collective-permute-start | bytes 393224 | tf_op jit(solution)/shard_map/ppermute | solution.py:237
  30.0 3.4 %collective-permute-start.12 = (f32[128,256]{1,0:T(8,128)S(1)}, f32[128,256]{1,0:T(8,128)S(1)}, u32[]{:S(2)}, u32[]{:S(2)}) collective-permute-start(f32[128,256]{1,0:T(8,128)S(1)} %get-tuple-element.46), channel_id=1, source_target_pairs={{0,1},{1,0},{2,3},{3,2},{4,5},{5,4},{6,7},{7,6},{8,9},{9,8},{10,11... | collective-permute-start | bytes 393224 | tf_op jit(solution)/shard_map/ppermute | solution.py:241
  31.1 2.3 %collective-permute-start.13 = (f32[128,256]{1,0:T(8,128)S(1)}, f32[128,256]{1,0:T(8,128)S(1)}, u32[]{:S(2)}, u32[]{:S(2)}) collective-permute-start(f32[128,256]{1,0:T(8,128)S(1)} %get-tuple-element.47), channel_id=1, source_target_pairs={{0,1},{1,0},{2,3},{3,2},{4,5},{5,4},{6,7},{7,6},{8,9},{9,8},{10,11... | collective-permute-start | bytes 393224 | tf_op jit(solution)/shard_map/ppermute | solution.py:241
  31.6 2.7 %collective-permute-start.14 = (f32[128,256]{1,0:T(8,128)S(1)}, f32[128,256]{1,0:T(8,128)S(1)}, u32[]{:S(2)}, u32[]{:S(2)}) collective-permute-start(f32[128,256]{1,0:T(8,128)S(1)} %add.15.w_ref), channel_id=1, source_target_pairs={{0,1},{1,0},{2,3},{3,2},{4,5},{5,4},{6,7},{7,6},{8,9},{9,8},{10,11... | collective-permute-start | bytes 393224 | tf_op jit(solution)/shard_map/ppermute | solution.py:241
  33.3 1.3 %collective-permute-start.15 = (f32[128,256]{1,0:T(8,128)S(1)}, f32[128,256]{1,0:T(8,128)S(1)}, u32[]{:S(2)}, u32[]{:S(2)}) collective-permute-start(f32[128,256]{1,0:T(8,128)S(1)} %collective-permute-done.11.far_ref), channel_id=1, source_target_pairs={{0,1},{1,0},{2,3},{3,2},{4,5},{5,4},{6,7},{7,6},{8,9},{9,8},{10,11... | collective-permute-start | bytes 393224 | tf_op jit(solution)/shard_map/ppermute | solution.py:241

commit v7 on v6

--- a/solution.py
+++ b/solution.py
@@ -11,26 +11,24 @@
 VMEM = pl.BlockSpec(memory_space=pltpu.VMEM)
 
 
-def dot(a, b):
-    return jnp.dot(a, b, precision=lax.Precision.HIGH, preferred_element_type=F32)
-
-
-def dot_t(a, b):
-    return lax.dot_general(
-        a, b, (((0,), (0,)), ((), ())), precision=lax.Precision.HIGH, preferred_element_type=F32
-    )
-
-
 def halves(x):
     high = x.astype(BF16)
     return high, (x - high.astype(F32)).astype(BF16)
 
 
-def dot3(a, b):
+def dot3(a, b, dims=((1,), (0,))):
     def one(x, y):
-        return jnp.dot(x, y, preferred_element_type=F32)
+        return lax.dot_general(x, y, (dims, ((), ())), preferred_element_type=F32)
 
     return one(a[0], b[0]) + one(a[0], b[1]) + one(a[1], b[0])
+
+
+def dot(a, b):
+    return dot3(halves(a), halves(b))
+
+
+def dot_t(a, b):
+    return dot3(halves(a), halves(b), ((0,), (0,)))
 
 
 def shape(*dims, dtype=F32):
@@ -337,7 +335,7 @@
         functools.partial(solve_own, rest), (shape(rows, half),) * 2,
         (lower, first_rows, last_rows, row_bases, top, far, *k_other), 0,
     )
-    pieces = 4
+    pieces = 8
     return call(
         functools.partial(solve_other, rest, pieces), shape(rows, cols),
         (own, less, top, w_other, far_other), 0,

time: 36.3 us -> 36.2 us (level)
  no operation moved by 1% of the time
where the time goes in v7:
time: 36.2 us; the launch traced here: 36.1 us
  starting transfers between devices  15.5 us (43%)
  Pallas kernels  13.2 us (36%)
  waiting for transfers between devices  7.08 us (20%)
    pallas_call x15, Pallas kernels, call(): pl.pallas_call(body, in_specs=in_specs or [VMEM] * len(args), out_specs=j...  13.2 us
    ppermute x5, starting transfers between devices, swap_crossed(): return lax.ppermute(x, ('wide', 'narrow'), route)  7.28 us
    ppermute x4, starting transfers between devices, swap_wide(): return lax.ppermute(x, 'wide', [(w, w ^ 1 << bit) for w in range(count)])  6.49 us
    ppermute x4, waiting for transfers between devices, swap_wide(): return lax.ppermute(x, 'wide', [(w, w ^ 1 << bit) for w in range(count)])  3.41 us
    ppermute x5, waiting for transfers between devices, swap_crossed(): return lax.ppermute(x, ('wide', 'narrow'), route)  2.61 us
    ppermute x7, starting transfers between devices, swap_narrow(): return lax.ppermute(x, 'narrow', [(0, 1), (1, 0)])  1.74 us
    ppermute x7, waiting for transfers between devices, swap_narrow(): return lax.ppermute(x, 'narrow', [(0, 1), (1, 0)])  1.07 us
  transfers between devices with their start and end apart: 16, of which 7 were waited for; matrix products, arithmetic and copies ran while one was open for 0% of the time, Pallas kernels for 27%

profile of v7, /device:TPU:0, one launch (start us, length us, event | category | flops | bytes accessed | tf_op | source)
XLA Modules:
  0.0 36.1 jit_solution(14295963374156918273)
XLA Ops:
  0.0 1.8 %shard_map.55.last_ref = f32[128,128]{1,0:T(8,128)S(1)} custom-call(f32[3,1024,128]{2,1,0:T(8,128)} %dual_ref.3, f32[3,1024,128]{2,1,0:T(8,128)} %row_ref.9), custom_call_target="tpu_custom_call" | custom-call | flops 16106127360 | tf_op jit(solution)/shard_map/pallas_call | solution.py:40
  1.8 0.0 copy-start.3
  1.8 2.4 %collective-permute-start = (f32[128,128]{1,0:T(8,128)S(1)}, f32[128,128]{1,0:T(8,128)S(1)}, u32[]{:S(2)}, u32[]{:S(2)}) collective-permute-start(f32[128,128]{1,0:T(8,128)S(1)} %shard_map.55.last_ref), channel_id=1, source_target_pairs={{0,3},{1,2},{2,1},{3,0},{4,7},{5,6},{6,5},{7,4},{8,11},{9,10},{10,... | collective-permute-start | bytes 196616 | tf_op jit(solution)/shard_map/ppermute | solution.py:249
  4.2 0.0 copy-done.1
  4.3 0.6 %shard_map.58.pairs_ref = f32[256,128]{1,0:T(8,128)S(1)} custom-call(f32[3,1024,128]{2,1,0:T(8,128)S(1)} %copy-done.4, f32[3,1024,128]{2,1,0:T(8,128)S(1)} %copy-done.1, f32[128,128]{1,0:T(8,128)S(1)} %shard_map.55.last_ref), custom_call_target="tpu_custom_call" | custom-call | flops 67108864 | tf_op jit(solution)/shard_map/pallas_call | solution.py:40
  4.9 0.4 %collective-permute-start.2 = (f32[256,128]{1,0:T(8,128)S(1)}, f32[256,128]{1,0:T(8,128)S(1)}, u32[]{:S(2)}, u32[]{:S(2)}) collective-permute-start(f32[256,128]{1,0:T(8,128)S(1)} %shard_map.58.pairs_ref), channel_id=1, source_target_pairs={{0,3},{1,2},{2,1},{3,0},{4,7},{5,6},{6,5},{7,4},{8,11},{9,10},{10,... | collective-permute-start | bytes 393224 | tf_op jit(solution)/shard_map/ppermute | solution.py:249
  5.3 1.8 %shard_map.56.first_ref = f32[512,512]{1,0:T(8,128)S(1)} custom-call(f32[1024,1024]{1,0:T(8,128)S(1)} %copy-done.2, f32[1024,512]{1,0:T(8,128)S(1)} %copy-done.3), custom_call_target="tpu_custom_call" | custom-call | flops 1610612736 | tf_op jit(solution)/shard_map/pallas_call | solution.py:40
  7.1 0.0 collective-permute-done.last_x_ref
  7.1 0.0 copy-start
  7.1 1.9 %collective-permute-start.1 = (f32[128,128]{1,0:T(8,128)S(1)}, f32[128,128]{1,0:T(8,128)S(1)}, u32[]{:S(2)}, u32[]{:S(2)}) collective-permute-start(f32[128,128]{1,0:T(8,128)S(1)} %add.12), channel_id=1, source_target_pairs={{0,5},{1,4},{2,7},{3,6},{4,1},{5,0},{6,3},{7,2},{8,13},{9,12},{10,... | collective-permute-start | bytes 196616 | tf_op jit(solution)/shard_map/ppermute | solution.py:249
  9.1 3.1 %shard_map.57 = (f32[512,512]{1,0:T(8,128)S(1)}, f32[384,256]{1,0:T(8,128)S(1)}, f32[384,256]{1,0:T(8,128)S(1)}) custom-call(f32[1024,1024]{1,0:T(8,128)S(1)} %copy-done.2, f32[1024,512]{1,0:T(8,128)S(1)} %copy-done.3, f32[3,1024,128]{2,1,0:T(8,128)S(1)} %copy-done.4, f32[512,512]{1,0:T(8,128)S(1)} %shard_map.56.first_ref), custom_call_target="tpu_custom_call" | custom-call | tf_op jit(solution)/shard_map/pallas_call | solution.py:40
  12.2 0.0 collective-permute-done.2.pairs_x_ref
  12.2 0.3 shard_map.59.fix_ref
  12.5 0.0 collective-permute-done.1.last_z_ref
  12.5 0.5 %collective-permute-start.3 = (f32[384,256]{1,0:T(8,128)S(1)}, f32[384,256]{1,0:T(8,128)S(1)}, u32[]{:S(2)}, u32[]{:S(2)}) collective-permute-start(f32[384,256]{1,0:T(8,128)S(1)} %get-tuple-element.33), channel_id=1, source_target_pairs={{0,1},{1,0},{2,3},{3,2},{4,5},{5,4},{6,7},{7,6},{8,9},{9,8},{10,11... | collective-permute-start | bytes 1179656 | tf_op jit(solution)/shard_map/ppermute | solution.py:239
  12.9 0.1 collective-permute-start.4
  13.0 0.2 shard_map.61.fix_ref
  13.3 0.5 %collective-permute-start.5 = (f32[128,128]{1,0:T(8,128)S(1)}, f32[128,128]{1,0:T(8,128)S(1)}, u32[]{:S(2)}, u32[]{:S(2)}) collective-permute-start(f32[128,128]{1,0:T(8,128)S(1)} %shard_map.61.fix_ref), channel_id=1, source_target_pairs={{0,1},{1,0},{2,3},{3,2},{4,5},{5,4},{6,7},{7,6},{8,9},{9,8},{10,11... | collective-permute-start | bytes 196616 | tf_op jit(solution)/shard_map/ppermute | solution.py:239
  13.7 0.7 %collective-permute-done.4.fix_other_ref = f32[256,128]{1,0:T(8,128)S(1)} collective-permute-done((f32[256,128]{1,0:T(8,128)S(1)}, f32[256,128]{1,0:T(8,128)S(1)}, u32[]{:S(2)}, u32[]{:S(2)}) %collective-permute-start.4) | collective-permute-done | bytes 131104 | tf_op jit(solution)/shard_map/ppermute | solution.py:239
  14.5 0.0 collective-permute-done.3.recv_ref
  14.5 0.3 shard_map.60
  14.7 0.0 collective-permute-done.5.fix_other_ref
  14.7 0.2 shard_map.62.refs_0_
  14.9 0.9 %collective-permute-start.8 = (f32[128,256]{1,0:T(8,128)S(1)}, f32[128,256]{1,0:T(8,128)S(1)}, u32[]{:S(2)}, u32[]{:S(2)}) collective-permute-start(f32[128,256]{1,0:T(8,128)S(1)} %shard_map.62.refs_0_), channel_id=1, source_target_pairs={{0,4},{1,3},{2,6},{3,1},{4,0},{5,7},{6,2},{7,5},{8,12},{9,11},{10,... | collective-permute-start | bytes 393224 | tf_op jit(solution)/shard_map/ppermute | solution.py:249
  15.9 1.6 %collective-permute-start.7 = (f32[128,256]{1,0:T(8,128)S(1)}, f32[128,256]{1,0:T(8,128)S(1)}, u32[]{:S(2)}, u32[]{:S(2)}) collective-permute-start(f32[128,256]{1,0:T(8,128)S(1)} %shard_map.65), channel_id=1, source_target_pairs={{0,2},{2,0},{4,6},{6,4},{8,10},{10,8},{12,14},{14,12},{1,3},{3,1},... | collective-permute-start | bytes 393224 | tf_op jit(solution)/shard_map/ppermute | solution.py:235
  17.5 0.6 %shard_map.63.refs_0_.top_ref = f32[2,1024,128]{2,1,0:T(8,128)S(1)} custom-call(f32[3,1024,128]{2,1,0:T(8,128)S(1)} %copy-done.1, f32[1792,256]{1,0:T(8,128)S(1)} %copy-done), custom_call_target="tpu_custom_call" | custom-call | tf_op jit(solution)/shard_map/pallas_call | solution.py:40
  18.0 1.9 %collective-permute-done.8 = f32[128,256]{1,0:T(8,128)S(1)} collective-permute-done((f32[128,256]{1,0:T(8,128)S(1)}, f32[128,256]{1,0:T(8,128)S(1)}, u32[]{:S(2)}, u32[]{:S(2)}) %collective-permute-start.8) | collective-permute-done | bytes 131104 | tf_op jit(solution)/shard_map/ppermute | solution.py:249
  20.0 1.6 %collective-permute-start.9 = (f32[128,256]{1,0:T(8,128)S(1)}, f32[128,256]{1,0:T(8,128)S(1)}, u32[]{:S(2)}, u32[]{:S(2)}) collective-permute-start(f32[128,256]{1,0:T(8,128)S(1)} %add.13), channel_id=1, source_target_pairs={{0,2},{1,5},{2,0},{3,7},{4,6},{5,1},{6,4},{7,3},{8,10},{9,13},{10,... | collective-permute-start | bytes 393224 | tf_op jit(solution)/shard_map/ppermute | solution.py:249
  21.6 0.6 %collective-permute-done.7 = f32[128,256]{1,0:T(8,128)S(1)} collective-permute-done((f32[128,256]{1,0:T(8,128)S(1)}, f32[128,256]{1,0:T(8,128)S(1)}, u32[]{:S(2)}, u32[]{:S(2)}) %collective-permute-start.7) | collective-permute-done | bytes 131104 | tf_op jit(solution)/shard_map/ppermute | solution.py:235
  22.2 0.7 %collective-permute-start.10 = (f32[128,256]{1,0:T(8,128)S(1)}, f32[128,256]{1,0:T(8,128)S(1)}, u32[]{:S(2)}, u32[]{:S(2)}) collective-permute-start(f32[128,256]{1,0:T(8,128)S(1)} %add.14.v_ref), channel_id=1, source_target_pairs={{0,4},{2,6},{4,0},{6,2},{8,12},{10,14},{12,8},{14,10},{1,5},{3,7},... | collective-permute-start | bytes 393224 | tf_op jit(solution)/shard_map/ppermute | solution.py:235
  22.9 1.6 %collective-permute-start.6 = (f32[128,256]{1,0:T(8,128)S(1)}, f32[128,256]{1,0:T(8,128)S(1)}, u32[]{:S(2)}, u32[]{:S(2)}) collective-permute-start(f32[128,256]{1,0:T(8,128)S(1)} %shard_map.64.q_ref), channel_id=1, source_target_pairs={{0,2},{2,0},{4,6},{6,4},{8,10},{10,8},{12,14},{14,12},{1,3},{3,1},... | collective-permute-start | bytes 393224 | tf_op jit(solution)/shard_map/ppermute | solution.py:235
  24.5 0.7 %collective-permute-done.9 = f32[128,256]{1,0:T(8,128)S(1)} collective-permute-done((f32[128,256]{1,0:T(8,128)S(1)}, f32[128,256]{1,0:T(8,128)S(1)}, u32[]{:S(2)}, u32[]{:S(2)}) %collective-permute-start.9) | collective-permute-done | bytes 131104 | tf_op jit(solution)/shard_map/ppermute | solution.py:249
  25.2 2.6 %collective-permute-start.11 = (f32[128,256]{1,0:T(8,128)S(1)}, f32[128,256]{1,0:T(8,128)S(1)}, u32[]{:S(2)}, u32[]{:S(2)}) collective-permute-start(f32[128,256]{1,0:T(8,128)S(1)} %add.15.w_ref), channel_id=1, source_target_pairs={{0,8},{2,10},{4,12},{6,14},{8,0},{10,2},{12,4},{14,6},{1,9},{3,11}... | collective-permute-start | bytes 393224 | tf_op jit(solution)/shard_map/ppermute | solution.py:235
  27.8 1.2 %collective-permute-done.10.vz_ref = f32[128,256]{1,0:T(8,128)S(1)} collective-permute-done((f32[128,256]{1,0:T(8,128)S(1)}, f32[128,256]{1,0:T(8,128)S(1)}, u32[]{:S(2)}, u32[]{:S(2)}) %collective-permute-start.10) | collective-permute-done | bytes 131104 | tf_op jit(solution)/shard_map/ppermute | solution.py:235
  29.0 1.0 %shard_map.66 = (f32[128,256]{1,0:T(8,128)S(1)}, f32[1024,256]{1,0:T(8,128)S(1)}) custom-call(f32[128,256]{1,0:T(8,128)S(1)} %add.14.v_ref, f32[128,256]{1,0:T(8,128)S(1)} %collective-permute-done.10.vz_ref, f32[1792,256]{1,0:T(8,128)S(1)} %copy-done, f32[512,512]{1,0:T(8,128)S(1)} %shard_map.56.first_ref, f32[512,512]{1,0:T(8,128)S(1)} %get-tuple-element.43.last_ref, ...), custom_call_target="tpu_custom_call" | custom-call | tf_op jit(solution)/shard_map/pallas_call | solution.py:40
  30.0 0.1 collective-permute-start.12
  30.1 0.0 collective-permute-done.6.qx_ref
  30.1 1.0 %shard_map.67 = (f32[128,256]{1,0:T(8,128)S(1)}, f32[1024,256]{1,0:T(8,128)S(1)}) custom-call(f32[128,256]{1,0:T(8,128)S(1)} %shard_map.64.q_ref, f32[128,256]{1,0:T(8,128)S(1)} %collective-permute-done.6.qx_ref, f32[1792,256]{1,0:T(8,128)S(1)} %copy-done, f32[1024,256]{1,0:T(8,128)S(1)} %get-tuple-element.44.field_ref, f32[3,1024,128]{2,1,0:T(8,128)S(1)} %copy-done.1, ...), custom_call_target="tpu_custom_call" | custom-call | tf_op jit(solution)/shard_map/pallas_call | solution.py:40
  31.1 0.6 %collective-permute-start.13 = (f32[128,256]{1,0:T(8,128)S(1)}, f32[128,256]{1,0:T(8,128)S(1)}, u32[]{:S(2)}, u32[]{:S(2)}) collective-permute-start(f32[128,256]{1,0:T(8,128)S(1)} %get-tuple-element.47), channel_id=1, source_target_pairs={{0,1},{1,0},{2,3},{3,2},{4,5},{5,4},{6,7},{7,6},{8,9},{9,8},{10,11... | collective-permute-start | bytes 393224 | tf_op jit(solution)/shard_map/ppermute | solution.py:239
  31.6 0.1 collective-permute-start.14
  31.7 1.6 %collective-permute-done.11.far_ref = f32[128,256]{1,0:T(8,128)S(1)} collective-permute-done((f32[128,256]{1,0:T(8,128)S(1)}, f32[128,256]{1,0:T(8,128)S(1)}, u32[]{:S(2)}, u32[]{:S(2)}) %collective-permute-start.11) | collective-permute-done | bytes 131104 | tf_op jit(solution)/shard_map/ppermute | solution.py:235
  33.3 0.0 collective-permute-start.15
  33.3 0.0 collective-permute-done.13.refs_1_
  33.3 0.0 collective-permute-done.12.refs_0_
  33.3 1.0 %shard_map.68 = (f32[1024,256]{1,0:T(8,128)S(1)}, f32[1024,256]{1,0:T(8,128)S(1)}) custom-call(f32[1024,256]{1,0:T(8,128)S(1)} %get-tuple-element.45.own_ref, f32[512,512]{1,0:T(8,128)S(1)} %shard_map.56.first_ref, f32[512,512]{1,0:T(8,128)S(1)} %get-tuple-element.43.last_ref, f32[3,1024,128]{2,1,0:T(8,128)S(1)} %copy-done.1, ...), custom_call_target="tpu_custom_call" | custom-call | tf_op jit(solution)/shard_map/pallas_call | solution.py:40
  34.4 0.0 collective-permute-done.14.w_ref
  34.4 0.3 collective-permute-done.15.far_ref
  34.7 1.4 %shard_map.69 = f32[1024,512]{1,0:T(8,128)} custom-call(f32[1024,256]{1,0:T(8,128)S(1)} %get-tuple-element.48.own_ref, f32[1024,256]{1,0:T(8,128)S(1)} %get-tuple-element.49.less_ref, f32[2,1024,128]{2,1,0:T(8,128)S(1)} %shard_map.63.refs_0_.top_ref, f32[128,256]{1,0:T(8,128)S(1)} %collective-permute-done.14.w_ref, ...), custom_call_target="tpu_custom_call" | custom-call | tf_op jit(solution)/shard_map/pallas_call | solution.py:40
  (13 shorter events, 0.1 us)
Async XLA Ops:
  0.0 4.2 %copy-start.1 = (f32[3,1024,128]{2,1,0:T(8,128)S(1)}, f32[3,1024,128]{2,1,0:T(8,128)}, u32[]{:S(2)}) copy-start(f32[3,1024,128]{2,1,0:T(8,128)} %row_ref.9) | copy-start | bytes 4718596
  0.0 4.3 %copy-start.4 = (f32[3,1024,128]{2,1,0:T(8,128)S(1)}, f32[3,1024,128]{2,1,0:T(8,128)}, u32[]{:S(2)}) copy-start(f32[3,1024,128]{2,1,0:T(8,128)} %dual_ref.3) | copy-start | bytes 4718596
  0.0 5.3 %copy-start.2 = (f32[1024,1024]{1,0:T(8,128)S(1)}, f32[1024,1024]{1,0:T(8,128)}, u32[]{:S(2)}) copy-start(f32[1024,1024]{1,0:T(8,128)} %leaf_ref.3) | copy-start | bytes 12582916
  1.8 3.5 %copy-start.3 = (f32[1024,512]{1,0:T(8,128)S(1)}, f32[1024,512]{1,0:T(8,128)}, u32[]{:S(2)}) copy-start(f32[1024,512]{1,0:T(8,128)} %right_ref.1) | copy-start | bytes 6291460
  1.8 5.3 %collective-permute-start = (f32[128,128]{1,0:T(8,128)S(1)}, f32[128,128]{1,0:T(8,128)S(1)}, u32[]{:S(2)}, u32[]{:S(2)}) collective-permute-start(f32[128,128]{1,0:T(8,128)S(1)} %shard_map.55.last_ref), channel_id=1, source_target_pairs={{0,3},{1,2},{2,1},{3,0},{4,7},{5,6},{6,5},{7,4},{8,11},{9,10},{10,... | collective-permute-start | bytes 196616 | tf_op jit(solution)/shard_map/ppermute | solution.py:249
  4.9 7.3 %collective-permute-start.2 = (f32[256,128]{1,0:T(8,128)S(1)}, f32[256,128]{1,0:T(8,128)S(1)}, u32[]{:S(2)}, u32[]{:S(2)}) collective-permute-start(f32[256,128]{1,0:T(8,128)S(1)} %shard_map.58.pairs_ref), channel_id=1, source_target_pairs={{0,3},{1,2},{2,1},{3,0},{4,7},{5,6},{6,5},{7,4},{8,11},{9,10},{10,... | collective-permute-start | bytes 393224 | tf_op jit(solution)/shard_map/ppermute | solution.py:249
  7.1 5.0 %copy-start = (f32[1792,256]{1,0:T(8,128)S(1)}, f32[1792,256]{1,0:T(8,128)}, u32[]{:S(2)}) copy-start(f32[1792,256]{1,0:T(8,128)} %cores_ref.8) | copy-start | bytes 5505028
  7.1 5.3 %collective-permute-start.1 = (f32[128,128]{1,0:T(8,128)S(1)}, f32[128,128]{1,0:T(8,128)S(1)}, u32[]{:S(2)}, u32[]{:S(2)}) collective-permute-start(f32[128,128]{1,0:T(8,128)S(1)} %add.12), channel_id=1, source_target_pairs={{0,5},{1,4},{2,7},{3,6},{4,1},{5,0},{6,3},{7,2},{8,13},{9,12},{10,... | collective-permute-start | bytes 196616 | tf_op jit(solution)/shard_map/ppermute | solution.py:249
  12.5 2.0 %collective-permute-start.3 = (f32[384,256]{1,0:T(8,128)S(1)}, f32[384,256]{1,0:T(8,128)S(1)}, u32[]{:S(2)}, u32[]{:S(2)}) collective-permute-start(f32[384,256]{1,0:T(8,128)S(1)} %get-tuple-element.33), channel_id=1, source_target_pairs={{0,1},{1,0},{2,3},{3,2},{4,5},{5,4},{6,7},{7,6},{8,9},{9,8},{10,11... | collective-permute-start | bytes 1179656 | tf_op jit(solution)/shard_map/ppermute | solution.py:239
  12.9 1.5 %collective-permute-start.4 = (f32[256,128]{1,0:T(8,128)S(1)}, f32[256,128]{1,0:T(8,128)S(1)}, u32[]{:S(2)}, u32[]{:S(2)}) collective-permute-start(f32[256,128]{1,0:T(8,128)S(1)} %shard_map.59.fix_ref), channel_id=1, source_target_pairs={{0,1},{1,0},{2,3},{3,2},{4,5},{5,4},{6,7},{7,6},{8,9},{9,8},{10,11... | collective-permute-start | bytes 393224 | tf_op jit(solution)/shard_map/ppermute | solution.py:239
  13.3 1.5 %collective-permute-start.5 = (f32[128,128]{1,0:T(8,128)S(1)}, f32[128,128]{1,0:T(8,128)S(1)}, u32[]{:S(2)}, u32[]{:S(2)}) collective-permute-start(f32[128,128]{1,0:T(8,128)S(1)} %shard_map.61.fix_ref), channel_id=1, source_target_pairs={{0,1},{1,0},{2,3},{3,2},{4,5},{5,4},{6,7},{7,6},{8,9},{9,8},{10,11... | collective-permute-start | bytes 196616 | tf_op jit(solution)/shard_map/ppermute | solution.py:239
  14.9 5.0 %collective-permute-start.8 = (f32[128,256]{1,0:T(8,128)S(1)}, f32[128,256]{1,0:T(8,128)S(1)}, u32[]{:S(2)}, u32[]{:S(2)}) collective-permute-start(f32[128,256]{1,0:T(8,128)S(1)} %shard_map.62.refs_0_), channel_id=1, source_target_pairs={{0,4},{1,3},{2,6},{3,1},{4,0},{5,7},{6,2},{7,5},{8,12},{9,11},{10,... | collective-permute-start | bytes 393224 | tf_op jit(solution)/shard_map/ppermute | solution.py:249
  15.9 6.3 %collective-permute-start.7 = (f32[128,256]{1,0:T(8,128)S(1)}, f32[128,256]{1,0:T(8,128)S(1)}, u32[]{:S(2)}, u32[]{:S(2)}) collective-permute-start(f32[128,256]{1,0:T(8,128)S(1)} %shard_map.65), channel_id=1, source_target_pairs={{0,2},{2,0},{4,6},{6,4},{8,10},{10,8},{12,14},{14,12},{1,3},{3,1},... | collective-permute-start | bytes 393224 | tf_op jit(solution)/shard_map/ppermute | solution.py:235
  20.0 5.2 %collective-permute-start.9 = (f32[128,256]{1,0:T(8,128)S(1)}, f32[128,256]{1,0:T(8,128)S(1)}, u32[]{:S(2)}, u32[]{:S(2)}) collective-permute-start(f32[128,256]{1,0:T(8,128)S(1)} %add.13), channel_id=1, source_target_pairs={{0,2},{1,5},{2,0},{3,7},{4,6},{5,1},{6,4},{7,3},{8,10},{9,13},{10,... | collective-permute-start | bytes 393224 | tf_op jit(solution)/shard_map/ppermute | solution.py:249
  22.2 6.8 %collective-permute-start.10 = (f32[128,256]{1,0:T(8,128)S(1)}, f32[128,256]{1,0:T(8,128)S(1)}, u32[]{:S(2)}, u32[]{:S(2)}) collective-permute-start(f32[128,256]{1,0:T(8,128)S(1)} %add.14.v_ref), channel_id=1, source_target_pairs={{0,4},{2,6},{4,0},{6,2},{8,12},{10,14},{12,8},{14,10},{1,5},{3,7},... | collective-permute-start | bytes 393224 | tf_op jit(solution)/shard_map/ppermute | solution.py:235
  22.9 7.1 %collective-permute-start.6 = (f32[128,256]{1,0:T(8,128)S(1)}, f32[128,256]{1,0:T(8,128)S(1)}, u32[]{:S(2)}, u32[]{:S(2)}) collective-permute-start(f32[128,256]{1,0:T(8,128)S(1)} %shard_map.64.q_ref), channel_id=1, source_target_pairs={{0,2},{2,0},{4,6},{6,4},{8,10},{10,8},{12,14},{14,12},{1,3},{3,1},... | collective-permute-start | bytes 393224 | tf_op jit(solution)/shard_map/ppermute | solution.py:235
  25.2 8.2 %collective-permute-start.11 = (f32[128,256]{1,0:T(8,128)S(1)}, f32[128,256]{1,0:T(8,128)S(1)}, u32[]{:S(2)}, u32[]{:S(2)}) collective-permute-start(f32[128,256]{1,0:T(8,128)S(1)} %add.15.w_ref), channel_id=1, source_target_pairs={{0,8},{2,10},{4,12},{6,14},{8,0},{10,2},{12,4},{14,6},{1,9},{3,11}... | collective-permute-start | bytes 393224 | tf_op jit(solution)/shard_map/ppermute | solution.py:235
  30.0 3.4 %collective-permute-start.12 = (f32[128,256]{1,0:T(8,128)S(1)}, f32[128,256]{1,0:T(8,128)S(1)}, u32[]{:S(2)}, u32[]{:S(2)}) collective-permute-start(f32[128,256]{1,0:T(8,128)S(1)} %get-tuple-element.46), channel_id=1, source_target_pairs={{0,1},{1,0},{2,3},{3,2},{4,5},{5,4},{6,7},{7,6},{8,9},{9,8},{10,11... | collective-permute-start | bytes 393224 | tf_op jit(solution)/shard_map/ppermute | solution.py:239
  31.1 2.3 %collective-permute-start.13 = (f32[128,256]{1,0:T(8,128)S(1)}, f32[128,256]{1,0:T(8,128)S(1)}, u32[]{:S(2)}, u32[]{:S(2)}) collective-permute-start(f32[128,256]{1,0:T(8,128)S(1)} %get-tuple-element.47), channel_id=1, source_target_pairs={{0,1},{1,0},{2,3},{3,2},{4,5},{5,4},{6,7},{7,6},{8,9},{9,8},{10,11... | collective-permute-start | bytes 393224 | tf_op jit(solution)/shard_map/ppermute | solution.py:239
  31.6 2.7 %collective-permute-start.14 = (f32[128,256]{1,0:T(8,128)S(1)}, f32[128,256]{1,0:T(8,128)S(1)}, u32[]{:S(2)}, u32[]{:S(2)}) collective-permute-start(f32[128,256]{1,0:T(8,128)S(1)} %add.15.w_ref), channel_id=1, source_target_pairs={{0,1},{1,0},{2,3},{3,2},{4,5},{5,4},{6,7},{7,6},{8,9},{9,8},{10,11... | collective-permute-start | bytes 393224 | tf_op jit(solution)/shard_map/ppermute | solution.py:239
  33.3 1.3 %collective-permute-start.15 = (f32[128,256]{1,0:T(8,128)S(1)}, f32[128,256]{1,0:T(8,128)S(1)}, u32[]{:S(2)}, u32[]{:S(2)}) collective-permute-start(f32[128,256]{1,0:T(8,128)S(1)} %collective-permute-done.11.far_ref), channel_id=1, source_target_pairs={{0,1},{1,0},{2,3},{3,2},{4,5},{5,4},{6,7},{7,6},{8,9},{9,8},{10,11... | collective-permute-start | bytes 393224 | tf_op jit(solution)/shard_map/ppermute | solution.py:239

commit v8 on v7

--- a/solution.py
+++ b/solution.py
@@ -84,8 +84,8 @@
 
 def pair_products(dual_ref, row_ref, last_ref, out_ref):
     rank = row_ref.shape[2]
-    out_ref[:rank] = dot_t(dual_ref[1], row_ref[2])
-    out_ref[rank:] = dot_t(dual_ref[0], row_ref[2])
+    both = dot_t(jnp.concatenate([dual_ref[1], dual_ref[0]], 1), row_ref[2])
+    out_ref[...] = both
 
 
 def leaf_rows(start, leaf_ref, right_ref, field_ref):
@@ -313,10 +313,9 @@
         functools.partial(top_matrix, rest), shape(2, rows, rank),
         (row_bases, after(woodbury_cores, w)), 0,
     )
-    w = w_mid = w + after(swap_crossed(w, bit2, bit3), top, q)
-    q = tie(q, top)
-    q_x = swap_wide(q, bit3)
+    w = w_mid = w + after(swap_crossed(w, bit2, bit3), top)
     v = v + after(v_x, w_mid)
+    q_x = swap_wide(after(q, v), bit3)
     v_z = swap_wide(v, bit2)
     w = w + after(swap_crossed(w, bit3, bit2), v)
     far = swap_wide(w, bit1)

time: 36.2 us -> 36.2 us (level)
    pallas_call x15 -> x14, Pallas kernels: 13.2 us -> 13.2 us  [call(): pl.pallas_call(body, in_specs=in_specs or [VMEM] * len(args), out_specs=j...]
where the time goes in v8:
time: 36.2 us; the launch traced here: 36.1 us
  starting transfers between devices  15.4 us (43%)
  Pallas kernels  13.2 us (36%)
  waiting for transfers between devices  7.18 us (20%)
    pallas_call x14, Pallas kernels, call(): pl.pallas_call(body, in_specs=in_specs or [VMEM] * len(args), out_specs=j...  13.2 us
    ppermute x5, starting transfers between devices, swap_crossed(): return lax.ppermute(x, ('wide', 'narrow'), route)  7.28 us
    ppermute x4, starting transfers between devices, swap_wide(): return lax.ppermute(x, 'wide', [(w, w ^ 1 << bit) for w in range(count)])  6.43 us
    ppermute x4, waiting for transfers between devices, swap_wide(): return lax.ppermute(x, 'wide', [(w, w ^ 1 << bit) for w in range(count)])  3.4 us
    ppermute x5, waiting for transfers between devices, swap_crossed(): return lax.ppermute(x, ('wide', 'narrow'), route)  2.71 us
    ppermute x7, starting transfers between devices, swap_narrow(): return lax.ppermute(x, 'narrow', [(0, 1), (1, 0)])  1.73 us
    ppermute x7, waiting for transfers between devices, swap_narrow(): return lax.ppermute(x, 'narrow', [(0, 1), (1, 0)])  1.07 us
  transfers between devices with their start and end apart: 16, of which 7 were waited for; matrix products, arithmetic and copies ran while one was open for 0% of the time, Pallas kernels for 27%

profile of v8, /device:TPU:0, one launch (start us, length us, event | category | flops | bytes accessed | tf_op | source)
XLA Modules:
  0.0 36.1 jit_solution(4860430026625456703)
XLA Ops:
  0.0 1.8 %shard_map.55.last_ref = f32[128,128]{1,0:T(8,128)S(1)} custom-call(f32[3,1024,128]{2,1,0:T(8,128)} %dual_ref.3, f32[3,1024,128]{2,1,0:T(8,128)} %row_ref.9), custom_call_target="tpu_custom_call" | custom-call | flops 16106127360 | tf_op jit(solution)/shard_map/pallas_call | solution.py:40
  1.8 0.0 copy-start.3
  1.8 2.4 %collective-permute-start = (f32[128,128]{1,0:T(8,128)S(1)}, f32[128,128]{1,0:T(8,128)S(1)}, u32[]{:S(2)}, u32[]{:S(2)}) collective-permute-start(f32[128,128]{1,0:T(8,128)S(1)} %shard_map.55.last_ref), channel_id=1, source_target_pairs={{0,3},{1,2},{2,1},{3,0},{4,7},{5,6},{6,5},{7,4},{8,11},{9,10},{10,... | collective-permute-start | bytes 196616 | tf_op jit(solution)/shard_map/ppermute | solution.py:249
  4.3 0.6 %shard_map.58.pairs_ref = f32[256,128]{1,0:T(8,128)S(1)} custom-call(f32[3,1024,128]{2,1,0:T(8,128)S(1)} %copy-done.4, f32[3,1024,128]{2,1,0:T(8,128)S(1)} %copy-done.1, f32[128,128]{1,0:T(8,128)S(1)} %shard_map.55.last_ref), custom_call_target="tpu_custom_call" | custom-call | flops 67108864 | tf_op jit(solution)/shard_map/pallas_call | solution.py:40
  4.9 0.4 %collective-permute-start.2 = (f32[256,128]{1,0:T(8,128)S(1)}, f32[256,128]{1,0:T(8,128)S(1)}, u32[]{:S(2)}, u32[]{:S(2)}) collective-permute-start(f32[256,128]{1,0:T(8,128)S(1)} %shard_map.58.pairs_ref), channel_id=1, source_target_pairs={{0,3},{1,2},{2,1},{3,0},{4,7},{5,6},{6,5},{7,4},{8,11},{9,10},{10,... | collective-permute-start | bytes 393224 | tf_op jit(solution)/shard_map/ppermute | solution.py:249
  5.3 0.0 copy-done.3
  5.3 1.8 %shard_map.56.first_ref = f32[512,512]{1,0:T(8,128)S(1)} custom-call(f32[1024,1024]{1,0:T(8,128)S(1)} %copy-done.2, f32[1024,512]{1,0:T(8,128)S(1)} %copy-done.3), custom_call_target="tpu_custom_call" | custom-call | flops 1610612736 | tf_op jit(solution)/shard_map/pallas_call | solution.py:40
  7.1 0.0 collective-permute-done.last_x_ref
  7.1 0.0 copy-start
  7.1 1.9 %collective-permute-start.1 = (f32[128,128]{1,0:T(8,128)S(1)}, f32[128,128]{1,0:T(8,128)S(1)}, u32[]{:S(2)}, u32[]{:S(2)}) collective-permute-start(f32[128,128]{1,0:T(8,128)S(1)} %add.12), channel_id=1, source_target_pairs={{0,5},{1,4},{2,7},{3,6},{4,1},{5,0},{6,3},{7,2},{8,13},{9,12},{10,... | collective-permute-start | bytes 196616 | tf_op jit(solution)/shard_map/ppermute | solution.py:249
  9.1 3.1 %shard_map.57 = (f32[512,512]{1,0:T(8,128)S(1)}, f32[384,256]{1,0:T(8,128)S(1)}, f32[384,256]{1,0:T(8,128)S(1)}) custom-call(f32[1024,1024]{1,0:T(8,128)S(1)} %copy-done.2, f32[1024,512]{1,0:T(8,128)S(1)} %copy-done.3, f32[3,1024,128]{2,1,0:T(8,128)S(1)} %copy-done.4, f32[512,512]{1,0:T(8,128)S(1)} %shard_map.56.first_ref), custom_call_target="tpu_custom_call" | custom-call | tf_op jit(solution)/shard_map/pallas_call | solution.py:40
  12.2 0.0 collective-permute-done.2.pairs_x_ref
  12.2 0.3 shard_map.59.fix_ref
  12.5 0.0 collective-permute-done.1.last_z_ref
  12.5 0.5 %collective-permute-start.3 = (f32[384,256]{1,0:T(8,128)S(1)}, f32[384,256]{1,0:T(8,128)S(1)}, u32[]{:S(2)}, u32[]{:S(2)}) collective-permute-start(f32[384,256]{1,0:T(8,128)S(1)} %get-tuple-element.34), channel_id=1, source_target_pairs={{0,1},{1,0},{2,3},{3,2},{4,5},{5,4},{6,7},{7,6},{8,9},{9,8},{10,11... | collective-permute-start | bytes 1179656 | tf_op jit(solution)/shard_map/ppermute | solution.py:239
  12.9 0.1 collective-permute-start.4
  13.0 0.2 shard_map.61.fix_ref
  13.3 0.5 %collective-permute-start.5 = (f32[128,128]{1,0:T(8,128)S(1)}, f32[128,128]{1,0:T(8,128)S(1)}, u32[]{:S(2)}, u32[]{:S(2)}) collective-permute-start(f32[128,128]{1,0:T(8,128)S(1)} %shard_map.61.fix_ref), channel_id=1, source_target_pairs={{0,1},{1,0},{2,3},{3,2},{4,5},{5,4},{6,7},{7,6},{8,9},{9,8},{10,11... | collective-permute-start | bytes 196616 | tf_op jit(solution)/shard_map/ppermute | solution.py:239
  13.7 0.7 %collective-permute-done.4.fix_other_ref = f32[256,128]{1,0:T(8,128)S(1)} collective-permute-done((f32[256,128]{1,0:T(8,128)S(1)}, f32[256,128]{1,0:T(8,128)S(1)}, u32[]{:S(2)}, u32[]{:S(2)}) %collective-permute-start.4) | collective-permute-done | bytes 131104 | tf_op jit(solution)/shard_map/ppermute | solution.py:239
  14.5 0.0 collective-permute-done.3.recv_ref
  14.5 0.3 shard_map.60
  14.7 0.0 collective-permute-done.5.fix_other_ref
  14.7 0.2 shard_map.62.refs_0_
  14.9 0.9 %collective-permute-start.7 = (f32[128,256]{1,0:T(8,128)S(1)}, f32[128,256]{1,0:T(8,128)S(1)}, u32[]{:S(2)}, u32[]{:S(2)}) collective-permute-start(f32[128,256]{1,0:T(8,128)S(1)} %shard_map.62.refs_0_), channel_id=1, source_target_pairs={{0,4},{1,3},{2,6},{3,1},{4,0},{5,7},{6,2},{7,5},{8,12},{9,11},{10,... | collective-permute-start | bytes 393224 | tf_op jit(solution)/shard_map/ppermute | solution.py:249
  15.9 1.6 %collective-permute-start.6 = (f32[128,256]{1,0:T(8,128)S(1)}, f32[128,256]{1,0:T(8,128)S(1)}, u32[]{:S(2)}, u32[]{:S(2)}) collective-permute-start(f32[128,256]{1,0:T(8,128)S(1)} %shard_map.63), channel_id=1, source_target_pairs={{0,2},{2,0},{4,6},{6,4},{8,10},{10,8},{12,14},{14,12},{1,3},{3,1},... | collective-permute-start | bytes 393224 | tf_op jit(solution)/shard_map/ppermute | solution.py:235
  17.5 0.6 %shard_map.64.top_ref = f32[2,1024,128]{2,1,0:T(8,128)S(1)} custom-call(f32[3,1024,128]{2,1,0:T(8,128)S(1)} %copy-done.1, f32[1792,256]{1,0:T(8,128)S(1)} %copy-done), custom_call_target="tpu_custom_call" | custom-call | tf_op jit(solution)/shard_map/pallas_call | solution.py:40
  18.0 1.9 %collective-permute-done.7 = f32[128,256]{1,0:T(8,128)S(1)} collective-permute-done((f32[128,256]{1,0:T(8,128)S(1)}, f32[128,256]{1,0:T(8,128)S(1)}, u32[]{:S(2)}, u32[]{:S(2)}) %collective-permute-start.7) | collective-permute-done | bytes 131104 | tf_op jit(solution)/shard_map/ppermute | solution.py:249
  20.0 1.6 %collective-permute-start.9 = (f32[128,256]{1,0:T(8,128)S(1)}, f32[128,256]{1,0:T(8,128)S(1)}, u32[]{:S(2)}, u32[]{:S(2)}) collective-permute-start(f32[128,256]{1,0:T(8,128)S(1)} %add.13), channel_id=1, source_target_pairs={{0,2},{1,5},{2,0},{3,7},{4,6},{5,1},{6,4},{7,3},{8,10},{9,13},{10,... | collective-permute-start | bytes 393224 | tf_op jit(solution)/shard_map/ppermute | solution.py:249
  21.6 0.6 %collective-permute-done.6 = f32[128,256]{1,0:T(8,128)S(1)} collective-permute-done((f32[128,256]{1,0:T(8,128)S(1)}, f32[128,256]{1,0:T(8,128)S(1)}, u32[]{:S(2)}, u32[]{:S(2)}) %collective-permute-start.6) | collective-permute-done | bytes 131104 | tf_op jit(solution)/shard_map/ppermute | solution.py:235
  22.2 0.7 %collective-permute-start.10 = (f32[128,256]{1,0:T(8,128)S(1)}, f32[128,256]{1,0:T(8,128)S(1)}, u32[]{:S(2)}, u32[]{:S(2)}) collective-permute-start(f32[128,256]{1,0:T(8,128)S(1)} %add.14.v_ref), channel_id=1, source_target_pairs={{0,4},{2,6},{4,0},{6,2},{8,12},{10,14},{12,8},{14,10},{1,5},{3,7},... | collective-permute-start | bytes 393224 | tf_op jit(solution)/shard_map/ppermute | solution.py:235
  22.9 1.5 %collective-permute-start.8 = (f32[128,256]{1,0:T(8,128)S(1)}, f32[128,256]{1,0:T(8,128)S(1)}, u32[]{:S(2)}, u32[]{:S(2)}) collective-permute-start(f32[128,256]{1,0:T(8,128)S(1)} %get-tuple-element.42.q_ref), channel_id=1, source_target_pairs={{0,2},{2,0},{4,6},{6,4},{8,10},{10,8},{12,14},{14,12},{1,3},{3,1},... | collective-permute-start | bytes 393224 | tf_op jit(solution)/shard_map/ppermute | solution.py:235
  24.4 0.8 %collective-permute-done.9 = f32[128,256]{1,0:T(8,128)S(1)} collective-permute-done((f32[128,256]{1,0:T(8,128)S(1)}, f32[128,256]{1,0:T(8,128)S(1)}, u32[]{:S(2)}, u32[]{:S(2)}) %collective-permute-start.9) | collective-permute-done | bytes 131104 | tf_op jit(solution)/shard_map/ppermute | solution.py:249
  25.2 2.6 %collective-permute-start.11 = (f32[128,256]{1,0:T(8,128)S(1)}, f32[128,256]{1,0:T(8,128)S(1)}, u32[]{:S(2)}, u32[]{:S(2)}) collective-permute-start(f32[128,256]{1,0:T(8,128)S(1)} %add.15.w_ref), channel_id=1, source_target_pairs={{0,8},{2,10},{4,12},{6,14},{8,0},{10,2},{12,4},{14,6},{1,9},{3,11}... | collective-permute-start | bytes 393224 | tf_op jit(solution)/shard_map/ppermute | solution.py:235
  27.8 1.1 %collective-permute-done.10.vz_ref = f32[128,256]{1,0:T(8,128)S(1)} collective-permute-done((f32[128,256]{1,0:T(8,128)S(1)}, f32[128,256]{1,0:T(8,128)S(1)}, u32[]{:S(2)}, u32[]{:S(2)}) %collective-permute-start.10) | collective-permute-done | bytes 131104 | tf_op jit(solution)/shard_map/ppermute | solution.py:235
  29.0 1.0 %shard_map.65 = (f32[128,256]{1,0:T(8,128)S(1)}, f32[1024,256]{1,0:T(8,128)S(1)}) custom-call(f32[128,256]{1,0:T(8,128)S(1)} %add.14.v_ref, f32[128,256]{1,0:T(8,128)S(1)} %collective-permute-done.10.vz_ref, f32[1792,256]{1,0:T(8,128)S(1)} %copy-done, f32[512,512]{1,0:T(8,128)S(1)} %shard_map.56.first_ref, f32[512,512]{1,0:T(8,128)S(1)} %get-tuple-element.45.last_ref, ...), custom_call_target="tpu_custom_call" | custom-call | tf_op jit(solution)/shard_map/pallas_call | solution.py:40
  30.0 0.1 collective-permute-start.12
  30.1 0.0 collective-permute-done.8.qx_ref
  30.1 1.0 %shard_map.66 = (f32[128,256]{1,0:T(8,128)S(1)}, f32[1024,256]{1,0:T(8,128)S(1)}) custom-call(f32[128,256]{1,0:T(8,128)S(1)} %get-tuple-element.42.q_ref, f32[128,256]{1,0:T(8,128)S(1)} %collective-permute-done.8.qx_ref, f32[1792,256]{1,0:T(8,128)S(1)} %copy-done, f32[1024,256]{1,0:T(8,128)S(1)} %get-tuple-element.46.field_ref, ...), custom_call_target="tpu_custom_call" | custom-call | tf_op jit(solution)/shard_map/pallas_call | solution.py:40
  31.1 0.6 %collective-permute-start.13 = (f32[128,256]{1,0:T(8,128)S(1)}, f32[128,256]{1,0:T(8,128)S(1)}, u32[]{:S(2)}, u32[]{:S(2)}) collective-permute-start(f32[128,256]{1,0:T(8,128)S(1)} %get-tuple-element.49), channel_id=1, source_target_pairs={{0,1},{1,0},{2,3},{3,2},{4,5},{5,4},{6,7},{7,6},{8,9},{9,8},{10,11... | collective-permute-start | bytes 393224 | tf_op jit(solution)/shard_map/ppermute | solution.py:239
  31.6 0.1 collective-permute-start.14
  31.7 1.6 %collective-permute-done.11.far_ref = f32[128,256]{1,0:T(8,128)S(1)} collective-permute-done((f32[128,256]{1,0:T(8,128)S(1)}, f32[128,256]{1,0:T(8,128)S(1)}, u32[]{:S(2)}, u32[]{:S(2)}) %collective-permute-start.11) | collective-permute-done | bytes 131104 | tf_op jit(solution)/shard_map/ppermute | solution.py:235
  33.3 0.0 collective-permute-start.15
  33.4 0.0 collective-permute-done.13.refs_1_
  33.4 0.0 collective-permute-done.12.refs_0_
  33.4 1.0 %shard_map.67 = (f32[1024,256]{1,0:T(8,128)S(1)}, f32[1024,256]{1,0:T(8,128)S(1)}) custom-call(f32[1024,256]{1,0:T(8,128)S(1)} %get-tuple-element.47.own_ref, f32[512,512]{1,0:T(8,128)S(1)} %shard_map.56.first_ref, f32[512,512]{1,0:T(8,128)S(1)} %get-tuple-element.45.last_ref, f32[3,1024,128]{2,1,0:T(8,128)S(1)} %copy-done.1, ...), custom_call_target="tpu_custom_call" | custom-call | tf_op jit(solution)/shard_map/pallas_call | solution.py:40
  34.4 0.0 collective-permute-done.14.w_ref
  34.4 0.3 collective-permute-done.15.far_ref
  34.7 1.4 %shard_map.68 = f32[1024,512]{1,0:T(8,128)} custom-call(f32[1024,256]{1,0:T(8,128)S(1)} %get-tuple-element.50.own_ref, f32[1024,256]{1,0:T(8,128)S(1)} %get-tuple-element.51.less_ref, f32[2,1024,128]{2,1,0:T(8,128)S(1)} %shard_map.64.top_ref, f32[128,256]{1,0:T(8,128)S(1)} %collective-permute-done.14.w_ref, f32[128,256]{1,0:T(8,128)S(1)} %collective-permute-done.15.far_ref), custom_call_target="tpu_custom_call" | custom-call | tf_op jit(solution)/shard_map/pallas_call | solution.py:40
  (12 shorter events, 0.1 us)
Async XLA Ops:
  0.0 4.2 %copy-start.1 = (f32[3,1024,128]{2,1,0:T(8,128)S(1)}, f32[3,1024,128]{2,1,0:T(8,128)}, u32[]{:S(2)}) copy-start(f32[3,1024,128]{2,1,0:T(8,128)} %row_ref.9) | copy-start | bytes 4718596
  0.0 4.3 %copy-start.4 = (f32[3,1024,128]{2,1,0:T(8,128)S(1)}, f32[3,1024,128]{2,1,0:T(8,128)}, u32[]{:S(2)}) copy-start(f32[3,1024,128]{2,1,0:T(8,128)} %dual_ref.3) | copy-start | bytes 4718596
  0.0 5.3 %copy-start.2 = (f32[1024,1024]{1,0:T(8,128)S(1)}, f32[1024,1024]{1,0:T(8,128)}, u32[]{:S(2)}) copy-start(f32[1024,1024]{1,0:T(8,128)} %leaf_ref.3) | copy-start | bytes 12582916
  1.8 3.5 %copy-start.3 = (f32[1024,512]{1,0:T(8,128)S(1)}, f32[1024,512]{1,0:T(8,128)}, u32[]{:S(2)}) copy-start(f32[1024,512]{1,0:T(8,128)} %right_ref.1) | copy-start | bytes 6291460
  1.8 5.3 %collective-permute-start = (f32[128,128]{1,0:T(8,128)S(1)}, f32[128,128]{1,0:T(8,128)S(1)}, u32[]{:S(2)}, u32[]{:S(2)}) collective-permute-start(f32[128,128]{1,0:T(8,128)S(1)} %shard_map.55.last_ref), channel_id=1, source_target_pairs={{0,3},{1,2},{2,1},{3,0},{4,7},{5,6},{6,5},{7,4},{8,11},{9,10},{10,... | collective-permute-start | bytes 196616 | tf_op jit(solution)/shard_map/ppermute | solution.py:249
  4.9 7.3 %collective-permute-start.2 = (f32[256,128]{1,0:T(8,128)S(1)}, f32[256,128]{1,0:T(8,128)S(1)}, u32[]{:S(2)}, u32[]{:S(2)}) collective-permute-start(f32[256,128]{1,0:T(8,128)S(1)} %shard_map.58.pairs_ref), channel_id=1, source_target_pairs={{0,3},{1,2},{2,1},{3,0},{4,7},{5,6},{6,5},{7,4},{8,11},{9,10},{10,... | collective-permute-start | bytes 393224 | tf_op jit(solution)/shard_map/ppermute | solution.py:249
  7.1 5.1 %copy-start = (f32[1792,256]{1,0:T(8,128)S(1)}, f32[1792,256]{1,0:T(8,128)}, u32[]{:S(2)}) copy-start(f32[1792,256]{1,0:T(8,128)} %cores_ref.8) | copy-start | bytes 5505028
  7.1 5.3 %collective-permute-start.1 = (f32[128,128]{1,0:T(8,128)S(1)}, f32[128,128]{1,0:T(8,128)S(1)}, u32[]{:S(2)}, u32[]{:S(2)}) collective-permute-start(f32[128,128]{1,0:T(8,128)S(1)} %add.12), channel_id=1, source_target_pairs={{0,5},{1,4},{2,7},{3,6},{4,1},{5,0},{6,3},{7,2},{8,13},{9,12},{10,... | collective-permute-start | bytes 196616 | tf_op jit(solution)/shard_map/ppermute | solution.py:249
  12.5 2.0 %collective-permute-start.3 = (f32[384,256]{1,0:T(8,128)S(1)}, f32[384,256]{1,0:T(8,128)S(1)}, u32[]{:S(2)}, u32[]{:S(2)}) collective-permute-start(f32[384,256]{1,0:T(8,128)S(1)} %get-tuple-element.34), channel_id=1, source_target_pairs={{0,1},{1,0},{2,3},{3,2},{4,5},{5,4},{6,7},{7,6},{8,9},{9,8},{10,11... | collective-permute-start | bytes 1179656 | tf_op jit(solution)/shard_map/ppermute | solution.py:239
  12.9 1.5 %collective-permute-start.4 = (f32[256,128]{1,0:T(8,128)S(1)}, f32[256,128]{1,0:T(8,128)S(1)}, u32[]{:S(2)}, u32[]{:S(2)}) collective-permute-start(f32[256,128]{1,0:T(8,128)S(1)} %shard_map.59.fix_ref), channel_id=1, source_target_pairs={{0,1},{1,0},{2,3},{3,2},{4,5},{5,4},{6,7},{7,6},{8,9},{9,8},{10,11... | collective-permute-start | bytes 393224 | tf_op jit(solution)/shard_map/ppermute | solution.py:239
  13.3 1.5 %collective-permute-start.5 = (f32[128,128]{1,0:T(8,128)S(1)}, f32[128,128]{1,0:T(8,128)S(1)}, u32[]{:S(2)}, u32[]{:S(2)}) collective-permute-start(f32[128,128]{1,0:T(8,128)S(1)} %shard_map.61.fix_ref), channel_id=1, source_target_pairs={{0,1},{1,0},{2,3},{3,2},{4,5},{5,4},{6,7},{7,6},{8,9},{9,8},{10,11... | collective-permute-start | bytes 196616 | tf_op jit(solution)/shard_map/ppermute | solution.py:239
  14.9 5.0 %collective-permute-start.7 = (f32[128,256]{1,0:T(8,128)S(1)}, f32[128,256]{1,0:T(8,128)S(1)}, u32[]{:S(2)}, u32[]{:S(2)}) collective-permute-start(f32[128,256]{1,0:T(8,128)S(1)} %shard_map.62.refs_0_), channel_id=1, source_target_pairs={{0,4},{1,3},{2,6},{3,1},{4,0},{5,7},{6,2},{7,5},{8,12},{9,11},{10,... | collective-permute-start | bytes 393224 | tf_op jit(solution)/shard_map/ppermute | solution.py:249
  15.9 6.3 %collective-permute-start.6 = (f32[128,256]{1,0:T(8,128)S(1)}, f32[128,256]{1,0:T(8,128)S(1)}, u32[]{:S(2)}, u32[]{:S(2)}) collective-permute-start(f32[128,256]{1,0:T(8,128)S(1)} %shard_map.63), channel_id=1, source_target_pairs={{0,2},{2,0},{4,6},{6,4},{8,10},{10,8},{12,14},{14,12},{1,3},{3,1},... | collective-permute-start | bytes 393224 | tf_op jit(solution)/shard_map/ppermute | solution.py:235
  20.0 5.2 %collective-permute-start.9 = (f32[128,256]{1,0:T(8,128)S(1)}, f32[128,256]{1,0:T(8,128)S(1)}, u32[]{:S(2)}, u32[]{:S(2)}) collective-permute-start(f32[128,256]{1,0:T(8,128)S(1)} %add.13), channel_id=1, source_target_pairs={{0,2},{1,5},{2,0},{3,7},{4,6},{5,1},{6,4},{7,3},{8,10},{9,13},{10,... | collective-permute-start | bytes 393224 | tf_op jit(solution)/shard_map/ppermute | solution.py:249
  22.2 6.8 %collective-permute-start.10 = (f32[128,256]{1,0:T(8,128)S(1)}, f32[128,256]{1,0:T(8,128)S(1)}, u32[]{:S(2)}, u32[]{:S(2)}) collective-permute-start(f32[128,256]{1,0:T(8,128)S(1)} %add.14.v_ref), channel_id=1, source_target_pairs={{0,4},{2,6},{4,0},{6,2},{8,12},{10,14},{12,8},{14,10},{1,5},{3,7},... | collective-permute-start | bytes 393224 | tf_op jit(solution)/shard_map/ppermute | solution.py:235
  22.9 7.2 %collective-permute-start.8 = (f32[128,256]{1,0:T(8,128)S(1)}, f32[128,256]{1,0:T(8,128)S(1)}, u32[]{:S(2)}, u32[]{:S(2)}) collective-permute-start(f32[128,256]{1,0:T(8,128)S(1)} %get-tuple-element.42.q_ref), channel_id=1, source_target_pairs={{0,2},{2,0},{4,6},{6,4},{8,10},{10,8},{12,14},{14,12},{1,3},{3,1},... | collective-permute-start | bytes 393224 | tf_op jit(solution)/shard_map/ppermute | solution.py:235
  25.2 8.1 %collective-permute-start.11 = (f32[128,256]{1,0:T(8,128)S(1)}, f32[128,256]{1,0:T(8,128)S(1)}, u32[]{:S(2)}, u32[]{:S(2)}) collective-permute-start(f32[128,256]{1,0:T(8,128)S(1)} %add.15.w_ref), channel_id=1, source_target_pairs={{0,8},{2,10},{4,12},{6,14},{8,0},{10,2},{12,4},{14,6},{1,9},{3,11}... | collective-permute-start | bytes 393224 | tf_op jit(solution)/shard_map/ppermute | solution.py:235
  30.0 3.4 %collective-permute-start.12 = (f32[128,256]{1,0:T(8,128)S(1)}, f32[128,256]{1,0:T(8,128)S(1)}, u32[]{:S(2)}, u32[]{:S(2)}) collective-permute-start(f32[128,256]{1,0:T(8,128)S(1)} %get-tuple-element.48), channel_id=1, source_target_pairs={{0,1},{1,0},{2,3},{3,2},{4,5},{5,4},{6,7},{7,6},{8,9},{9,8},{10,11... | collective-permute-start | bytes 393224 | tf_op jit(solution)/shard_map/ppermute | solution.py:239
  31.1 2.3 %collective-permute-start.13 = (f32[128,256]{1,0:T(8,128)S(1)}, f32[128,256]{1,0:T(8,128)S(1)}, u32[]{:S(2)}, u32[]{:S(2)}) collective-permute-start(f32[128,256]{1,0:T(8,128)S(1)} %get-tuple-element.49), channel_id=1, source_target_pairs={{0,1},{1,0},{2,3},{3,2},{4,5},{5,4},{6,7},{7,6},{8,9},{9,8},{10,11... | collective-permute-start | bytes 393224 | tf_op jit(solution)/shard_map/ppermute | solution.py:239
  31.6 2.8 %collective-permute-start.14 = (f32[128,256]{1,0:T(8,128)S(1)}, f32[128,256]{1,0:T(8,128)S(1)}, u32[]{:S(2)}, u32[]{:S(2)}) collective-permute-start(f32[128,256]{1,0:T(8,128)S(1)} %add.15.w_ref), channel_id=1, source_target_pairs={{0,1},{1,0},{2,3},{3,2},{4,5},{5,4},{6,7},{7,6},{8,9},{9,8},{10,11... | collective-permute-start | bytes 393224 | tf_op jit(solution)/shard_map/ppermute | solution.py:239
  33.3 1.3 %collective-permute-start.15 = (f32[128,256]{1,0:T(8,128)S(1)}, f32[128,256]{1,0:T(8,128)S(1)}, u32[]{:S(2)}, u32[]{:S(2)}) collective-permute-start(f32[128,256]{1,0:T(8,128)S(1)} %collective-permute-done.11.far_ref), channel_id=1, source_target_pairs={{0,1},{1,0},{2,3},{3,2},{4,5},{5,4},{6,7},{7,6},{8,9},{9,8},{10,11... | collective-permute-start | bytes 393224 | tf_op jit(solution)/shard_map/ppermute | solution.py:239

commit v9 on v8

--- a/solution.py
+++ b/solution.py
@@ -328,7 +328,7 @@
         (q, q_x, woodbury_cores, lower, row_bases, top, w), 0,
     )
     k_other = [swap_narrow(k2), swap_narrow(k3)]
-    w_other = swap_narrow(after(w, k2))
+    w_other = swap_narrow(after(w, k3))
     far_other = swap_narrow(far)
     own, less = call(
         functools.partial(solve_own, rest), (shape(rows, half),) * 2,

time: 36.2 us -> 36.2 us (level)
  no operation moved by 1% of the time
where the time goes in v9:
time: 36.2 us; the launch traced here: 36.1 us
  starting transfers between devices  15.4 us (43%)
  Pallas kernels  13.2 us (36%)
  waiting for transfers between devices  7.24 us (20%)
    pallas_call x14, Pallas kernels, call(): pl.pallas_call(body, in_specs=in_specs or [VMEM] * len(args), out_specs=j...  13.2 us
    ppermute x5, starting transfers between devices, swap_crossed(): return lax.ppermute(x, ('wide', 'narrow'), route)  7.28 us
    ppermute x4, starting transfers between devices, swap_wide(): return lax.ppermute(x, 'wide', [(w, w ^ 1 << bit) for w in range(count)])  6.43 us
    ppermute x4, waiting for transfers between devices, swap_wide(): return lax.ppermute(x, 'wide', [(w, w ^ 1 << bit) for w in range(count)])  3.45 us
    ppermute x5, waiting for transfers between devices, swap_crossed(): return lax.ppermute(x, ('wide', 'narrow'), route)  2.71 us
    ppermute x7, starting transfers between devices, swap_narrow(): return lax.ppermute(x, 'narrow', [(0, 1), (1, 0)])  1.68 us
    ppermute x7, waiting for transfers between devices, swap_narrow(): return lax.ppermute(x, 'narrow', [(0, 1), (1, 0)])  1.07 us
  transfers between devices with their start and end apart: 16, of which 7 were waited for; matrix products, arithmetic and copies ran while one was open for 0% of the time, Pallas kernels for 27%

profile of v9, /device:TPU:0, one launch (start us, length us, event | category | flops | bytes accessed | tf_op | source)
XLA Modules:
  0.0 36.1 jit_solution(15742767145500057647)
XLA Ops:
  0.0 1.8 %shard_map.55.last_ref = f32[128,128]{1,0:T(8,128)S(1)} custom-call(f32[3,1024,128]{2,1,0:T(8,128)} %dual_ref.3, f32[3,1024,128]{2,1,0:T(8,128)} %row_ref.9), custom_call_target="tpu_custom_call" | custom-call | flops 16106127360 | tf_op jit(solution)/shard_map/pallas_call | solution.py:40
  1.8 0.0 copy-start.3
  1.8 2.4 %collective-permute-start = (f32[128,128]{1,0:T(8,128)S(1)}, f32[128,128]{1,0:T(8,128)S(1)}, u32[]{:S(2)}, u32[]{:S(2)}) collective-permute-start(f32[128,128]{1,0:T(8,128)S(1)} %shard_map.55.last_ref), channel_id=1, source_target_pairs={{0,3},{1,2},{2,1},{3,0},{4,7},{5,6},{6,5},{7,4},{8,11},{9,10},{10,... | collective-permute-start | bytes 196616 | tf_op jit(solution)/shard_map/ppermute | solution.py:249
  4.3 0.6 %shard_map.58.pairs_ref = f32[256,128]{1,0:T(8,128)S(1)} custom-call(f32[3,1024,128]{2,1,0:T(8,128)S(1)} %copy-done.4, f32[3,1024,128]{2,1,0:T(8,128)S(1)} %copy-done.1, f32[128,128]{1,0:T(8,128)S(1)} %shard_map.55.last_ref), custom_call_target="tpu_custom_call" | custom-call | flops 67108864 | tf_op jit(solution)/shard_map/pallas_call | solution.py:40
  4.9 0.4 %collective-permute-start.2 = (f32[256,128]{1,0:T(8,128)S(1)}, f32[256,128]{1,0:T(8,128)S(1)}, u32[]{:S(2)}, u32[]{:S(2)}) collective-permute-start(f32[256,128]{1,0:T(8,128)S(1)} %shard_map.58.pairs_ref), channel_id=1, source_target_pairs={{0,3},{1,2},{2,1},{3,0},{4,7},{5,6},{6,5},{7,4},{8,11},{9,10},{10,... | collective-permute-start | bytes 393224 | tf_op jit(solution)/shard_map/ppermute | solution.py:249
  5.3 0.0 copy-done.3
  5.3 1.8 %shard_map.56.first_ref = f32[512,512]{1,0:T(8,128)S(1)} custom-call(f32[1024,1024]{1,0:T(8,128)S(1)} %copy-done.2, f32[1024,512]{1,0:T(8,128)S(1)} %copy-done.3), custom_call_target="tpu_custom_call" | custom-call | flops 1610612736 | tf_op jit(solution)/shard_map/pallas_call | solution.py:40
  7.1 0.0 collective-permute-done.last_x_ref
  7.1 0.0 copy-start
  7.1 1.9 %collective-permute-start.1 = (f32[128,128]{1,0:T(8,128)S(1)}, f32[128,128]{1,0:T(8,128)S(1)}, u32[]{:S(2)}, u32[]{:S(2)}) collective-permute-start(f32[128,128]{1,0:T(8,128)S(1)} %add.12), channel_id=1, source_target_pairs={{0,5},{1,4},{2,7},{3,6},{4,1},{5,0},{6,3},{7,2},{8,13},{9,12},{10,... | collective-permute-start | bytes 196616 | tf_op jit(solution)/shard_map/ppermute | solution.py:249
  9.1 3.1 %shard_map.57 = (f32[512,512]{1,0:T(8,128)S(1)}, f32[384,256]{1,0:T(8,128)S(1)}, f32[384,256]{1,0:T(8,128)S(1)}) custom-call(f32[1024,1024]{1,0:T(8,128)S(1)} %copy-done.2, f32[1024,512]{1,0:T(8,128)S(1)} %copy-done.3, f32[3,1024,128]{2,1,0:T(8,128)S(1)} %copy-done.4, f32[512,512]{1,0:T(8,128)S(1)} %shard_map.56.first_ref), custom_call_target="tpu_custom_call" | custom-call | tf_op jit(solution)/shard_map/pallas_call | solution.py:40
  12.2 0.0 collective-permute-done.2.pairs_x_ref
  12.2 0.3 shard_map.59.fix_ref
  12.5 0.0 collective-permute-done.1.last_z_ref
  12.5 0.5 %collective-permute-start.3 = (f32[384,256]{1,0:T(8,128)S(1)}, f32[384,256]{1,0:T(8,128)S(1)}, u32[]{:S(2)}, u32[]{:S(2)}) collective-permute-start(f32[384,256]{1,0:T(8,128)S(1)} %get-tuple-element.34), channel_id=1, source_target_pairs={{0,1},{1,0},{2,3},{3,2},{4,5},{5,4},{6,7},{7,6},{8,9},{9,8},{10,11... | collective-permute-start | bytes 1179656 | tf_op jit(solution)/shard_map/ppermute | solution.py:239
  12.9 0.1 collective-permute-start.4
  13.0 0.2 shard_map.61.fix_ref
  13.3 0.5 %collective-permute-start.5 = (f32[128,128]{1,0:T(8,128)S(1)}, f32[128,128]{1,0:T(8,128)S(1)}, u32[]{:S(2)}, u32[]{:S(2)}) collective-permute-start(f32[128,128]{1,0:T(8,128)S(1)} %shard_map.61.fix_ref), channel_id=1, source_target_pairs={{0,1},{1,0},{2,3},{3,2},{4,5},{5,4},{6,7},{7,6},{8,9},{9,8},{10,11... | collective-permute-start | bytes 196616 | tf_op jit(solution)/shard_map/ppermute | solution.py:239
  13.7 0.7 %collective-permute-done.4.fix_other_ref = f32[256,128]{1,0:T(8,128)S(1)} collective-permute-done((f32[256,128]{1,0:T(8,128)S(1)}, f32[256,128]{1,0:T(8,128)S(1)}, u32[]{:S(2)}, u32[]{:S(2)}) %collective-permute-start.4) | collective-permute-done | bytes 131104 | tf_op jit(solution)/shard_map/ppermute | solution.py:239
  14.5 0.0 collective-permute-done.3.recv_ref
  14.5 0.3 shard_map.60
  14.7 0.0 collective-permute-done.5.fix_other_ref
  14.7 0.2 shard_map.62.refs_0_
  14.9 0.9 %collective-permute-start.7 = (f32[128,256]{1,0:T(8,128)S(1)}, f32[128,256]{1,0:T(8,128)S(1)}, u32[]{:S(2)}, u32[]{:S(2)}) collective-permute-start(f32[128,256]{1,0:T(8,128)S(1)} %shard_map.62.refs_0_), channel_id=1, source_target_pairs={{0,4},{1,3},{2,6},{3,1},{4,0},{5,7},{6,2},{7,5},{8,12},{9,11},{10,... | collective-permute-start | bytes 393224 | tf_op jit(solution)/shard_map/ppermute | solution.py:249
  15.9 1.6 %collective-permute-start.6 = (f32[128,256]{1,0:T(8,128)S(1)}, f32[128,256]{1,0:T(8,128)S(1)}, u32[]{:S(2)}, u32[]{:S(2)}) collective-permute-start(f32[128,256]{1,0:T(8,128)S(1)} %shard_map.63), channel_id=1, source_target_pairs={{0,2},{2,0},{4,6},{6,4},{8,10},{10,8},{12,14},{14,12},{1,3},{3,1},... | collective-permute-start | bytes 393224 | tf_op jit(solution)/shard_map/ppermute | solution.py:235
  17.5 0.6 %shard_map.64.top_ref = f32[2,1024,128]{2,1,0:T(8,128)S(1)} custom-call(f32[3,1024,128]{2,1,0:T(8,128)S(1)} %copy-done.1, f32[1792,256]{1,0:T(8,128)S(1)} %copy-done), custom_call_target="tpu_custom_call" | custom-call | tf_op jit(solution)/shard_map/pallas_call | solution.py:40
  18.0 1.9 %collective-permute-done.7 = f32[128,256]{1,0:T(8,128)S(1)} collective-permute-done((f32[128,256]{1,0:T(8,128)S(1)}, f32[128,256]{1,0:T(8,128)S(1)}, u32[]{:S(2)}, u32[]{:S(2)}) %collective-permute-start.7) | collective-permute-done | bytes 131104 | tf_op jit(solution)/shard_map/ppermute | solution.py:249
  20.0 1.6 %collective-permute-start.9 = (f32[128,256]{1,0:T(8,128)S(1)}, f32[128,256]{1,0:T(8,128)S(1)}, u32[]{:S(2)}, u32[]{:S(2)}) collective-permute-start(f32[128,256]{1,0:T(8,128)S(1)} %add.13), channel_id=1, source_target_pairs={{0,2},{1,5},{2,0},{3,7},{4,6},{5,1},{6,4},{7,3},{8,10},{9,13},{10,... | collective-permute-start | bytes 393224 | tf_op jit(solution)/shard_map/ppermute | solution.py:249
  21.6 0.6 %collective-permute-done.6 = f32[128,256]{1,0:T(8,128)S(1)} collective-permute-done((f32[128,256]{1,0:T(8,128)S(1)}, f32[128,256]{1,0:T(8,128)S(1)}, u32[]{:S(2)}, u32[]{:S(2)}) %collective-permute-start.6) | collective-permute-done | bytes 131104 | tf_op jit(solution)/shard_map/ppermute | solution.py:235
  22.2 0.7 %collective-permute-start.10 = (f32[128,256]{1,0:T(8,128)S(1)}, f32[128,256]{1,0:T(8,128)S(1)}, u32[]{:S(2)}, u32[]{:S(2)}) collective-permute-start(f32[128,256]{1,0:T(8,128)S(1)} %add.14.v_ref), channel_id=1, source_target_pairs={{0,4},{2,6},{4,0},{6,2},{8,12},{10,14},{12,8},{14,10},{1,5},{3,7},... | collective-permute-start | bytes 393224 | tf_op jit(solution)/shard_map/ppermute | solution.py:235
  22.9 1.5 %collective-permute-start.8 = (f32[128,256]{1,0:T(8,128)S(1)}, f32[128,256]{1,0:T(8,128)S(1)}, u32[]{:S(2)}, u32[]{:S(2)}) collective-permute-start(f32[128,256]{1,0:T(8,128)S(1)} %get-tuple-element.42.q_ref), channel_id=1, source_target_pairs={{0,2},{2,0},{4,6},{6,4},{8,10},{10,8},{12,14},{14,12},{1,3},{3,1},... | collective-permute-start | bytes 393224 | tf_op jit(solution)/shard_map/ppermute | solution.py:235
  24.4 0.8 %collective-permute-done.9 = f32[128,256]{1,0:T(8,128)S(1)} collective-permute-done((f32[128,256]{1,0:T(8,128)S(1)}, f32[128,256]{1,0:T(8,128)S(1)}, u32[]{:S(2)}, u32[]{:S(2)}) %collective-permute-start.9) | collective-permute-done | bytes 131104 | tf_op jit(solution)/shard_map/ppermute | solution.py:249
  25.2 2.6 %collective-permute-start.11 = (f32[128,256]{1,0:T(8,128)S(1)}, f32[128,256]{1,0:T(8,128)S(1)}, u32[]{:S(2)}, u32[]{:S(2)}) collective-permute-start(f32[128,256]{1,0:T(8,128)S(1)} %add.15.w_ref), channel_id=1, source_target_pairs={{0,8},{2,10},{4,12},{6,14},{8,0},{10,2},{12,4},{14,6},{1,9},{3,11}... | collective-permute-start | bytes 393224 | tf_op jit(solution)/shard_map/ppermute | solution.py:235
  27.8 1.1 %collective-permute-done.10.vz_ref = f32[128,256]{1,0:T(8,128)S(1)} collective-permute-done((f32[128,256]{1,0:T(8,128)S(1)}, f32[128,256]{1,0:T(8,128)S(1)}, u32[]{:S(2)}, u32[]{:S(2)}) %collective-permute-start.10) | collective-permute-done | bytes 131104 | tf_op jit(solution)/shard_map/ppermute | solution.py:235
  29.0 1.0 %shard_map.65 = (f32[128,256]{1,0:T(8,128)S(1)}, f32[1024,256]{1,0:T(8,128)S(1)}) custom-call(f32[128,256]{1,0:T(8,128)S(1)} %add.14.v_ref, f32[128,256]{1,0:T(8,128)S(1)} %collective-permute-done.10.vz_ref, f32[1792,256]{1,0:T(8,128)S(1)} %copy-done, f32[512,512]{1,0:T(8,128)S(1)} %shard_map.56.first_ref, f32[512,512]{1,0:T(8,128)S(1)} %get-tuple-element.45.last_ref, ...), custom_call_target="tpu_custom_call" | custom-call | tf_op jit(solution)/shard_map/pallas_call | solution.py:40
  30.0 0.0 collective-permute-done.8.qx_ref
  30.0 1.0 %shard_map.66 = (f32[128,256]{1,0:T(8,128)S(1)}, f32[1024,256]{1,0:T(8,128)S(1)}) custom-call(f32[128,256]{1,0:T(8,128)S(1)} %get-tuple-element.42.q_ref, f32[128,256]{1,0:T(8,128)S(1)} %collective-permute-done.8.qx_ref, f32[1792,256]{1,0:T(8,128)S(1)} %copy-done, f32[1024,256]{1,0:T(8,128)S(1)} %get-tuple-element.46.field_ref, ...), custom_call_target="tpu_custom_call" | custom-call | tf_op jit(solution)/shard_map/pallas_call | solution.py:40
  31.0 0.1 collective-permute-start.13
  31.1 0.5 %collective-permute-start.12 = (f32[128,256]{1,0:T(8,128)S(1)}, f32[128,256]{1,0:T(8,128)S(1)}, u32[]{:S(2)}, u32[]{:S(2)}) collective-permute-start(f32[128,256]{1,0:T(8,128)S(1)} %get-tuple-element.48), channel_id=1, source_target_pairs={{0,1},{1,0},{2,3},{3,2},{4,5},{5,4},{6,7},{7,6},{8,9},{9,8},{10,11... | collective-permute-start | bytes 393224 | tf_op jit(solution)/shard_map/ppermute | solution.py:239
  31.6 0.1 collective-permute-start.14
  31.6 1.7 %collective-permute-done.11.far_ref = f32[128,256]{1,0:T(8,128)S(1)} collective-permute-done((f32[128,256]{1,0:T(8,128)S(1)}, f32[128,256]{1,0:T(8,128)S(1)}, u32[]{:S(2)}, u32[]{:S(2)}) %collective-permute-start.11) | collective-permute-done | bytes 131104 | tf_op jit(solution)/shard_map/ppermute | solution.py:235
  33.3 0.0 collective-permute-start.15
  33.4 0.0 collective-permute-done.13.refs_1_
  33.4 0.0 collective-permute-done.12.refs_0_
  33.4 1.0 %shard_map.67 = (f32[1024,256]{1,0:T(8,128)S(1)}, f32[1024,256]{1,0:T(8,128)S(1)}) custom-call(f32[1024,256]{1,0:T(8,128)S(1)} %get-tuple-element.47.own_ref, f32[512,512]{1,0:T(8,128)S(1)} %shard_map.56.first_ref, f32[512,512]{1,0:T(8,128)S(1)} %get-tuple-element.45.last_ref, f32[3,1024,128]{2,1,0:T(8,128)S(1)} %copy-done.1, ...), custom_call_target="tpu_custom_call" | custom-call | tf_op jit(solution)/shard_map/pallas_call | solution.py:40
  34.4 0.0 collective-permute-done.14.w_ref
  34.4 0.3 collective-permute-done.15.far_ref
  34.7 1.4 %shard_map.68 = f32[1024,512]{1,0:T(8,128)} custom-call(f32[1024,256]{1,0:T(8,128)S(1)} %get-tuple-element.50.own_ref, f32[1024,256]{1,0:T(8,128)S(1)} %get-tuple-element.51.less_ref, f32[2,1024,128]{2,1,0:T(8,128)S(1)} %shard_map.64.top_ref, f32[128,256]{1,0:T(8,128)S(1)} %collective-permute-done.14.w_ref, f32[128,256]{1,0:T(8,128)S(1)} %collective-permute-done.15.far_ref), custom_call_target="tpu_custom_call" | custom-call | tf_op jit(solution)/shard_map/pallas_call | solution.py:40
  (12 shorter events, 0.1 us)
Async XLA Ops:
  0.0 4.2 %copy-start.1 = (f32[3,1024,128]{2,1,0:T(8,128)S(1)}, f32[3,1024,128]{2,1,0:T(8,128)}, u32[]{:S(2)}) copy-start(f32[3,1024,128]{2,1,0:T(8,128)} %row_ref.9) | copy-start | bytes 4718596
  0.0 4.3 %copy-start.4 = (f32[3,1024,128]{2,1,0:T(8,128)S(1)}, f32[3,1024,128]{2,1,0:T(8,128)}, u32[]{:S(2)}) copy-start(f32[3,1024,128]{2,1,0:T(8,128)} %dual_ref.3) | copy-start | bytes 4718596
  0.0 5.3 %copy-start.2 = (f32[1024,1024]{1,0:T(8,128)S(1)}, f32[1024,1024]{1,0:T(8,128)}, u32[]{:S(2)}) copy-start(f32[1024,1024]{1,0:T(8,128)} %leaf_ref.3) | copy-start | bytes 12582916
  1.8 3.5 %copy-start.3 = (f32[1024,512]{1,0:T(8,128)S(1)}, f32[1024,512]{1,0:T(8,128)}, u32[]{:S(2)}) copy-start(f32[1024,512]{1,0:T(8,128)} %right_ref.1) | copy-start | bytes 6291460
  1.8 5.3 %collective-permute-start = (f32[128,128]{1,0:T(8,128)S(1)}, f32[128,128]{1,0:T(8,128)S(1)}, u32[]{:S(2)}, u32[]{:S(2)}) collective-permute-start(f32[128,128]{1,0:T(8,128)S(1)} %shard_map.55.last_ref), channel_id=1, source_target_pairs={{0,3},{1,2},{2,1},{3,0},{4,7},{5,6},{6,5},{7,4},{8,11},{9,10},{10,... | collective-permute-start | bytes 196616 | tf_op jit(solution)/shard_map/ppermute | solution.py:249
  4.9 7.3 %collective-permute-start.2 = (f32[256,128]{1,0:T(8,128)S(1)}, f32[256,128]{1,0:T(8,128)S(1)}, u32[]{:S(2)}, u32[]{:S(2)}) collective-permute-start(f32[256,128]{1,0:T(8,128)S(1)} %shard_map.58.pairs_ref), channel_id=1, source_target_pairs={{0,3},{1,2},{2,1},{3,0},{4,7},{5,6},{6,5},{7,4},{8,11},{9,10},{10,... | collective-permute-start | bytes 393224 | tf_op jit(solution)/shard_map/ppermute | solution.py:249
  7.1 5.1 %copy-start = (f32[1792,256]{1,0:T(8,128)S(1)}, f32[1792,256]{1,0:T(8,128)}, u32[]{:S(2)}) copy-start(f32[1792,256]{1,0:T(8,128)} %cores_ref.8) | copy-start | bytes 5505028
  7.1 5.3 %collective-permute-start.1 = (f32[128,128]{1,0:T(8,128)S(1)}, f32[128,128]{1,0:T(8,128)S(1)}, u32[]{:S(2)}, u32[]{:S(2)}) collective-permute-start(f32[128,128]{1,0:T(8,128)S(1)} %add.12), channel_id=1, source_target_pairs={{0,5},{1,4},{2,7},{3,6},{4,1},{5,0},{6,3},{7,2},{8,13},{9,12},{10,... | collective-permute-start | bytes 196616 | tf_op jit(solution)/shard_map/ppermute | solution.py:249
  12.5 2.0 %collective-permute-start.3 = (f32[384,256]{1,0:T(8,128)S(1)}, f32[384,256]{1,0:T(8,128)S(1)}, u32[]{:S(2)}, u32[]{:S(2)}) collective-permute-start(f32[384,256]{1,0:T(8,128)S(1)} %get-tuple-element.34), channel_id=1, source_target_pairs={{0,1},{1,0},{2,3},{3,2},{4,5},{5,4},{6,7},{7,6},{8,9},{9,8},{10,11... | collective-permute-start | bytes 1179656 | tf_op jit(solution)/shard_map/ppermute | solution.py:239
  12.9 1.5 %collective-permute-start.4 = (f32[256,128]{1,0:T(8,128)S(1)}, f32[256,128]{1,0:T(8,128)S(1)}, u32[]{:S(2)}, u32[]{:S(2)}) collective-permute-start(f32[256,128]{1,0:T(8,128)S(1)} %shard_map.59.fix_ref), channel_id=1, source_target_pairs={{0,1},{1,0},{2,3},{3,2},{4,5},{5,4},{6,7},{7,6},{8,9},{9,8},{10,11... | collective-permute-start | bytes 393224 | tf_op jit(solution)/shard_map/ppermute | solution.py:239
  13.3 1.5 %collective-permute-start.5 = (f32[128,128]{1,0:T(8,128)S(1)}, f32[128,128]{1,0:T(8,128)S(1)}, u32[]{:S(2)}, u32[]{:S(2)}) collective-permute-start(f32[128,128]{1,0:T(8,128)S(1)} %shard_map.61.fix_ref), channel_id=1, source_target_pairs={{0,1},{1,0},{2,3},{3,2},{4,5},{5,4},{6,7},{7,6},{8,9},{9,8},{10,11... | collective-permute-start | bytes 196616 | tf_op jit(solution)/shard_map/ppermute | solution.py:239
  14.9 5.0 %collective-permute-start.7 = (f32[128,256]{1,0:T(8,128)S(1)}, f32[128,256]{1,0:T(8,128)S(1)}, u32[]{:S(2)}, u32[]{:S(2)}) collective-permute-start(f32[128,256]{1,0:T(8,128)S(1)} %shard_map.62.refs_0_), channel_id=1, source_target_pairs={{0,4},{1,3},{2,6},{3,1},{4,0},{5,7},{6,2},{7,5},{8,12},{9,11},{10,... | collective-permute-start | bytes 393224 | tf_op jit(solution)/shard_map/ppermute | solution.py:249
  15.9 6.3 %collective-permute-start.6 = (f32[128,256]{1,0:T(8,128)S(1)}, f32[128,256]{1,0:T(8,128)S(1)}, u32[]{:S(2)}, u32[]{:S(2)}) collective-permute-start(f32[128,256]{1,0:T(8,128)S(1)} %shard_map.63), channel_id=1, source_target_pairs={{0,2},{2,0},{4,6},{6,4},{8,10},{10,8},{12,14},{14,12},{1,3},{3,1},... | collective-permute-start | bytes 393224 | tf_op jit(solution)/shard_map/ppermute | solution.py:235
  20.0 5.2 %collective-permute-start.9 = (f32[128,256]{1,0:T(8,128)S(1)}, f32[128,256]{1,0:T(8,128)S(1)}, u32[]{:S(2)}, u32[]{:S(2)}) collective-permute-start(f32[128,256]{1,0:T(8,128)S(1)} %add.13), channel_id=1, source_target_pairs={{0,2},{1,5},{2,0},{3,7},{4,6},{5,1},{6,4},{7,3},{8,10},{9,13},{10,... | collective-permute-start | bytes 393224 | tf_op jit(solution)/shard_map/ppermute | solution.py:249
  22.2 6.8 %collective-permute-start.10 = (f32[128,256]{1,0:T(8,128)S(1)}, f32[128,256]{1,0:T(8,128)S(1)}, u32[]{:S(2)}, u32[]{:S(2)}) collective-permute-start(f32[128,256]{1,0:T(8,128)S(1)} %add.14.v_ref), channel_id=1, source_target_pairs={{0,4},{2,6},{4,0},{6,2},{8,12},{10,14},{12,8},{14,10},{1,5},{3,7},... | collective-permute-start | bytes 393224 | tf_op jit(solution)/shard_map/ppermute | solution.py:235
  22.9 7.1 %collective-permute-start.8 = (f32[128,256]{1,0:T(8,128)S(1)}, f32[128,256]{1,0:T(8,128)S(1)}, u32[]{:S(2)}, u32[]{:S(2)}) collective-permute-start(f32[128,256]{1,0:T(8,128)S(1)} %get-tuple-element.42.q_ref), channel_id=1, source_target_pairs={{0,2},{2,0},{4,6},{6,4},{8,10},{10,8},{12,14},{14,12},{1,3},{3,1},... | collective-permute-start | bytes 393224 | tf_op jit(solution)/shard_map/ppermute | solution.py:235
  25.2 8.1 %collective-permute-start.11 = (f32[128,256]{1,0:T(8,128)S(1)}, f32[128,256]{1,0:T(8,128)S(1)}, u32[]{:S(2)}, u32[]{:S(2)}) collective-permute-start(f32[128,256]{1,0:T(8,128)S(1)} %add.15.w_ref), channel_id=1, source_target_pairs={{0,8},{2,10},{4,12},{6,14},{8,0},{10,2},{12,4},{14,6},{1,9},{3,11}... | collective-permute-start | bytes 393224 | tf_op jit(solution)/shard_map/ppermute | solution.py:235
  31.0 2.4 %collective-permute-start.13 = (f32[128,256]{1,0:T(8,128)S(1)}, f32[128,256]{1,0:T(8,128)S(1)}, u32[]{:S(2)}, u32[]{:S(2)}) collective-permute-start(f32[128,256]{1,0:T(8,128)S(1)} %get-tuple-element.49), channel_id=1, source_target_pairs={{0,1},{1,0},{2,3},{3,2},{4,5},{5,4},{6,7},{7,6},{8,9},{9,8},{10,11... | collective-permute-start | bytes 393224 | tf_op jit(solution)/shard_map/ppermute | solution.py:239
  31.1 2.3 %collective-permute-start.12 = (f32[128,256]{1,0:T(8,128)S(1)}, f32[128,256]{1,0:T(8,128)S(1)}, u32[]{:S(2)}, u32[]{:S(2)}) collective-permute-start(f32[128,256]{1,0:T(8,128)S(1)} %get-tuple-element.48), channel_id=1, source_target_pairs={{0,1},{1,0},{2,3},{3,2},{4,5},{5,4},{6,7},{7,6},{8,9},{9,8},{10,11... | collective-permute-start | bytes 393224 | tf_op jit(solution)/shard_map/ppermute | solution.py:239
  31.6 2.8 %collective-permute-start.14 = (f32[128,256]{1,0:T(8,128)S(1)}, f32[128,256]{1,0:T(8,128)S(1)}, u32[]{:S(2)}, u32[]{:S(2)}) collective-permute-start(f32[128,256]{1,0:T(8,128)S(1)} %add.15.w_ref), channel_id=1, source_target_pairs={{0,1},{1,0},{2,3},{3,2},{4,5},{5,4},{6,7},{7,6},{8,9},{9,8},{10,11... | collective-permute-start | bytes 393224 | tf_op jit(solution)/shard_map/ppermute | solution.py:239
  33.3 1.3 %collective-permute-start.15 = (f32[128,256]{1,0:T(8,128)S(1)}, f32[128,256]{1,0:T(8,128)S(1)}, u32[]{:S(2)}, u32[]{:S(2)}) collective-permute-start(f32[128,256]{1,0:T(8,128)S(1)} %collective-permute-done.11.far_ref), channel_id=1, source_target_pairs={{0,1},{1,0},{2,3},{3,2},{4,5},{5,4},{6,7},{7,6},{8,9},{9,8},{10,11... | collective-permute-start | bytes 393224 | tf_op jit(solution)/shard_map/ppermute | solution.py:239
